TPU v7x, 32 devices: a whole 2x2x4 slice. The times are simulated.
32 devices in a mesh: hst: 16 (over z, y, core), local: 2 (over x).
Axes of the slice: x: 2, y: 2, z: 4, core: 2. Of those that a mesh axis runs over, the one named last changes fastest.
Arguments:
- gate_act: bfloat16 [2048, 11008], P('hst', 'local'), may hold values from -6 to 6
- up_act: bfloat16 [2048, 11008], P('hst', 'local'), may hold values from -6 to 6
- cotangent: bfloat16 [2048, 4096], P('hst', 'local'), may hold values from -6 to 6
- down_weight: bfloat16 [11008, 4096], P('local', 'hst'), may hold values from -0.0546875 to 0.0546875
Outputs:
- output: bfloat16 [2048, 4096], P('hst', 'local')
- gate_delta: bfloat16 [2048, 11008], P('hst', 'local')
- up_delta: bfloat16 [2048, 11008], P('hst', 'local')
- down_grad: float32 [11008, 4096], P('local', 'hst')
All inputs are finite; a program needn't handle non-finite values.
Results may differ from a plain program's by a relative error of at most 0.005.
Values may be sent and summed in bfloat16 or wider, within the bound.
No kernel may reach another device: no remote copies, remote signals or barrier semaphores. Data moves between devices by JAX's collectives and lax.ppermute only.
A program may use at most 320 MiB of HBM per device.

v0:
```python
import jax
import jax.numpy as jnp
from jax import lax
from jax.sharding import PartitionSpec as P


def on_device(gate_act, up_act, cotangent, down_weight):
    contract_last = (((1,), (1,)), ((), ()))
    contract_first = (((0,), (0,)), ((), ()))
    gate_wide = gate_act.astype(jnp.float32)
    up_wide = up_act.astype(jnp.float32)
    sigmoid_gate = jax.nn.sigmoid(gate_wide)
    hidden = (gate_wide * sigmoid_gate * up_wide).astype(jnp.bfloat16)
    weight_rows = lax.all_gather(down_weight, "hst", axis=1, tiled=True)
    partial_value = jnp.dot(hidden, weight_rows, preferred_element_type=jnp.float32)
    output = lax.psum_scatter(partial_value, "local", scatter_dimension=1, tiled=True).astype(
        jnp.bfloat16
    )
    cot_full = lax.all_gather(cotangent, "local", axis=1, tiled=True)
    hidden_grad = lax.dot_general(
        cot_full, weight_rows, contract_last, preferred_element_type=jnp.float32
    )
    up_delta = (hidden_grad * gate_wide * sigmoid_gate).astype(jnp.bfloat16)
    gate_delta = (
        hidden_grad * up_wide * sigmoid_gate * (1.0 + gate_wide * (1.0 - sigmoid_gate))
    ).astype(jnp.bfloat16)
    weight_terms = lax.dot_general(
        hidden, cot_full, contract_first, preferred_element_type=jnp.float32
    )
    down_grad = lax.psum_scatter(weight_terms, "hst", scatter_dimension=1, tiled=True)
    return (output, gate_delta, up_delta, down_grad)


def solution(mesh):
    in_specs = (P("hst", "local"), P("hst", "local"), P("hst", "local"), P("local", "hst"))
    out_specs = (P("hst", "local"), P("hst", "local"), P("hst", "local"), P("local", "hst"))
    return jax.shard_map(
        on_device, mesh=mesh, in_specs=in_specs, out_specs=out_specs, check_vma=False
    )
```

profile of v0, /device:TPU:8, one launch (start us, length us, event | category | flops | bytes accessed | tf_op | source)
XLA Modules:
  0.0 1128.9 jit_solution(12515036150248492285)
XLA Ops:
  7.2 0.0 copy-start
  7.2 0.0 copy-start.1
  7.2 0.0 all-gather.3.cloned.1.call-start
  7.2 0.7 all-gather.3.cloned.1.call-update
  7.9 0.0 all-gather.5.cloned.1.call-start
  8.0 0.7 all-gather.5.cloned.1.call-update
  8.7 0.0 reduce-scatter.3.cloned.1.call-start
  8.7 233.1 %all-gather.3.cloned.1.call-done = bf16[5504,4096]{1,0:T(8,128)(2,1)} async-done(((bf16[5504,256]{1,0:T(8,128)(2,1)}), bf16[5504,4096]{1,0:T(8,128)(2,1)}) %all-gather.3.cloned.1.call-update) | async-done | bytes 45088784 | tf_op jit(solution)/shard_map/all_gather | solution.py:14
  241.9 0.0 copy-done
  241.9 0.0 copy-done.1
  241.9 19.2 %fusion.12 = f32[128,4096]{1,0:T(8,128)} fusion(bf16[5504,4096]{1,0:T(8,128)(2,1)} %all-gather.3.cloned.1.call-done, bf16[128,5504]{1,0:T(8,128)(2,1)S(1)} %copy-done, bf16[128,5504]{1,0:T(8,128)(2,1)S(1)} %copy-done.1), kind=kOutput, calls=%fused_computation.17 | convolution fusion | flops 5776998400 | bytes 50003968 | tf_op jit(solution)/shard_map/dot_general | solution.py:15
  261.1 0.0 reduce-scatter.3.cloned.1.call-update
  261.1 0.0 reduce-scatter.5.cloned.1.call-start
  261.1 3.4 all-gather.5.cloned.1.call-done
  264.6 33.2 %fusion.10 = f32[5504,4096]{1,0:T(8,128)} fusion(bf16[128,4096]{1,0:T(8,128)(2,1)} %all-gather.5.cloned.1.call-done, bf16[128,5504]{1,0:T(8,128)(2,1)S(1)} %copy-done, bf16[128,5504]{1,0:T(8,128)(2,1)S(1)} %copy-done.1), kind=kOutput, calls=%fused_computation.16 | convolution fusion | flops 5776998400 | bytes 94044160 | tf_op jit(solution)/shard_map/dot_general | solution.py:27
  297.8 0.0 reduce-scatter.5.cloned.1.call-update
  297.8 24.4 %fusion.9 = (bf16[128,5504]{1,0:T(8,128)(2,1)}, bf16[128,5504]{1,0:T(8,128)(2,1)}) fusion(bf16[128,5504]{1,0:T(8,128)(2,1)S(1)} %copy-done.1, bf16[128,5504]{1,0:T(8,128)(2,1)S(1)} %copy-done, bf16[128,4096]{1,0:T(8,128)(2,1)} %all-gather.5.cloned.1.call-done, bf16[5504,4096]{1,0:T(8,128)(2,1)} %all-gather.3.cloned.1.call-done), kind=kOutput, calls=%fused_computation.15 | convolution fusion | flops 5781929984 | bytes 51773440 | tf_op jit(solution)/shard_map/dot_general | solution.py:20
  322.2 0.0 reduce-scatter.3.cloned.1.call-done
  322.2 2.2 convert_element_type.21
  324.4 797.9 %reduce-scatter.5.cloned.1.call-done = f32[5504,256]{1,0:T(8,128)} async-done(((f32[5504,4096]{1,0:T(8,128)}), f32[5504,256]{1,0:T(8,128)}) %reduce-scatter.5.cloned.1.call-update) | async-done | bytes 5636112 | tf_op jit(solution)/shard_map/reduce_scatter | solution.py:30
Async XLA Ops:
  7.2 234.7 %copy-start = (bf16[128,5504]{1,0:T(8,128)(2,1)S(1)}, bf16[128,5504]{1,0:T(8,128)(2,1)}, u32[]{:S(2)}) copy-start(bf16[128,5504]{1,0:T(8,128)(2,1)} %param.5) | copy-start | bytes 4227076
  7.2 234.7 %copy-start.1 = (bf16[128,5504]{1,0:T(8,128)(2,1)S(1)}, bf16[128,5504]{1,0:T(8,128)(2,1)}, u32[]{:S(2)}) copy-start(bf16[128,5504]{1,0:T(8,128)(2,1)} %param.4) | copy-start | bytes 4227076
  7.2 234.7 %all-gather.3.cloned.1.call-start = ((), (), s32[]{:S(2)}) async-start(), calls=%async_computation.2 | async-start | bytes 47906816 | tf_op jit(solution)/shard_map/all_gather | solution.py:14
  7.9 256.6 %all-gather.5.cloned.1.call-start = ((), (), s32[]{:S(2)}) async-start(), calls=%async_computation.4 | async-start | bytes 1572864 | tf_op jit(solution)/shard_map/all_gather | solution.py:19
  8.7 313.5 %reduce-scatter.3.cloned.1.call-start = ((), (), s32[]{:S(2)}) async-start(), calls=%async_computation.3 | async-start | bytes 3145728 | tf_op jit(solution)/shard_map/reduce_scatter | solution.py:16
  261.1 861.3 %reduce-scatter.5.cloned.1.call-start = ((), (), s32[]{:S(2)}) async-start(), calls=%async_computation.5 | async-start | bytes 95813632 | tf_op jit(solution)/shard_map/reduce_scatter | solution.py:30
Sparse Core Ops, SparseCore 0:
  9.5 232.2 all-gather.2
  243.4 21.1 all-gather.4
  266.8 31.8 reduce-scatter.2
  304.0 818.2 reduce-scatter.4
where the time goes:
time: 1130 us
  waiting for transfers between devices  1040 us (92%)
  matrix products  76.8 us (7%)
  between operations  13.8 us (1%)
    reduce_scatter x1, waiting for transfers between devices, on_device(): lax.psum_scatter(weight_terms, 'hst', scatter_dimension=1, tiled=True)  798 us
    all_gather x1, waiting for transfers between devices, on_device(): weight_rows = lax.all_gather(down_weight, 'hst', axis=1, tiled=True)  233 us
    dot_general x1, matrix products, on_device(): lax.dot_general(hidden, cot_full, contract_first, preferred_element_type=...  33.2 us
    dot_general x1, matrix products, on_device(): lax.dot_general(cot_full, weight_rows, contract_last, preferred_element_t...  24.4 us
  transfers between devices with their start and end apart: 4, of which 3 were waited for; matrix products, arithmetic and copies ran while one was open for 7% of the time, Pallas kernels for 0%

commit v1 on v0

v1 whole, which is shorter than its diff:
```python
import jax
import jax.numpy as jnp
from jax import lax
from jax.sharding import PartitionSpec as P

QUAD = 4
CHUNKS = 2


def cuts(extent, parts):
    lanes = -(-extent // 128)
    edges = [min(extent, 128 * ((lanes * i + parts - 1) // parts)) for i in range(parts + 1)]
    return [(lo, hi) for lo, hi in zip(edges, edges[1:]) if hi > lo]


def solution(mesh):
    n_hst, n_local = mesh.shape["hst"], mesh.shape["local"]
    n_far = n_hst // QUAD

    def swap(value, bit):
        return lax.ppermute(value, "hst", [(h, h ^ bit) for h in range(n_hst)])

    def shift(value, step):
        pairs = [(h, (h + step * QUAD) % n_hst) for h in range(n_hst)]
        return lax.ppermute(value, "hst", pairs)

    def hop(value, way, sources):
        pairs = [(s * QUAD + q, (s + way) * QUAD + q) for s in sources for q in range(QUAD)]
        return lax.ppermute(value, "hst", pairs)

    def local_shift(value, step):
        return lax.ppermute(value, "local", [(i, (i + step) % n_local) for i in range(n_local)])

    def gather_far(own, far):
        above, below = {}, {}
        up = down = own
        for d in range(1, n_far):
            up = below[d] = hop(up, 1, range(d - 1, n_far - 1))
            down = above[d] = hop(down, -1, range(1, n_far - d + 1))
        slots = [own]
        for e in range(1, n_far):
            slots.append(jnp.where(far + e < n_far, above[e], below[n_far - e]))
        return jnp.concatenate(slots, axis=0)

    def reduce_far(slots):
        up = down = None
        for d in range(n_far - 1, 0, -1):
            up_term, down_term = slots[d], slots[n_far - d]
            if up is not None:
                up_term = up_term + up.astype(jnp.float32)
                down_term = down_term + down.astype(jnp.float32)
            up = hop(up_term.astype(jnp.bfloat16), 1, range(0, n_far - d))
            down = hop(down_term.astype(jnp.bfloat16), -1, range(d, n_far))
        return slots[0] + up.astype(jnp.float32) + down.astype(jnp.float32)

    def on_device(gate_act, up_act, cotangent, down_weight):
        h = lax.axis_index("hst")
        x = lax.axis_index("local")
        far, near = h // QUAD, h % QUAD
        tokens, half = cotangent.shape
        width = down_weight.shape[1]
        hidden_units = gate_act.shape[1]
        order = (0, 2, 1, 3)
        bounds = cuts(hidden_units, CHUNKS)

        parts = [cotangent]
        for step in range(1, n_local):
            parts.append(local_shift(cotangent, n_local - step))
        twice = jnp.concatenate(parts + parts[:-1], axis=1)
        cot_full = lax.dynamic_slice_in_dim(
            twice, ((n_local - x) % n_local) * half, n_local * half, axis=1
        )
        cot_view = cot_full.reshape(tokens, n_far, QUAD, width)
        cot_view = jnp.concatenate(
            [lax.dynamic_slice_in_dim(cot_view, near ^ k, 1, axis=2) for k in order], axis=2
        )
        cot_view = cot_view.reshape(tokens, n_far, QUAD * width)

        def cot_for(step):
            return lax.dynamic_index_in_dim(cot_view, (far + step) % n_far, axis=1, keepdims=False)

        cot_rows = jnp.concatenate(
            [cot_for(0)] + [shift(cot_for(n_far - e), n_far - e) for e in range(1, n_far)], axis=0
        )

        out_sum = 0.0
        gate_parts, up_parts, grad_parts = [], [], []
        for lo, hi in bounds:
            gate_wide = gate_act[:, lo:hi].astype(jnp.float32)
            up_wide = up_act[:, lo:hi].astype(jnp.float32)
            sigmoid_gate = jax.nn.sigmoid(gate_wide)
            hidden = (gate_wide * sigmoid_gate * up_wide).astype(jnp.bfloat16)

            weight = down_weight[lo:hi]
            pair = jnp.concatenate([weight, swap(weight, 2)], axis=1)
            weight_cols = jnp.concatenate([pair, swap(pair, 1)], axis=1)

            terms = lax.dot_general(
                cot_rows, weight_cols, (((1,), (1,)), ((), ())), preferred_element_type=jnp.float32
            )
            hidden_grad = reduce_far([terms[e * tokens : (e + 1) * tokens] for e in range(n_far)])
            up_parts.append((hidden_grad * gate_wide * sigmoid_gate).astype(jnp.bfloat16))
            gate_parts.append(
                (
                    hidden_grad * up_wide * sigmoid_gate * (1.0 + gate_wide * (1.0 - sigmoid_gate))
                ).astype(jnp.bfloat16)
            )

            hidden_rows = gather_far(hidden, far)
            out_sum = out_sum + jnp.dot(
                hidden_rows, weight_cols, preferred_element_type=jnp.float32
            )
            grad = lax.dot_general(
                hidden_rows, cot_rows, (((0,), (0,)), ((), ())), preferred_element_type=jnp.float32
            )
            theirs = swap(grad[:, 2 * width :].astype(jnp.bfloat16), 1)
            grad = grad[:, : 2 * width] + theirs.astype(jnp.float32)
            theirs = swap(grad[:, width:].astype(jnp.bfloat16), 2)
            grad_parts.append(grad[:, :width] + theirs.astype(jnp.float32))

        out_terms = out_sum.astype(jnp.bfloat16)
        slots = [out_terms[:tokens]]
        for e in range(1, n_far):
            slots.append(shift(out_terms[e * tokens : (e + 1) * tokens], e))
        back = [slots[0]] + slots[:0:-1]
        twice = jnp.concatenate(back + back[:-1], axis=1)
        columns = QUAD * width
        mine = lax.dynamic_slice_in_dim(
            twice, ((n_far - far) % n_far) * columns, n_far * columns, axis=1
        )
        mine = mine.reshape(tokens, n_far, QUAD, width)
        mine = jnp.concatenate(
            [lax.dynamic_slice_in_dim(mine, slot, 1, axis=2) for slot in slot_of(near)],
            axis=2,
        )
        mine = mine.reshape(tokens, n_local, half)

        def half_of(step):
            return lax.dynamic_index_in_dim(mine, (x + step) % n_local, axis=1, keepdims=False)

        output = half_of(0).astype(jnp.float32)
        for step in range(1, n_local):
            output = output + local_shift(half_of(step), step).astype(jnp.float32)
        return (
            output.astype(jnp.bfloat16),
            jnp.concatenate(gate_parts, axis=1),
            jnp.concatenate(up_parts, axis=1),
            jnp.concatenate(grad_parts, axis=0),
        )

    def slot_of(near):
        result = []
        for block in range(QUAD):
            k = near ^ block
            result.append(((k & 1) << 1) | (k >> 1))
        return result

    specs = (P("hst", "local"), P("hst", "local"), P("hst", "local"), P("local", "hst"))
    return jax.shard_map(
        on_device, mesh=mesh, in_specs=specs, out_specs=specs, check_vma=False
    )
```

time: 1130 us -> 427 us (0.38)
  waiting for transfers between devices: 1040 us -> 267 us
  starting transfers between devices: 0.16 us -> 62.5 us
  matrix products: 76.8 us -> 30.5 us
  other arithmetic: 2.25 us -> 36.8 us
  local copies, waits for them, and re-layouts: 0.01 us -> 27.5 us
  between operations: 13.8 us -> 1.48 us
    reduce_scatter x2 -> x0, waiting for transfers between devices: 798 us -> none  [the longest x1 798 us: on_device(): lax.psum_scatter(weight_terms, 'hst', scatter_dimension=1, tiled=True)]
    ppermute x0 -> x40, waiting for transfers between devices: none -> 267 us  [the longest x24 129 us: hop(): return lax.ppermute(value, 'hst', pairs)]
    all_gather x2 -> x0, waiting for transfers between devices: 237 us -> none  [the longest x1 233 us: on_device(): weight_rows = lax.all_gather(down_weight, 'hst', axis=1, tiled=True)]
    ppermute x0 -> x40, starting transfers between devices: none -> 62.5 us  [the longest x24 47.1 us: hop(): return lax.ppermute(value, 'hst', pairs)]
    dot_general x3 -> x6, matrix products: 76.8 us -> 30.5 us  [the longest x2 11.1 us: on_device(): lax.dot_general(cot_rows, weight_cols, (((1,), (1,)), ((), ())), preferre...]
    unnamed x4 -> x49, local copies, waits for them, and re-layouts: 0.01 us -> 15.6 us
    concatenate x0 -> x7, other arithmetic: none -> 14.2 us  [the longest x2 5.13 us: on_device(): pair = jnp.concatenate([weight, swap(weight, 2)], axis=1)]
  transfers between devices with their start and end apart: 4 -> 40, of which waited for: 3 -> 22; matrix products, arithmetic and copies ran while one was open for 7% -> 19% of each run, Pallas kernels for 0% -> 0%
where the time goes in v1:
time: 427 us; the launch traced here: 425 us
  waiting for transfers between devices  267 us (63%)
  starting transfers between devices  62.5 us (15%)
  other arithmetic  36.8 us (9%)
  matrix products  30.5 us (7%)
  local copies, waits for them, and re-layouts  27.5 us (6%)
    ppermute x24, waiting for transfers between devices, hop(): return lax.ppermute(value, 'hst', pairs)  129 us
    ppermute x8, waiting for transfers between devices, swap(): return lax.ppermute(value, 'hst', [(h, h ^ bit) for h in range(n_hst)])  104 us
    ppermute x24, starting transfers between devices, hop(): return lax.ppermute(value, 'hst', pairs)  47.1 us
    ppermute x6, waiting for transfers between devices, shift(): return lax.ppermute(value, 'hst', pairs)  33 us
    unnamed x49, local copies, waits for them, and re-layouts  15.6 us
    dot_general x2, matrix products, on_device(): lax.dot_general(cot_rows, weight_cols, (((1,), (1,)), ((), ())), preferre...  11.1 us
    dot_general x2, matrix products, on_device(): jnp.dot(hidden_rows, weight_cols, preferred_element_type=jnp.float32)  10.6 us
    dot_general x2, matrix products, on_device(): lax.dot_general(hidden_rows, cot_rows, (((0,), (0,)), ((), ())), preferre...  8.75 us
  transfers between devices with their start and end apart: 40, of which 22 were waited for; matrix products, arithmetic and copies ran while one was open for 19% of the time, Pallas kernels for 0%

profile of v1, /device:TPU:8, one launch (start us, length us, event | category | flops | bytes accessed | tf_op | source)
XLA Modules:
  0.0 425.5 jit_solution(17527259524286448303)
XLA Ops:
  5.7 29.5 %collective-permute-done.14 = bf16[2688,256]{1,0:T(8,128)(2,1)S(1)} collective-permute-done((bf16[2688,256]{1,0:T(8,128)(2,1)S(1)}, bf16[2688,256]{1,0:T(8,128)(2,1)S(1)}, u32[]{:S(2)}, u32[]{:S(2)}) %collective-permute-start.14) | collective-permute-done | bytes 1376288 | tf_op jit(solution)/shard_map/ppermute | solution.py:21
  35.2 2.0 pad_maximum_fusion.6
  40.1 25.0 %collective-permute-done.6 = bf16[2816,256]{1,0:T(8,128)(2,1)} collective-permute-done((bf16[2816,256]{1,0:T(8,128)(2,1)S(1)}, bf16[2816,256]{1,0:T(8,128)(2,1)}, u32[]{:S(2)}, u32[]{:S(2)}) %collective-permute-start.6) | collective-permute-done | bytes 1441824 | tf_op jit(solution)/shard_map/ppermute | solution.py:21
  65.1 3.1 pad_maximum_fusion.4
  68.2 4.2 fusion.27
  80.0 2.6 collective-permute-start.22
  82.8 14.8 %collective-permute-done.23 = bf16[128,1024]{1,0:T(8,128)(2,1)} collective-permute-done((bf16[128,1024]{1,0:T(8,128)(2,1)}, bf16[128,1024]{1,0:T(8,128)(2,1)}, u32[]{:S(2)}, u32[]{:S(2)}) %collective-permute-start.23) | collective-permute-done | bytes 262176 | tf_op jit(solution)/shard_map/ppermute | solution.py:25
  97.6 5.4 %collective-permute-done.22 = bf16[128,1024]{1,0:T(8,128)(2,1)} collective-permute-done((bf16[128,1024]{1,0:T(8,128)(2,1)}, bf16[128,1024]{1,0:T(8,128)(2,1)}, u32[]{:S(2)}, u32[]{:S(2)}) %collective-permute-start.22) | collective-permute-done | bytes 262176 | tf_op jit(solution)/shard_map/ppermute | solution.py:25
  103.0 5.6 %fusion.2 = f32[512,2688]{1,0:T(8,128)S(1)} fusion(bf16[2688,512]{1,0:T(8,128)(2,1)} %collective-permute-done.15, bf16[2688,256]{1,0:T(8,128)(2,1)} %copy-done.10, bf16[2688,256]{1,0:T(8,128)(2,1)S(1)} %slice.87, bf16[128,1024]{1,0:T(8,128)(2,1)} %collective-permute-done.23, bf16[128,1024]{1,0:T(8,128)(2,1)} %collective-permute-done.22, ...), kind=kOutput, calls=%fused_computation.25 | convolution fusion | flops 2839281664 | bytes 12058624 | tf_op jit(solution)/shard_map/dot_general | solution.py:98
  110.8 5.5 %fusion = f32[512,2816]{1,0:T(8,128)S(1)} fusion(bf16[2816,512]{1,0:T(8,128)(2,1)} %collective-permute-done.7, bf16[2816,256]{1,0:T(8,128)(2,1)} %collective-permute-done.6, bf16[2816,256]{1,0:T(8,128)(2,1)S(1)} %slice.84, bf16[128,1024]{1,0:T(8,128)(2,1)} %collective-permute-done.23, bf16[128,1024]{1,0:T(8,128)(2,1)} %collective-permute-done.22, ...), kind=kOutput, calls=%fused_computation.23 | convolution fusion | flops 2974285824 | bytes 12582912 | tf_op jit(solution)/shard_map/dot_general | solution.py:98
  118.4 11.0 %collective-permute-done.30 = bf16[128,2688]{1,0:T(8,128)(2,1)S(1)} collective-permute-done((bf16[128,2688]{1,0:T(8,128)(2,1)S(1)}, bf16[128,2688]{1,0:T(8,128)(2,1)S(1)}, u32[]{:S(2)}, u32[]{:S(2)}) %collective-permute-start.30) | collective-permute-done | bytes 688160 | tf_op jit(solution)/shard_map/ppermute | solution.py:29
  131.5 13.4 %collective-permute-done.24 = bf16[128,2816]{1,0:T(8,128)(2,1)S(1)} collective-permute-done((bf16[128,2816]{1,0:T(8,128)(2,1)S(1)}, bf16[128,2816]{1,0:T(8,128)(2,1)S(1)}, u32[]{:S(2)}, u32[]{:S(2)}) %collective-permute-start.24) | collective-permute-done | bytes 720928 | tf_op jit(solution)/shard_map/ppermute | solution.py:29
  147.0 12.7 %collective-permute-done.31 = bf16[128,2688]{1,0:T(8,128)(2,1)S(1)} collective-permute-done((bf16[128,2688]{1,0:T(8,128)(2,1)S(1)}, bf16[128,2688]{1,0:T(8,128)(2,1)S(1)}, u32[]{:S(2)}, u32[]{:S(2)}) %collective-permute-start.31) | collective-permute-done | bytes 688160 | tf_op jit(solution)/shard_map/ppermute | solution.py:29
  159.9 1.9 collective-permute-start.32
  163.3 11.8 %collective-permute-done.25 = bf16[128,2816]{1,0:T(8,128)(2,1)S(1)} collective-permute-done((bf16[128,2816]{1,0:T(8,128)(2,1)S(1)}, bf16[128,2816]{1,0:T(8,128)(2,1)S(1)}, u32[]{:S(2)}, u32[]{:S(2)}) %collective-permute-start.25) | collective-permute-done | bytes 720928 | tf_op jit(solution)/shard_map/ppermute | solution.py:29
  180.1 2.3 collective-permute-start.35
  182.4 15.9 %collective-permute-done.28 = bf16[128,2816]{1,0:T(8,128)(2,1)S(1)} collective-permute-done((bf16[128,2816]{1,0:T(8,128)(2,1)S(1)}, bf16[128,2816]{1,0:T(8,128)(2,1)S(1)}, u32[]{:S(2)}, u32[]{:S(2)}) %collective-permute-start.28) | collective-permute-done | bytes 720928 | tf_op jit(solution)/shard_map/ppermute | solution.py:29
  200.4 12.7 %collective-permute-done.35 = bf16[128,2688]{1,0:T(8,128)(2,1)S(1)} collective-permute-done((bf16[128,2688]{1,0:T(8,128)(2,1)S(1)}, bf16[128,2688]{1,0:T(8,128)(2,1)S(1)}, u32[]{:S(2)}, u32[]{:S(2)}) %collective-permute-start.35) | collective-permute-done | bytes 688160 | tf_op jit(solution)/shard_map/ppermute | solution.py:29
  213.1 2.1 fusion.24
  217.1 4.8 %collective-permute-start.8 = (bf16[128,2688]{1,0:T(8,128)(2,1)S(1)}, bf16[128,2688]{1,0:T(8,128)(2,1)}, u32[]{:S(2)}, u32[]{:S(2)}) collective-permute-start(bf16[128,2688]{1,0:T(8,128)(2,1)S(1)} %get-tuple-element.24), channel_id=1, source_target_pairs={{8,0},{10,2},{12,4},{14,6},{16,8},{18,10},{20,12},{22,14},{24,16},... | collective-permute-start | bytes 2064392 | tf_op jit(solution)/shard_map/ppermute | solution.py:29
  221.9 6.6 %collective-permute-done.29 = bf16[128,2816]{1,0:T(8,128)(2,1)S(1)} collective-permute-done((bf16[128,2816]{1,0:T(8,128)(2,1)S(1)}, bf16[128,2816]{1,0:T(8,128)(2,1)S(1)}, u32[]{:S(2)}, u32[]{:S(2)}) %collective-permute-start.29) | collective-permute-done | bytes 720928 | tf_op jit(solution)/shard_map/ppermute | solution.py:29
  228.5 2.1 fusion.13
  232.5 4.8 %collective-permute-start = (bf16[128,2816]{1,0:T(8,128)(2,1)}, bf16[128,2816]{1,0:T(8,128)(2,1)}, u32[]{:S(2)}, u32[]{:S(2)}) collective-permute-start(bf16[128,2816]{1,0:T(8,128)(2,1)} %get-tuple-element.25), channel_id=1, source_target_pairs={{8,0},{10,2},{12,4},{14,6},{16,8},{18,10},{20,12},{22,14},{24,16},... | collective-permute-start | bytes 2162696 | tf_op jit(solution)/shard_map/ppermute | solution.py:29
  237.3 2.2 collective-permute-start.10
  239.5 3.8 collective-permute-done.8
  245.4 4.0 collective-permute-done.1
  249.4 4.4 %collective-permute-start.2 = (bf16[128,2816]{1,0:T(8,128)(2,1)}, bf16[128,2816]{1,0:T(8,128)(2,1)S(1)}, u32[]{:S(2)}, u32[]{:S(2)}) collective-permute-start(bf16[128,2816]{1,0:T(8,128)(2,1)} %collective-permute-done.1), channel_id=1, source_target_pairs={{8,16},{10,18},{12,20},{14,22},{16,24},{18,26},{20,28},{22,30},{9,... | collective-permute-start | bytes 2162696 | tf_op jit(solution)/shard_map/ppermute | solution.py:29
  253.8 5.0 %collective-permute-done = bf16[128,2816]{1,0:T(8,128)(2,1)} collective-permute-done((bf16[128,2816]{1,0:T(8,128)(2,1)}, bf16[128,2816]{1,0:T(8,128)(2,1)}, u32[]{:S(2)}, u32[]{:S(2)}) %collective-permute-start) | collective-permute-done | bytes 720928 | tf_op jit(solution)/shard_map/ppermute | solution.py:29
  260.7 3.5 collective-permute-done.10
  264.9 8.7 %collective-permute-done.12 = bf16[128,2688]{1,0:T(8,128)(2,1)} collective-permute-done((bf16[128,2688]{1,0:T(8,128)(2,1)}, bf16[128,2688]{1,0:T(8,128)(2,1)}, u32[]{:S(2)}, u32[]{:S(2)}) %collective-permute-start.12) | collective-permute-done | bytes 688160 | tf_op jit(solution)/shard_map/ppermute | solution.py:29
  276.8 10.0 %collective-permute-done.4 = bf16[128,2816]{1,0:T(8,128)(2,1)S(1)} collective-permute-done((bf16[128,2816]{1,0:T(8,128)(2,1)}, bf16[128,2816]{1,0:T(8,128)(2,1)S(1)}, u32[]{:S(2)}, u32[]{:S(2)}) %collective-permute-start.4) | collective-permute-done | bytes 720928 | tf_op jit(solution)/shard_map/ppermute | solution.py:29
  290.2 9.0 %collective-permute-done.13 = bf16[128,2688]{1,0:T(8,128)(2,1)S(1)} collective-permute-done((bf16[128,2688]{1,0:T(8,128)(2,1)}, bf16[128,2688]{1,0:T(8,128)(2,1)S(1)}, u32[]{:S(2)}, u32[]{:S(2)}) %collective-permute-start.13) | collective-permute-done | bytes 688160 | tf_op jit(solution)/shard_map/ppermute | solution.py:29
  300.3 4.2 fusion.30
  304.5 4.0 copy-done.4
  308.6 2.0 slice.175
  310.5 5.0 %fusion.3 = f32[512,1024]{1,0:T(8,128)S(1)} fusion(bf16[2688,512]{1,0:T(8,128)(2,1)} %collective-permute-done.15, bf16[2688,256]{1,0:T(8,128)(2,1)S(1)} %copy-done.11, bf16[2688,256]{1,0:T(8,128)(2,1)S(1)} %slice.87, bf16[128,2688]{1,0:T(8,128)(2,1)S(1)} %broadcast_select_fusion.3, bf16[128,2688]{1,0:T(8,128)(2,1)S(1)} %broadcast_select_fusion.4, ...), kind=kOutput, calls=%fused_computation.26 | convolution fusion | flops 2846097408 | bytes 10354688 | tf_op jit(solution)/shard_map/dot_general | solution.py:110
  318.0 5.6 %add_convert_fusion = bf16[512,1024]{1,0:T(8,128)(2,1)S(1)} fusion(f32[512,1024]{1,0:T(8,128)S(1)} %fusion.3, bf16[2816,512]{1,0:T(8,128)(2,1)} %collective-permute-done.7, bf16[2816,256]{1,0:T(8,128)(2,1)} %collective-permute-done.6, bf16[2816,256]{1,0:T(8,128)(2,1)S(1)} %slice.84, bf16[128,2816]{1,0:T(8,128)(2,1)S(1)} %broadcast_select_fusion, ...), kind=kOutput, calls=%fused_computation.27 | convolution fusion | flops 2982674432 | bytes 11796480 | tf_op jit(solution)/shard_map/dot_general | solution.py:110
  323.7 2.5 collective-permute-start.17
  326.3 4.6 %fusion.29 = f32[2816,1024]{1,0:T(8,128)S(1)} fusion(bf16[128,2816]{1,0:T(8,128)(2,1)S(1)} %broadcast_select_fusion, bf16[128,2816]{1,0:T(8,128)(2,1)S(1)} %broadcast_select_fusion.1, bf16[128,2816]{1,0:T(8,128)(2,1)S(1)} %broadcast_select_fusion.2, bf16[128,2816]{1,0:T(8,128)(2,1)} %get-tuple-element.25, bf16[128,1024]{1,0:T(8,128)(2,1)} %collective-permute-done.23, ...), kind=kOutput, calls=%fused_computation.87 | convolution fusion | flops 2968518656 | bytes 15466496 | tf_op jit(solution)/shard_map/dot_general | solution.py:113
  330.9 4.2 copy-done.3
  335.1 2.0 slice.174
  337.1 12.8 %collective-permute-done.16 = bf16[128,1024]{1,0:T(8,128)(2,1)S(1)} collective-permute-done((bf16[128,1024]{1,0:T(8,128)(2,1)S(1)}, bf16[128,1024]{1,0:T(8,128)(2,1)S(1)}, u32[]{:S(2)}, u32[]{:S(2)}) %collective-permute-start.16) | collective-permute-done | bytes 262176 | tf_op jit(solution)/shard_map/ppermute | solution.py:25
  352.7 5.0 %slice_add_fusion.1 = f32[2688,512]{1,0:T(8,128)S(1)} fusion(f32[2688,1024]{1,0:T(8,128)} %copy-done.4, bf16[2688,512]{1,0:T(8,128)(2,1)} %collective-permute-done.38), kind=kLoop, calls=%fused_computation.5 | loop fusion | flops 2752512 | bytes 13762560 | tf_op jit(solution)/shard_map/add | solution.py:117
  360.8 3.0 slice_add_fusion
  369.7 22.9 %collective-permute-done.39 = bf16[2688,256]{1,0:T(8,128)(2,1)} collective-permute-done((bf16[2688,256]{1,0:T(8,128)(2,1)}, bf16[2688,256]{1,0:T(8,128)(2,1)}, u32[]{:S(2)}, u32[]{:S(2)}) %collective-permute-start.39) | collective-permute-done | bytes 1376288 | tf_op jit(solution)/shard_map/ppermute | solution.py:21
  392.6 2.5 slice_add_fusion.3
  395.1 27.1 %collective-permute-done.37 = bf16[2816,256]{1,0:T(8,128)(2,1)S(1)} collective-permute-done((bf16[2816,256]{1,0:T(8,128)(2,1)}, bf16[2816,256]{1,0:T(8,128)(2,1)S(1)}, u32[]{:S(2)}, u32[]{:S(2)}) %collective-permute-start.37) | collective-permute-done | bytes 1441824 | tf_op jit(solution)/shard_map/ppermute | solution.py:21
  422.6 2.9 pad_maximum_fusion.1
  (130 shorter events, 63.5 us)
Async XLA Ops:
  2.1 33.1 %collective-permute-start.14 = (bf16[2688,256]{1,0:T(8,128)(2,1)S(1)}, bf16[2688,256]{1,0:T(8,128)(2,1)S(1)}, u32[]{:S(2)}, u32[]{:S(2)}) collective-permute-start(bf16[2688,256]{1,0:T(8,128)(2,1)S(1)} %slice.87), channel_id=1, source_target_pairs={{0,4},{2,6},{4,0},{6,2},{8,12},{10,14},{12,8},{14,10},{16,20},{18,... | collective-permute-start | bytes 4128776 | tf_op jit(solution)/shard_map/ppermute | solution.py:21
  5.1 59.9 %collective-permute-start.6 = (bf16[2816,256]{1,0:T(8,128)(2,1)S(1)}, bf16[2816,256]{1,0:T(8,128)(2,1)}, u32[]{:S(2)}, u32[]{:S(2)}) collective-permute-start(bf16[2816,256]{1,0:T(8,128)(2,1)S(1)} %slice.84), channel_id=1, source_target_pairs={{0,4},{2,6},{4,0},{6,2},{8,12},{10,14},{12,8},{14,10},{16,20},{18,... | collective-permute-start | bytes 4325384 | tf_op jit(solution)/shard_map/ppermute | solution.py:21
  37.2 65.8 %collective-permute-start.15 = (bf16[2688,512]{1,0:T(8,128)(2,1)}, bf16[2688,512]{1,0:T(8,128)(2,1)}, u32[]{:S(2)}, u32[]{:S(2)}) collective-permute-start(bf16[2688,512]{1,0:T(8,128)(2,1)} %pad_maximum_fusion.6), channel_id=1, source_target_pairs={{0,2},{2,0},{4,6},{6,4},{8,10},{10,8},{12,14},{14,12},{16,18},{18,... | collective-permute-start | bytes 8257544 | tf_op jit(solution)/shard_map/ppermute | solution.py:21
  38.5 29.7 %collective-permute-start.20 = (bf16[128,2048]{0,1:T(8,128)(2,1)S(1)}, bf16[128,2048]{0,1:T(8,128)(2,1)}, u32[]{:S(2)}, u32[]{:S(2)}) collective-permute-start(bf16[128,2048]{0,1:T(8,128)(2,1)S(1)} %copy.11), channel_id=1, source_target_pairs={{0,1},{1,0},{2,3},{3,2},{4,5},{5,4},{6,7},{7,6},{8,9},{9,8},{10,11... | collective-permute-start | bytes 1572872 | tf_op jit(solution)/shard_map/ppermute | solution.py:32
  68.2 42.5 %collective-permute-start.7 = (bf16[2816,512]{1,0:T(8,128)(2,1)}, bf16[2816,512]{1,0:T(8,128)(2,1)}, u32[]{:S(2)}, u32[]{:S(2)}) collective-permute-start(bf16[2816,512]{1,0:T(8,128)(2,1)} %pad_maximum_fusion.4), channel_id=1, source_target_pairs={{0,2},{2,0},{4,6},{6,4},{8,10},{10,8},{12,14},{14,12},{16,18},{18,... | collective-permute-start | bytes 8650760 | tf_op jit(solution)/shard_map/ppermute | solution.py:21
  78.0 19.6 %collective-permute-start.23 = (bf16[128,1024]{1,0:T(8,128)(2,1)}, bf16[128,1024]{1,0:T(8,128)(2,1)}, u32[]{:S(2)}, u32[]{:S(2)}) collective-permute-start(bf16[128,1024]{1,0:T(8,128)(2,1)} %bitcast.26), channel_id=1, source_target_pairs={{0,8},{2,10},{4,12},{6,14},{8,16},{10,18},{12,20},{14,22},{16,24},... | collective-permute-start | bytes 786440 | tf_op jit(solution)/shard_map/ppermute | solution.py:25
  79.6 18.0 %collective-permute-start.21 = (bf16[128,1024]{1,0:T(8,128)(2,1)}, bf16[128,1024]{1,0:T(8,128)(2,1)}, u32[]{:S(2)}, u32[]{:S(2)}) collective-permute-start(bf16[128,1024]{1,0:T(8,128)(2,1)} %bitcast.25), channel_id=1, source_target_pairs={{0,24},{2,26},{4,28},{6,30},{8,0},{10,2},{12,4},{14,6},{16,8},{18,... | collective-permute-start | bytes 786440 | tf_op jit(solution)/shard_map/ppermute | solution.py:25
  80.0 23.0 %collective-permute-start.22 = (bf16[128,1024]{1,0:T(8,128)(2,1)}, bf16[128,1024]{1,0:T(8,128)(2,1)}, u32[]{:S(2)}, u32[]{:S(2)}) collective-permute-start(bf16[128,1024]{1,0:T(8,128)(2,1)} %bitcast.24), channel_id=1, source_target_pairs={{0,16},{2,18},{4,20},{6,22},{8,24},{10,26},{12,28},{14,30},{16,0},... | collective-permute-start | bytes 786440 | tf_op jit(solution)/shard_map/ppermute | solution.py:25
  82.7 28.0 %copy-start.14 = (bf16[128,1,1024]{2,0,1:T(8,128)(2,1)}, bf16[128,1,1024]{2,0,1:T(8,128)(2,1)S(1)}, u32[]{:S(2)}) copy-start(bf16[128,1,1024]{2,0,1:T(8,128)(2,1)S(1)} %copy.18) | copy-start | bytes 786436
  108.7 20.7 %collective-permute-start.30 = (bf16[128,2688]{1,0:T(8,128)(2,1)S(1)}, bf16[128,2688]{1,0:T(8,128)(2,1)S(1)}, u32[]{:S(2)}, u32[]{:S(2)}) collective-permute-start(bf16[128,2688]{1,0:T(8,128)(2,1)S(1)} %get-tuple-element.22), channel_id=1, source_target_pairs={{0,8},{2,10},{4,12},{6,14},{1,9},{3,11},{5,13},{7,15}} | collective-permute-start | bytes 2064392 | tf_op jit(solution)/shard_map/ppermute | solution.py:29
  110.0 36.9 %collective-permute-start.33 = (bf16[128,2688]{1,0:T(8,128)(2,1)S(1)}, bf16[128,2688]{1,0:T(8,128)(2,1)S(1)}, u32[]{:S(2)}, u32[]{:S(2)}) collective-permute-start(bf16[128,2688]{1,0:T(8,128)(2,1)S(1)} %get-tuple-element.23), channel_id=1, source_target_pairs={{24,16},{26,18},{28,20},{30,22},{25,17},{27,19},{29,21},{31,23}} | collective-permute-start | bytes 2064392 | tf_op jit(solution)/shard_map/ppermute | solution.py:29
  116.4 28.5 %collective-permute-start.24 = (bf16[128,2816]{1,0:T(8,128)(2,1)S(1)}, bf16[128,2816]{1,0:T(8,128)(2,1)S(1)}, u32[]{:S(2)}, u32[]{:S(2)}) collective-permute-start(bf16[128,2816]{1,0:T(8,128)(2,1)S(1)} %get-tuple-element.18), channel_id=1, source_target_pairs={{0,8},{2,10},{4,12},{6,14},{1,9},{3,11},{5,13},{7,15}} | collective-permute-start | bytes 2162696 | tf_op jit(solution)/shard_map/ppermute | solution.py:29
  117.7 45.6 %collective-permute-start.27 = (bf16[128,2816]{1,0:T(8,128)(2,1)S(1)}, bf16[128,2816]{1,0:T(8,128)(2,1)S(1)}, u32[]{:S(2)}, u32[]{:S(2)}) collective-permute-start(bf16[128,2816]{1,0:T(8,128)(2,1)S(1)} %get-tuple-element.19), channel_id=1, source_target_pairs={{24,16},{26,18},{28,20},{30,22},{25,17},{27,19},{29,21},{31,23}} | collective-permute-start | bytes 2162696 | tf_op jit(solution)/shard_map/ppermute | solution.py:29
  129.6 30.1 %collective-permute-start.31 = (bf16[128,2688]{1,0:T(8,128)(2,1)S(1)}, bf16[128,2688]{1,0:T(8,128)(2,1)S(1)}, u32[]{:S(2)}, u32[]{:S(2)}) collective-permute-start(bf16[128,2688]{1,0:T(8,128)(2,1)S(1)} %add_convert_fusion.8), channel_id=1, source_target_pairs={{0,8},{2,10},{4,12},{6,14},{8,16},{10,18},{12,20},{14,22},{1,9},{3... | collective-permute-start | bytes 2064392 | tf_op jit(solution)/shard_map/ppermute | solution.py:29
  145.0 30.0 %collective-permute-start.25 = (bf16[128,2816]{1,0:T(8,128)(2,1)S(1)}, bf16[128,2816]{1,0:T(8,128)(2,1)S(1)}, u32[]{:S(2)}, u32[]{:S(2)}) collective-permute-start(bf16[128,2816]{1,0:T(8,128)(2,1)S(1)} %add_convert_fusion.4), channel_id=1, source_target_pairs={{0,8},{2,10},{4,12},{6,14},{8,16},{10,18},{12,20},{14,22},{1,9},{3... | collective-permute-start | bytes 2162696 | tf_op jit(solution)/shard_map/ppermute | solution.py:29
  159.9 40.5 %collective-permute-start.32 = (bf16[128,2688]{1,0:T(8,128)(2,1)S(1)}, bf16[128,2688]{1,0:T(8,128)(2,1)S(1)}, u32[]{:S(2)}, u32[]{:S(2)}) collective-permute-start(bf16[128,2688]{1,0:T(8,128)(2,1)S(1)} %get-tuple-element.20), channel_id=1, source_target_pairs={{0,8},{2,10},{4,12},{6,14},{8,16},{10,18},{12,20},{14,22},{16,24},... | collective-permute-start | bytes 2064392 | tf_op jit(solution)/shard_map/ppermute | solution.py:29
  161.8 18.2 %collective-permute-start.34 = (bf16[128,2688]{1,0:T(8,128)(2,1)S(1)}, bf16[128,2688]{1,0:T(8,128)(2,1)S(1)}, u32[]{:S(2)}, u32[]{:S(2)}) collective-permute-start(bf16[128,2688]{1,0:T(8,128)(2,1)S(1)} %get-tuple-element.21), channel_id=1, source_target_pairs={{16,8},{18,10},{20,12},{22,14},{24,16},{26,18},{28,20},{30,22},{17... | collective-permute-start | bytes 2064392 | tf_op jit(solution)/shard_map/ppermute | solution.py:29
  175.4 46.4 %collective-permute-start.26 = (bf16[128,2816]{1,0:T(8,128)(2,1)S(1)}, bf16[128,2816]{1,0:T(8,128)(2,1)S(1)}, u32[]{:S(2)}, u32[]{:S(2)}) collective-permute-start(bf16[128,2816]{1,0:T(8,128)(2,1)S(1)} %get-tuple-element.16), channel_id=1, source_target_pairs={{0,8},{2,10},{4,12},{6,14},{8,16},{10,18},{12,20},{14,22},{16,24},... | collective-permute-start | bytes 2162696 | tf_op jit(solution)/shard_map/ppermute | solution.py:29
  177.3 21.0 %collective-permute-start.28 = (bf16[128,2816]{1,0:T(8,128)(2,1)S(1)}, bf16[128,2816]{1,0:T(8,128)(2,1)S(1)}, u32[]{:S(2)}, u32[]{:S(2)}) collective-permute-start(bf16[128,2816]{1,0:T(8,128)(2,1)S(1)} %get-tuple-element.17), channel_id=1, source_target_pairs={{16,8},{18,10},{20,12},{22,14},{24,16},{26,18},{28,20},{30,22},{17... | collective-permute-start | bytes 2162696 | tf_op jit(solution)/shard_map/ppermute | solution.py:29
  180.1 33.0 %copy-start.8 = (bf16[128,5504]{1,0:T(8,128)(2,1)S(1)}, bf16[128,5504]{1,0:T(8,128)(2,1)}, u32[]{:S(2)}) copy-start(bf16[128,5504]{1,0:T(8,128)(2,1)} %param.4) | copy-start | bytes 4227076
  180.1 33.0 %copy-start.9 = (bf16[128,5504]{1,0:T(8,128)(2,1)S(1)}, bf16[128,5504]{1,0:T(8,128)(2,1)}, u32[]{:S(2)}) copy-start(bf16[128,5504]{1,0:T(8,128)(2,1)} %param.5) | copy-start | bytes 4227076
  180.1 32.9 %collective-permute-start.35 = (bf16[128,2688]{1,0:T(8,128)(2,1)S(1)}, bf16[128,2688]{1,0:T(8,128)(2,1)S(1)}, u32[]{:S(2)}, u32[]{:S(2)}) collective-permute-start(bf16[128,2688]{1,0:T(8,128)(2,1)S(1)} %add_convert_fusion.5), channel_id=1, source_target_pairs={{8,0},{10,2},{12,4},{14,6},{16,8},{18,10},{20,12},{22,14},{24,16},... | collective-permute-start | bytes 2064392 | tf_op jit(solution)/shard_map/ppermute | solution.py:29
  198.5 30.0 %collective-permute-start.29 = (bf16[128,2816]{1,0:T(8,128)(2,1)S(1)}, bf16[128,2816]{1,0:T(8,128)(2,1)S(1)}, u32[]{:S(2)}, u32[]{:S(2)}) collective-permute-start(bf16[128,2816]{1,0:T(8,128)(2,1)S(1)} %add_convert_fusion.1), channel_id=1, source_target_pairs={{8,0},{10,2},{12,4},{14,6},{16,8},{18,10},{20,12},{22,14},{24,16},... | collective-permute-start | bytes 2162696 | tf_op jit(solution)/shard_map/ppermute | solution.py:29
  215.2 15.5 %copy-start.12 = (bf16[128,2688]{1,0:T(8,128)(2,1)}, bf16[128,2688]{1,0:T(8,128)(2,1)S(1)}, u32[]{:S(2)}) copy-start(bf16[128,2688]{1,0:T(8,128)(2,1)S(1)} %get-tuple-element.24) | copy-start | bytes 2064388
  215.2 22.2 %collective-permute-start.9 = (bf16[128,2688]{1,0:T(8,128)(2,1)S(1)}, bf16[128,2688]{1,0:T(8,128)(2,1)}, u32[]{:S(2)}, u32[]{:S(2)}) collective-permute-start(bf16[128,2688]{1,0:T(8,128)(2,1)S(1)} %get-tuple-element.24), channel_id=1, source_target_pairs={{0,8},{2,10},{4,12},{6,14},{8,16},{10,18},{12,20},{14,22},{16,24},... | collective-permute-start | bytes 2064392 | tf_op jit(solution)/shard_map/ppermute | solution.py:29
  217.1 26.3 %collective-permute-start.8 = (bf16[128,2688]{1,0:T(8,128)(2,1)S(1)}, bf16[128,2688]{1,0:T(8,128)(2,1)}, u32[]{:S(2)}, u32[]{:S(2)}) collective-permute-start(bf16[128,2688]{1,0:T(8,128)(2,1)S(1)} %get-tuple-element.24), channel_id=1, source_target_pairs={{8,0},{10,2},{12,4},{14,6},{16,8},{18,10},{20,12},{22,14},{24,16},... | collective-permute-start | bytes 2064392 | tf_op jit(solution)/shard_map/ppermute | solution.py:29
  230.6 18.8 %collective-permute-start.1 = (bf16[128,2816]{1,0:T(8,128)(2,1)}, bf16[128,2816]{1,0:T(8,128)(2,1)}, u32[]{:S(2)}, u32[]{:S(2)}) collective-permute-start(bf16[128,2816]{1,0:T(8,128)(2,1)} %get-tuple-element.25), channel_id=1, source_target_pairs={{0,8},{2,10},{4,12},{6,14},{8,16},{10,18},{12,20},{14,22},{16,24},... | collective-permute-start | bytes 2162696 | tf_op jit(solution)/shard_map/ppermute | solution.py:29
  232.5 26.3 %collective-permute-start = (bf16[128,2816]{1,0:T(8,128)(2,1)}, bf16[128,2816]{1,0:T(8,128)(2,1)}, u32[]{:S(2)}, u32[]{:S(2)}) collective-permute-start(bf16[128,2816]{1,0:T(8,128)(2,1)} %get-tuple-element.25), channel_id=1, source_target_pairs={{8,0},{10,2},{12,4},{14,6},{16,8},{18,10},{20,12},{22,14},{24,16},... | collective-permute-start | bytes 2162696 | tf_op jit(solution)/shard_map/ppermute | solution.py:29
  237.3 26.8 %collective-permute-start.10 = (bf16[128,2688]{1,0:T(8,128)(2,1)}, bf16[128,2688]{1,0:T(8,128)(2,1)}, u32[]{:S(2)}, u32[]{:S(2)}) collective-permute-start(bf16[128,2688]{1,0:T(8,128)(2,1)} %collective-permute-done.9), channel_id=1, source_target_pairs={{8,16},{10,18},{12,20},{14,22},{16,24},{18,26},{20,28},{22,30},{9,... | collective-permute-start | bytes 2064392 | tf_op jit(solution)/shard_map/ppermute | solution.py:29
  243.3 30.2 %collective-permute-start.12 = (bf16[128,2688]{1,0:T(8,128)(2,1)}, bf16[128,2688]{1,0:T(8,128)(2,1)}, u32[]{:S(2)}, u32[]{:S(2)}) collective-permute-start(bf16[128,2688]{1,0:T(8,128)(2,1)} %collective-permute-done.8), channel_id=1, source_target_pairs={{8,0},{10,2},{12,4},{14,6},{16,8},{18,10},{20,12},{22,14},{9,1},{1... | collective-permute-start | bytes 2064392 | tf_op jit(solution)/shard_map/ppermute | solution.py:29
  249.4 26.6 %collective-permute-start.2 = (bf16[128,2816]{1,0:T(8,128)(2,1)}, bf16[128,2816]{1,0:T(8,128)(2,1)S(1)}, u32[]{:S(2)}, u32[]{:S(2)}) collective-permute-start(bf16[128,2816]{1,0:T(8,128)(2,1)} %collective-permute-done.1), channel_id=1, source_target_pairs={{8,16},{10,18},{12,20},{14,22},{16,24},{18,26},{20,28},{22,30},{9,... | collective-permute-start | bytes 2162696 | tf_op jit(solution)/shard_map/ppermute | solution.py:29
  258.8 28.0 %collective-permute-start.4 = (bf16[128,2816]{1,0:T(8,128)(2,1)}, bf16[128,2816]{1,0:T(8,128)(2,1)S(1)}, u32[]{:S(2)}, u32[]{:S(2)}) collective-permute-start(bf16[128,2816]{1,0:T(8,128)(2,1)} %collective-permute-done), channel_id=1, source_target_pairs={{8,0},{10,2},{12,4},{14,6},{16,8},{18,10},{20,12},{22,14},{9,1},{1... | collective-permute-start | bytes 2162696 | tf_op jit(solution)/shard_map/ppermute | solution.py:29
  264.2 24.7 %collective-permute-start.11 = (bf16[128,2688]{1,0:T(8,128)(2,1)}, bf16[128,2688]{1,0:T(8,128)(2,1)S(1)}, u32[]{:S(2)}, u32[]{:S(2)}) collective-permute-start(bf16[128,2688]{1,0:T(8,128)(2,1)} %collective-permute-done.10), channel_id=1, source_target_pairs={{16,24},{18,26},{20,28},{22,30},{17,25},{19,27},{21,29},{23,31}} | collective-permute-start | bytes 2064392 | tf_op jit(solution)/shard_map/ppermute | solution.py:29
  273.5 25.6 %collective-permute-start.13 = (bf16[128,2688]{1,0:T(8,128)(2,1)}, bf16[128,2688]{1,0:T(8,128)(2,1)S(1)}, u32[]{:S(2)}, u32[]{:S(2)}) collective-permute-start(bf16[128,2688]{1,0:T(8,128)(2,1)} %collective-permute-done.12), channel_id=1, source_target_pairs={{8,0},{10,2},{12,4},{14,6},{9,1},{11,3},{13,5},{15,7}} | collective-permute-start | bytes 2064392 | tf_op jit(solution)/shard_map/ppermute | solution.py:29
  276.1 39.5 %collective-permute-start.3 = (bf16[128,2816]{1,0:T(8,128)(2,1)S(1)}, bf16[128,2816]{1,0:T(8,128)(2,1)S(1)}, u32[]{:S(2)}, u32[]{:S(2)}) collective-permute-start(bf16[128,2816]{1,0:T(8,128)(2,1)S(1)} %collective-permute-done.2), channel_id=1, source_target_pairs={{16,24},{18,26},{20,28},{22,30},{17,25},{19,27},{21,29},{23,31}} | collective-permute-start | bytes 2162696 | tf_op jit(solution)/shard_map/ppermute | solution.py:29
  286.8 30.0 %collective-permute-start.5 = (bf16[128,2816]{1,0:T(8,128)(2,1)S(1)}, bf16[128,2816]{1,0:T(8,128)(2,1)S(1)}, u32[]{:S(2)}, u32[]{:S(2)}) collective-permute-start(bf16[128,2816]{1,0:T(8,128)(2,1)S(1)} %collective-permute-done.4), channel_id=1, source_target_pairs={{8,0},{10,2},{12,4},{14,6},{9,1},{11,3},{13,5},{15,7}} | collective-permute-start | bytes 2162696 | tf_op jit(solution)/shard_map/ppermute | solution.py:29
  288.8 11.5 %copy-start.13 = (bf16[128,2688]{1,0:T(8,128)(2,1)S(1)}, bf16[128,2688]{1,0:T(8,128)(2,1)}, u32[]{:S(2)}) copy-start(bf16[128,2688]{1,0:T(8,128)(2,1)} %copy-done.12) | copy-start | bytes 2064388
  288.8 11.5 %copy-start.15 = (bf16[128,1,1024]{2,0,1:T(8,128)(2,1)S(1)}, bf16[128,1,1024]{2,0,1:T(8,128)(2,1)}, u32[]{:S(2)}) copy-start(bf16[128,1,1024]{2,0,1:T(8,128)(2,1)} %copy-done.14) | copy-start | bytes 786436
  310.5 42.2 %collective-permute-start.38 = (bf16[2688,512]{1,0:T(8,128)(2,1)}, bf16[2688,512]{1,0:T(8,128)(2,1)}, u32[]{:S(2)}, u32[]{:S(2)}) collective-permute-start(bf16[2688,512]{1,0:T(8,128)(2,1)} %slice.175), channel_id=1, source_target_pairs={{0,2},{2,0},{4,6},{6,4},{8,10},{10,8},{12,14},{14,12},{16,18},{18,... | collective-permute-start | bytes 8257544 | tf_op jit(solution)/shard_map/ppermute | solution.py:21
  323.7 26.2 %collective-permute-start.18 = (bf16[128,1024]{1,0:T(8,128)(2,1)S(1)}, bf16[128,1024]{1,0:T(8,128)(2,1)S(1)}, u32[]{:S(2)}, u32[]{:S(2)}) collective-permute-start(bf16[128,1024]{1,0:T(8,128)(2,1)S(1)} %get-tuple-element.38), channel_id=1, source_target_pairs={{0,8},{2,10},{4,12},{6,14},{8,16},{10,18},{12,20},{14,22},{16,24},... | collective-permute-start | bytes 786440 | tf_op jit(solution)/shard_map/ppermute | solution.py:25
  323.7 26.1 %collective-permute-start.17 = (bf16[128,1024]{1,0:T(8,128)(2,1)S(1)}, bf16[128,1024]{1,0:T(8,128)(2,1)S(1)}, u32[]{:S(2)}, u32[]{:S(2)}) collective-permute-start(bf16[128,1024]{1,0:T(8,128)(2,1)S(1)} %get-tuple-element.40), channel_id=1, source_target_pairs={{0,16},{2,18},{4,20},{6,22},{8,24},{10,26},{12,28},{14,30},{16,0},... | collective-permute-start | bytes 786440 | tf_op jit(solution)/shard_map/ppermute | solution.py:25
  326.3 23.6 %collective-permute-start.16 = (bf16[128,1024]{1,0:T(8,128)(2,1)S(1)}, bf16[128,1024]{1,0:T(8,128)(2,1)S(1)}, u32[]{:S(2)}, u32[]{:S(2)}) collective-permute-start(bf16[128,1024]{1,0:T(8,128)(2,1)S(1)} %get-tuple-element.41), channel_id=1, source_target_pairs={{0,24},{2,26},{4,28},{6,30},{8,0},{10,2},{12,4},{14,6},{16,8},{18,... | collective-permute-start | bytes 786440 | tf_op jit(solution)/shard_map/ppermute | solution.py:25
  337.1 23.6 %collective-permute-start.36 = (bf16[2816,512]{1,0:T(8,128)(2,1)}, bf16[2816,512]{1,0:T(8,128)(2,1)}, u32[]{:S(2)}, u32[]{:S(2)}) collective-permute-start(bf16[2816,512]{1,0:T(8,128)(2,1)} %slice.174), channel_id=1, source_target_pairs={{0,2},{2,0},{4,6},{6,4},{8,10},{10,8},{12,14},{14,12},{16,18},{18,... | collective-permute-start | bytes 8650760 | tf_op jit(solution)/shard_map/ppermute | solution.py:21
  350.8 9.9 %slice-start = ((s8[11534336]{0:T(1024)(128)(4,1)}), s8[4194304]{0:T(1024)(128)(4,1)S(1)}, s32[]{:S(2)}) async-start(s8[11534336]{0:T(1024)(128)(4,1)} %bitcast.13), calls=%async_computation | async-start | bytes 8388608
  351.1 17.4 %collective-permute-start.19 = (bf16[128,2048]{0,1:T(8,128)(2,1)S(1)}, bf16[128,2048]{0,1:T(8,128)(2,1)S(1)}, u32[]{:S(2)}, u32[]{:S(2)}) collective-permute-start(bf16[128,2048]{0,1:T(8,128)(2,1)S(1)} %dynamic-slice_bitcast_fusion), channel_id=1, source_target_pairs={{0,1},{1,0},{2,3},{3,2},{4,5},{5,4},{6,7},{7,6},{8,9},{9,8},{10,11... | collective-permute-start | bytes 1572872 | tf_op jit(solution)/shard_map/ppermute | solution.py:32
  359.2 33.4 %collective-permute-start.39 = (bf16[2688,256]{1,0:T(8,128)(2,1)}, bf16[2688,256]{1,0:T(8,128)(2,1)}, u32[]{:S(2)}, u32[]{:S(2)}) collective-permute-start(bf16[2688,256]{1,0:T(8,128)(2,1)} %slice.177), channel_id=1, source_target_pairs={{0,4},{2,6},{4,0},{6,2},{8,12},{10,14},{12,8},{14,10},{16,20},{18,... | collective-permute-start | bytes 4128776 | tf_op jit(solution)/shard_map/ppermute | solution.py:21
  365.1 57.0 %collective-permute-start.37 = (bf16[2816,256]{1,0:T(8,128)(2,1)}, bf16[2816,256]{1,0:T(8,128)(2,1)S(1)}, u32[]{:S(2)}, u32[]{:S(2)}) collective-permute-start(bf16[2816,256]{1,0:T(8,128)(2,1)} %slice.176), channel_id=1, source_target_pairs={{0,4},{2,6},{4,0},{6,2},{8,12},{10,14},{12,8},{14,10},{16,20},{18,... | collective-permute-start | bytes 4325384 | tf_op jit(solution)/shard_map/ppermute | solution.py:21
  369.7 52.4 %copy-start.1 = (f32[2816,512]{1,0:T(8,128)S(1)}, f32[2816,512]{1,0:T(8,128)}, u32[]{:S(2)}) copy-start(f32[2816,512]{1,0:T(8,128)} %copy-done) | copy-start | bytes 17301508
  (11 other events, 47.8 us)

commit v2 on v1

--- a/solution.py
+++ b/solution.py
@@ -31,16 +31,10 @@
     def local_shift(value, step):
         return lax.ppermute(value, "local", [(i, (i + step) % n_local) for i in range(n_local)])
 
+    far_groups = [[f * QUAD + q for f in range(n_far)] for q in range(QUAD)]
+
     def gather_far(own, far):
-        above, below = {}, {}
-        up = down = own
-        for d in range(1, n_far):
-            up = below[d] = hop(up, 1, range(d - 1, n_far - 1))
-            down = above[d] = hop(down, -1, range(1, n_far - d + 1))
-        slots = [own]
-        for e in range(1, n_far):
-            slots.append(jnp.where(far + e < n_far, above[e], below[n_far - e]))
-        return jnp.concatenate(slots, axis=0)
+        return lax.all_gather(own, "hst", axis=0, tiled=True, axis_index_groups=far_groups)
 
     def reduce_far(slots):
         up = down = None
@@ -83,6 +77,11 @@
             [cot_for(0)] + [shift(cot_for(n_far - e), n_far - e) for e in range(1, n_far)], axis=0
         )
 
+        twice = jnp.concatenate([cot_rows, cot_rows[:-tokens]], axis=0)
+        cot_sorted = lax.dynamic_slice_in_dim(
+            twice, ((n_far - far) % n_far) * tokens, n_far * tokens, axis=0
+        )
+
         out_sum = 0.0
         gate_parts, up_parts, grad_parts = [], [], []
         for lo, hi in bounds:
@@ -111,7 +110,7 @@
                 hidden_rows, weight_cols, preferred_element_type=jnp.float32
             )
             grad = lax.dot_general(
-                hidden_rows, cot_rows, (((0,), (0,)), ((), ())), preferred_element_type=jnp.float32
+                hidden_rows, cot_sorted, (((0,), (0,)), ((), ())), preferred_element_type=jnp.float32
             )
             theirs = swap(grad[:, 2 * width :].astype(jnp.bfloat16), 1)
             grad = grad[:, : 2 * width] + theirs.astype(jnp.float32)
@@ -119,9 +118,15 @@
             grad_parts.append(grad[:, :width] + theirs.astype(jnp.float32))
 
         out_terms = out_sum.astype(jnp.bfloat16)
-        slots = [out_terms[:tokens]]
+
+        def out_for(step):
+            return lax.dynamic_slice_in_dim(
+                out_terms, ((far + step) % n_far) * tokens, tokens, axis=0
+            )
+
+        slots = [out_for(0)]
         for e in range(1, n_far):
-            slots.append(shift(out_terms[e * tokens : (e + 1) * tokens], e))
+            slots.append(shift(out_for(e), e))
         back = [slots[0]] + slots[:0:-1]
         twice = jnp.concatenate(back + back[:-1], axis=1)
         columns = QUAD * width

time: 427 us -> 452 us (1.059)
  starting transfers between devices: 62.5 us -> 41.8 us
  local copies, waits for them, and re-layouts: 27.5 us -> 44.6 us
  waiting for transfers between devices: 267 us -> 282 us
  between operations: 1.48 us -> 14.7 us
    all_gather x0 -> x2, waiting for transfers between devices: none -> 28.1 us  [gather_far(): lax.all_gather(own, 'hst', axis=0, tiled=True, axis_index_groups=far_groups)]
    ppermute x24 -> x12, starting transfers between devices: 47.1 us -> 23.8 us  [hop(): return lax.ppermute(value, 'hst', pairs)]
    ppermute x8, waiting for transfers between devices: 104 us -> 81.9 us  [swap(): return lax.ppermute(value, 'hst', [(h, h ^ bit) for h in range(n_hst)])]
    unnamed x49 -> x75, local copies, waits for them, and re-layouts: 15.6 us -> 29.8 us
    ppermute x2, waiting for transfers between devices: 0.01 us -> 12.7 us  [local_shift(): lax.ppermute(value, 'local', [(i, (i + step) % n_local) for i in range(n_...]
    select_n x6 -> x0, other arithmetic: 6.17 us -> none  [gather_far(): slots.append(jnp.where(far + e < n_far, above[e], below[n_far - e]))]
    ppermute x6, waiting for transfers between devices: 33 us -> 27 us  [shift(): return lax.ppermute(value, 'hst', pairs)]
    ppermute x24 -> x12, waiting for transfers between devices: 129 us -> 132 us  [hop(): return lax.ppermute(value, 'hst', pairs)]
  transfers between devices with their start and end apart: 40 -> 30, of which waited for: 22 -> 18; matrix products, arithmetic and copies ran while one was open for 19% -> 21% of each run, Pallas kernels for 0% -> 0%
where the time goes in v2:
time: 452 us; the launch traced here: 451 us
  waiting for transfers between devices  282 us (62%)
  local copies, waits for them, and re-layouts  44.6 us (10%)
  starting transfers between devices  41.8 us (9%)
  other arithmetic  34.6 us (8%)
  matrix products  33.6 us (7%)
  between operations  14.7 us (3%)
    ppermute x12, waiting for transfers between devices, hop(): return lax.ppermute(value, 'hst', pairs)  132 us
    ppermute x8, waiting for transfers between devices, swap(): return lax.ppermute(value, 'hst', [(h, h ^ bit) for h in range(n_hst)])  81.9 us
    unnamed x75, local copies, waits for them, and re-layouts  29.8 us
    all_gather x2, waiting for transfers between devices, gather_far(): lax.all_gather(own, 'hst', axis=0, tiled=True, axis_index_groups=far_groups)  28.1 us
    ppermute x6, waiting for transfers between devices, shift(): return lax.ppermute(value, 'hst', pairs)  27 us
    ppermute x12, starting transfers between devices, hop(): return lax.ppermute(value, 'hst', pairs)  23.8 us
    dot_general x2, matrix products, on_device(): jnp.dot(hidden_rows, weight_cols, preferred_element_type=jnp.float32)  13.3 us
    ppermute x2, waiting for transfers between devices, local_shift(): lax.ppermute(value, 'local', [(i, (i + step) % n_local) for i in range(n_...  12.7 us
  transfers between devices with their start and end apart: 30, of which 18 were waited for; matrix products, arithmetic and copies ran while one was open for 21% of the time, Pallas kernels for 0%

profile of v2, /device:TPU:8, one launch (start us, length us, event | category | flops | bytes accessed | tf_op | source)
XLA Modules:
  0.0 451.0 jit_solution(4017803849594269724)
XLA Ops:
  10.2 30.4 %collective-permute-done.2 = bf16[2688,256]{1,0:T(8,128)(2,1)S(1)} collective-permute-done((bf16[2688,256]{1,0:T(8,128)(2,1)S(1)}, bf16[2688,256]{1,0:T(8,128)(2,1)S(1)}, u32[]{:S(2)}, u32[]{:S(2)}) %collective-permute-start.2) | collective-permute-done | bytes 1376288 | tf_op jit(solution)/shard_map/ppermute | solution.py:21
  40.6 1.9 pad_maximum_fusion.4
  47.2 12.7 %collective-permute-done.8 = bf16[128,2048]{0,1:T(8,128)(2,1)} collective-permute-done((bf16[128,2048]{0,1:T(8,128)(2,1)S(1)}, bf16[128,2048]{0,1:T(8,128)(2,1)}, u32[]{:S(2)}, u32[]{:S(2)}) %collective-permute-start.8) | collective-permute-done | bytes 524320 | tf_op jit(solution)/shard_map/ppermute | solution.py:32
  59.9 4.2 fusion.27
  66.3 1.9 copy.20
  68.2 1.8 copy.19
  72.9 2.6 collective-permute-start.10
  78.5 12.2 %collective-permute-done.11 = bf16[128,1024]{1,0:T(8,128)(2,1)S(1)} collective-permute-done((bf16[128,1024]{1,0:T(8,128)(2,1)}, bf16[128,1024]{1,0:T(8,128)(2,1)S(1)}, u32[]{:S(2)}, u32[]{:S(2)}) %collective-permute-start.11) | collective-permute-done | bytes 262176 | tf_op jit(solution)/shard_map/ppermute | solution.py:25
  90.8 4.0 collective-permute-done.10
  94.8 5.1 %fusion.2 = f32[512,2688]{1,0:T(8,128)S(1)} fusion(bf16[2688,512]{1,0:T(8,128)(2,1)} %collective-permute-done.3, bf16[2688,256]{1,0:T(8,128)(2,1)S(1)} %copy-done.16, bf16[2688,256]{1,0:T(8,128)(2,1)S(1)} %slice.77, bf16[128,1024]{1,0:T(8,128)(2,1)S(1)} %collective-permute-done.11, bf16[128,1024]{1,0:T(8,128)(2,1)S(1)} %collective-permute-done.10, ...), kind=kOutput, calls=%fused_computation.23 | convolution fusion | flops 2839281664 | bytes 12058624 | tf_op jit(solution)/shard_map/dot_general | solution.py:97
  102.0 18.0 %collective-permute-done.18 = bf16[128,2688]{1,0:T(8,128)(2,1)S(1)} collective-permute-done((bf16[128,2688]{1,0:T(8,128)(2,1)S(1)}, bf16[128,2688]{1,0:T(8,128)(2,1)S(1)}, u32[]{:S(2)}, u32[]{:S(2)}) %collective-permute-start.18) | collective-permute-done | bytes 688160 | tf_op jit(solution)/shard_map/ppermute | solution.py:29
  120.1 1.9 collective-permute-start.19
  122.1 5.6 %fusion = f32[512,2816]{1,0:T(8,128)S(1)} fusion(bf16[2816,512]{1,0:T(8,128)(2,1)S(1)} %collective-permute-done.1, bf16[2816,256]{1,0:T(8,128)(2,1)} %collective-permute-done, bf16[2816,256]{1,0:T(8,128)(2,1)S(1)} %slice.74, bf16[128,1024]{1,0:T(8,128)(2,1)S(1)} %collective-permute-done.11, bf16[128,1024]{1,0:T(8,128)(2,1)S(1)} %collective-permute-done.10, ...), kind=kOutput, calls=%fused_computation.21 | convolution fusion | flops 2974285824 | bytes 12582912 | tf_op jit(solution)/shard_map/dot_general | solution.py:97
  127.7 11.1 %collective-permute-done.19 = bf16[128,2688]{1,0:T(8,128)(2,1)S(1)} collective-permute-done((bf16[128,2688]{1,0:T(8,128)(2,1)S(1)}, bf16[128,2688]{1,0:T(8,128)(2,1)S(1)}, u32[]{:S(2)}, u32[]{:S(2)}) %collective-permute-start.19) | collective-permute-done | bytes 688160 | tf_op jit(solution)/shard_map/ppermute | solution.py:29
  143.5 4.6 %collective-permute-start.20 = (bf16[128,2688]{1,0:T(8,128)(2,1)S(1)}, bf16[128,2688]{1,0:T(8,128)(2,1)S(1)}, u32[]{:S(2)}, u32[]{:S(2)}) collective-permute-start(bf16[128,2688]{1,0:T(8,128)(2,1)S(1)} %get-tuple-element.20), channel_id=1, source_target_pairs={{0,8},{2,10},{4,12},{6,14},{8,16},{10,18},{12,20},{14,22},{16,24},... | collective-permute-start | bytes 2064392 | tf_op jit(solution)/shard_map/ppermute | solution.py:29
  148.1 8.8 %collective-permute-done.22 = bf16[128,2688]{1,0:T(8,128)(2,1)S(1)} collective-permute-done((bf16[128,2688]{1,0:T(8,128)(2,1)S(1)}, bf16[128,2688]{1,0:T(8,128)(2,1)S(1)}, u32[]{:S(2)}, u32[]{:S(2)}) %collective-permute-start.22) | collective-permute-done | bytes 688160 | tf_op jit(solution)/shard_map/ppermute | solution.py:29
  157.0 1.9 collective-permute-start.23
  158.9 3.6 collective-permute-done.12
  163.5 1.9 collective-permute-start.13
  165.4 11.8 %collective-permute-done.20 = bf16[128,2688]{1,0:T(8,128)(2,1)S(1)} collective-permute-done((bf16[128,2688]{1,0:T(8,128)(2,1)S(1)}, bf16[128,2688]{1,0:T(8,128)(2,1)S(1)}, u32[]{:S(2)}, u32[]{:S(2)}) %collective-permute-start.20) | collective-permute-done | bytes 688160 | tf_op jit(solution)/shard_map/ppermute | solution.py:29
  177.2 3.6 fusion.24
  180.9 9.4 %collective-permute-done.13 = bf16[128,2816]{1,0:T(8,128)(2,1)} collective-permute-done((bf16[128,2816]{1,0:T(8,128)(2,1)}, bf16[128,2816]{1,0:T(8,128)(2,1)}, u32[]{:S(2)}, u32[]{:S(2)}) %collective-permute-start.13) | collective-permute-done | bytes 720928 | tf_op jit(solution)/shard_map/ppermute | solution.py:29
  190.3 2.3 add_convert_fusion.3
  194.2 4.6 %collective-permute-start.14 = (bf16[128,2816]{1,0:T(8,128)(2,1)S(1)}, bf16[128,2816]{1,0:T(8,128)(2,1)S(1)}, u32[]{:S(2)}, u32[]{:S(2)}) collective-permute-start(bf16[128,2816]{1,0:T(8,128)(2,1)S(1)} %get-tuple-element.16), channel_id=1, source_target_pairs={{0,8},{2,10},{4,12},{6,14},{8,16},{10,18},{12,20},{14,22},{16,24},... | collective-permute-start | bytes 2162696 | tf_op jit(solution)/shard_map/ppermute | solution.py:29
  198.7 38.9 %collective-permute-done.16 = bf16[128,2816]{1,0:T(8,128)(2,1)S(1)} collective-permute-done((bf16[128,2816]{1,0:T(8,128)(2,1)S(1)}, bf16[128,2816]{1,0:T(8,128)(2,1)S(1)}, u32[]{:S(2)}, u32[]{:S(2)}) %collective-permute-start.16) | collective-permute-done | bytes 720928 | tf_op jit(solution)/shard_map/ppermute | solution.py:29
  237.8 1.9 collective-permute-start.17
  239.7 4.3 collective-permute-done.14
  244.0 26.1 %collective-permute-done.17 = bf16[128,2816]{1,0:T(8,128)(2,1)S(1)} collective-permute-done((bf16[128,2816]{1,0:T(8,128)(2,1)S(1)}, bf16[128,2816]{1,0:T(8,128)(2,1)S(1)}, u32[]{:S(2)}, u32[]{:S(2)}) %collective-permute-start.17) | collective-permute-done | bytes 720928 | tf_op jit(solution)/shard_map/ppermute | solution.py:29
  270.1 2.1 fusion.13
  281.4 5.1 %fusion.29 = f32[2688,1024]{1,0:T(8,128)S(1)} fusion(bf16[512,2688]{1,0:T(8,128)(2,1)} %all-gather.5.cloned.1.call-done, bf16[896,1024]{1,0:T(8,128)(2,1)} %constant_dynamic-update-slice_fusion.5, s32[]{:T(128)S(6)} %select_n.148), kind=kOutput, calls=%fused_computation.78 | convolution fusion | flops 2818572288 | bytes 14811140 | tf_op jit(solution)/shard_map/dot_general | solution.py:112
  286.6 4.1 copy-done.6
  290.6 1.9 slice.155
  293.8 6.3 %fusion.3 = f32[512,1024]{1,0:T(8,128)} fusion(bf16[512,2688]{1,0:T(8,128)(2,1)S(1)} %copy-done.25, bf16[2688,512]{1,0:T(8,128)(2,1)} %collective-permute-done.3, bf16[2688,256]{1,0:T(8,128)(2,1)S(1)} %copy-done.17, bf16[2688,256]{1,0:T(8,128)(2,1)S(1)} %slice.77), kind=kOutput, calls=%fused_computation.24 | convolution fusion | flops 2835087360 | bytes 10354688 | tf_op jit(solution)/shard_map/dot_general | solution.py:109
  300.2 28.1 %all-gather.3.cloned.1.call-done = bf16[512,2816]{1,0:T(8,128)(2,1)} async-done(((bf16[128,2816]{1,0:T(8,128)(2,1)}), bf16[512,2816]{1,0:T(8,128)(2,1)}) %all-gather.3.cloned.1.call-update) | async-done | bytes 2883600 | tf_op jit(solution)/shard_map/all_gather | solution.py:37
  328.3 7.0 %add_convert_fusion = bf16[512,1024]{1,0:T(8,128)(2,1)S(1)} fusion(f32[512,1024]{1,0:T(8,128)} %fusion.3, bf16[512,2816]{1,0:T(8,128)(2,1)} %all-gather.3.cloned.1.call-done, bf16[2816,512]{1,0:T(8,128)(2,1)} %copy-done.23, bf16[2816,256]{1,0:T(8,128)(2,1)} %collective-permute-done, bf16[2816,256]{1,0:T(8,128)(2,1)S(1)} %slice.74), kind=kOutput, calls=%fused_computation.25 | convolution fusion | flops 2971140096 | bytes 11796480 | tf_op jit(solution)/shard_map/dot_general | solution.py:109
  336.1 1.9 collective-permute-start.5
  338.1 1.8 collective-permute-start.4
  339.9 4.5 fusion.31
  344.3 4.2 copy-done.5
  348.5 2.0 slice.154
  350.9 10.8 %collective-permute-done.4 = bf16[128,1024]{1,0:T(8,128)(2,1)S(1)} collective-permute-done((bf16[128,1024]{1,0:T(8,128)(2,1)S(1)}, bf16[128,1024]{1,0:T(8,128)(2,1)S(1)}, u32[]{:S(2)}, u32[]{:S(2)}) %collective-permute-start.4) | collective-permute-done | bytes 262176 | tf_op jit(solution)/shard_map/ppermute | solution.py:25
  370.0 5.0 %slice_add_fusion.1 = f32[2688,512]{1,0:T(8,128)S(1)} fusion(f32[2688,1024]{1,0:T(8,128)} %copy-done.6, bf16[2688,512]{1,0:T(8,128)(2,1)} %collective-permute-done.26), kind=kLoop, calls=%fused_computation.5 | loop fusion | flops 2752512 | bytes 13762560 | tf_op jit(solution)/shard_map/add | solution.py:116
  378.0 3.0 slice_add_fusion
  386.9 22.9 %collective-permute-done.27 = bf16[2688,256]{1,0:T(8,128)(2,1)} collective-permute-done((bf16[2688,256]{1,0:T(8,128)(2,1)}, bf16[2688,256]{1,0:T(8,128)(2,1)}, u32[]{:S(2)}, u32[]{:S(2)}) %collective-permute-start.27) | collective-permute-done | bytes 1376288 | tf_op jit(solution)/shard_map/ppermute | solution.py:21
  409.9 2.4 slice_add_fusion.3
  412.3 27.1 %collective-permute-done.25 = bf16[2816,256]{1,0:T(8,128)(2,1)} collective-permute-done((bf16[2816,256]{1,0:T(8,128)(2,1)}, bf16[2816,256]{1,0:T(8,128)(2,1)}, u32[]{:S(2)}, u32[]{:S(2)}) %collective-permute-start.25) | collective-permute-done | bytes 1441824 | tf_op jit(solution)/shard_map/ppermute | solution.py:21
  439.5 1.9 slice_add_fusion.2
  441.3 2.9 pad_maximum_fusion.1
  (133 shorter events, 54.2 us)
Async XLA Ops:
  7.2 274.2 %all-gather.5.cloned.1.call-start = ((), (), s32[]{:S(2)}) async-start(), calls=%async_computation.1 | async-start | bytes 3440640 | tf_op jit(solution)/shard_map/all_gather | solution.py:37
  8.6 34.0 %copy-start.8 = (bf16[5504,256]{1,0:T(8,128)(2,1)S(1)}, bf16[5504,256]{1,0:T(8,128)(2,1)}, u32[]{:S(2)}) copy-start(bf16[5504,256]{1,0:T(8,128)(2,1)} %param.7) | copy-start | bytes 8454148
  8.7 32.0 %collective-permute-start.2 = (bf16[2688,256]{1,0:T(8,128)(2,1)S(1)}, bf16[2688,256]{1,0:T(8,128)(2,1)S(1)}, u32[]{:S(2)}, u32[]{:S(2)}) collective-permute-start(bf16[2688,256]{1,0:T(8,128)(2,1)S(1)} %slice.77), channel_id=1, source_target_pairs={{0,4},{2,6},{4,0},{6,2},{8,12},{10,14},{12,8},{14,10},{16,20},{18,... | collective-permute-start | bytes 4128776 | tf_op jit(solution)/shard_map/ppermute | solution.py:21
  42.6 52.1 %collective-permute-start.3 = (bf16[2688,512]{1,0:T(8,128)(2,1)}, bf16[2688,512]{1,0:T(8,128)(2,1)}, u32[]{:S(2)}, u32[]{:S(2)}) collective-permute-start(bf16[2688,512]{1,0:T(8,128)(2,1)} %pad_maximum_fusion.4), channel_id=1, source_target_pairs={{0,2},{2,0},{4,6},{6,4},{8,10},{10,8},{12,14},{14,12},{16,18},{18,... | collective-permute-start | bytes 8257544 | tf_op jit(solution)/shard_map/ppermute | solution.py:21
  42.7 34.2 %collective-permute-start = (bf16[2816,256]{1,0:T(8,128)(2,1)S(1)}, bf16[2816,256]{1,0:T(8,128)(2,1)}, u32[]{:S(2)}, u32[]{:S(2)}) collective-permute-start(bf16[2816,256]{1,0:T(8,128)(2,1)S(1)} %slice.74), channel_id=1, source_target_pairs={{0,4},{2,6},{4,0},{6,2},{8,12},{10,14},{12,8},{14,10},{16,20},{18,... | collective-permute-start | bytes 4325384 | tf_op jit(solution)/shard_map/ppermute | solution.py:21
  45.6 14.2 %collective-permute-start.8 = (bf16[128,2048]{0,1:T(8,128)(2,1)S(1)}, bf16[128,2048]{0,1:T(8,128)(2,1)}, u32[]{:S(2)}, u32[]{:S(2)}) collective-permute-start(bf16[128,2048]{0,1:T(8,128)(2,1)S(1)} %copy.11), channel_id=1, source_target_pairs={{0,1},{1,0},{2,3},{3,2},{4,5},{5,4},{6,7},{7,6},{8,9},{9,8},{10,11... | collective-permute-start | bytes 1572872 | tf_op jit(solution)/shard_map/ppermute | solution.py:32
  66.3 55.7 %copy-start.11 = (bf16[128,1,1024]{2,0,1:T(8,128)(2,1)}, bf16[128,1,1024]{2,0,1:T(8,128)(2,1)S(1)}, u32[]{:S(2)}) copy-start(bf16[128,1,1024]{2,0,1:T(8,128)(2,1)S(1)} %copy.18) | copy-start | bytes 786436
  70.9 19.9 %collective-permute-start.11 = (bf16[128,1024]{1,0:T(8,128)(2,1)}, bf16[128,1024]{1,0:T(8,128)(2,1)S(1)}, u32[]{:S(2)}, u32[]{:S(2)}) collective-permute-start(bf16[128,1024]{1,0:T(8,128)(2,1)} %bitcast.30), channel_id=1, source_target_pairs={{0,8},{2,10},{4,12},{6,14},{8,16},{10,18},{12,20},{14,22},{16,24},... | collective-permute-start | bytes 786440 | tf_op jit(solution)/shard_map/ppermute | solution.py:25
  72.4 18.3 %collective-permute-start.9 = (bf16[128,1024]{1,0:T(8,128)(2,1)}, bf16[128,1024]{1,0:T(8,128)(2,1)S(1)}, u32[]{:S(2)}, u32[]{:S(2)}) collective-permute-start(bf16[128,1024]{1,0:T(8,128)(2,1)} %bitcast.29), channel_id=1, source_target_pairs={{0,24},{2,26},{4,28},{6,30},{8,0},{10,2},{12,4},{14,6},{16,8},{18,... | collective-permute-start | bytes 786440 | tf_op jit(solution)/shard_map/ppermute | solution.py:25
  72.9 21.9 %copy-start.16 = (bf16[2688,256]{1,0:T(8,128)(2,1)S(1)}, bf16[2688,256]{1,0:T(8,128)(2,1)}, u32[]{:S(2)}) copy-start(bf16[2688,256]{1,0:T(8,128)(2,1)} %copy-done.15) | copy-start | bytes 4128772
  72.9 21.9 %collective-permute-start.10 = (bf16[128,1024]{1,0:T(8,128)(2,1)}, bf16[128,1024]{1,0:T(8,128)(2,1)S(1)}, u32[]{:S(2)}, u32[]{:S(2)}) collective-permute-start(bf16[128,1024]{1,0:T(8,128)(2,1)} %bitcast.28), channel_id=1, source_target_pairs={{0,16},{2,18},{4,20},{6,22},{8,24},{10,26},{12,28},{14,30},{16,0},... | collective-permute-start | bytes 786440 | tf_op jit(solution)/shard_map/ppermute | solution.py:25
  78.5 43.5 %collective-permute-start.1 = (bf16[2816,512]{1,0:T(8,128)(2,1)S(1)}, bf16[2816,512]{1,0:T(8,128)(2,1)S(1)}, u32[]{:S(2)}, u32[]{:S(2)}) collective-permute-start(bf16[2816,512]{1,0:T(8,128)(2,1)S(1)} %pad_maximum_fusion.3), channel_id=1, source_target_pairs={{0,2},{2,0},{4,6},{6,4},{8,10},{10,8},{12,14},{14,12},{16,18},{18,... | collective-permute-start | bytes 8650760 | tf_op jit(solution)/shard_map/ppermute | solution.py:21
  90.8 31.3 %copy-start.22 = (bf16[128,1024]{1,0:T(8,128)(2,1)}, bf16[128,1024]{1,0:T(8,128)(2,1)S(1)}, u32[]{:S(2)}) copy-start(bf16[128,1024]{1,0:T(8,128)(2,1)S(1)} %collective-permute-done.11) | copy-start | bytes 786436
  90.8 31.3 %copy-start.18 = (bf16[128,1024]{1,0:T(8,128)(2,1)}, bf16[128,1024]{1,0:T(8,128)(2,1)S(1)}, u32[]{:S(2)}) copy-start(bf16[128,1024]{1,0:T(8,128)(2,1)S(1)} %collective-permute-done.9) | copy-start | bytes 786436
  94.7 27.3 %copy-start.20 = (bf16[128,1024]{1,0:T(8,128)(2,1)}, bf16[128,1024]{1,0:T(8,128)(2,1)S(1)}, u32[]{:S(2)}) copy-start(bf16[128,1024]{1,0:T(8,128)(2,1)S(1)} %collective-permute-done.10) | copy-start | bytes 786436
  100.0 20.0 %collective-permute-start.18 = (bf16[128,2688]{1,0:T(8,128)(2,1)S(1)}, bf16[128,2688]{1,0:T(8,128)(2,1)S(1)}, u32[]{:S(2)}, u32[]{:S(2)}) collective-permute-start(bf16[128,2688]{1,0:T(8,128)(2,1)S(1)} %get-tuple-element.22), channel_id=1, source_target_pairs={{0,8},{2,10},{4,12},{6,14},{1,9},{3,11},{5,13},{7,15}} | collective-permute-start | bytes 2064392 | tf_op jit(solution)/shard_map/ppermute | solution.py:29
  101.3 26.4 %collective-permute-start.21 = (bf16[128,2688]{1,0:T(8,128)(2,1)S(1)}, bf16[128,2688]{1,0:T(8,128)(2,1)S(1)}, u32[]{:S(2)}, u32[]{:S(2)}) collective-permute-start(bf16[128,2688]{1,0:T(8,128)(2,1)S(1)} %get-tuple-element.23), channel_id=1, source_target_pairs={{24,16},{26,18},{28,20},{30,22},{25,17},{27,19},{29,21},{31,23}} | collective-permute-start | bytes 2064392 | tf_op jit(solution)/shard_map/ppermute | solution.py:29
  120.1 18.7 %collective-permute-start.19 = (bf16[128,2688]{1,0:T(8,128)(2,1)S(1)}, bf16[128,2688]{1,0:T(8,128)(2,1)S(1)}, u32[]{:S(2)}, u32[]{:S(2)}) collective-permute-start(bf16[128,2688]{1,0:T(8,128)(2,1)S(1)} %add_convert_fusion.8), channel_id=1, source_target_pairs={{0,8},{2,10},{4,12},{6,14},{8,16},{10,18},{12,20},{14,22},{1,9},{3... | collective-permute-start | bytes 2064392 | tf_op jit(solution)/shard_map/ppermute | solution.py:29
  127.7 34.8 %copy-start.3 = (f32[512,2816]{1,0:T(8,128)}, f32[512,2816]{1,0:T(8,128)S(1)}, u32[]{:S(2)}) copy-start(f32[512,2816]{1,0:T(8,128)S(1)} %fusion) | copy-start | bytes 17301508
  139.0 17.8 %collective-permute-start.22 = (bf16[128,2688]{1,0:T(8,128)(2,1)S(1)}, bf16[128,2688]{1,0:T(8,128)(2,1)S(1)}, u32[]{:S(2)}, u32[]{:S(2)}) collective-permute-start(bf16[128,2688]{1,0:T(8,128)(2,1)S(1)} %get-tuple-element.21), channel_id=1, source_target_pairs={{16,8},{18,10},{20,12},{22,14},{24,16},{26,18},{28,20},{30,22},{17... | collective-permute-start | bytes 2064392 | tf_op jit(solution)/shard_map/ppermute | solution.py:29
  141.5 21.0 %collective-permute-start.12 = (bf16[128,2816]{1,0:T(8,128)(2,1)S(1)}, bf16[128,2816]{1,0:T(8,128)(2,1)S(1)}, u32[]{:S(2)}, u32[]{:S(2)}) collective-permute-start(bf16[128,2816]{1,0:T(8,128)(2,1)S(1)} %get-tuple-element.18), channel_id=1, source_target_pairs={{0,8},{2,10},{4,12},{6,14},{1,9},{3,11},{5,13},{7,15}} | collective-permute-start | bytes 2162696 | tf_op jit(solution)/shard_map/ppermute | solution.py:29
  142.8 38.1 %collective-permute-start.15 = (bf16[128,2816]{1,0:T(8,128)(2,1)}, bf16[128,2816]{1,0:T(8,128)(2,1)S(1)}, u32[]{:S(2)}, u32[]{:S(2)}) collective-permute-start(bf16[128,2816]{1,0:T(8,128)(2,1)} %get-tuple-element.19), channel_id=1, source_target_pairs={{24,16},{26,18},{28,20},{30,22},{25,17},{27,19},{29,21},{31,23}} | collective-permute-start | bytes 2162696 | tf_op jit(solution)/shard_map/ppermute | solution.py:29
  143.5 33.7 %collective-permute-start.20 = (bf16[128,2688]{1,0:T(8,128)(2,1)S(1)}, bf16[128,2688]{1,0:T(8,128)(2,1)S(1)}, u32[]{:S(2)}, u32[]{:S(2)}) collective-permute-start(bf16[128,2688]{1,0:T(8,128)(2,1)S(1)} %get-tuple-element.20), channel_id=1, source_target_pairs={{0,8},{2,10},{4,12},{6,14},{8,16},{10,18},{12,20},{14,22},{16,24},... | collective-permute-start | bytes 2064392 | tf_op jit(solution)/shard_map/ppermute | solution.py:29
  157.0 20.3 %collective-permute-start.23 = (bf16[128,2688]{1,0:T(8,128)(2,1)S(1)}, bf16[128,2688]{1,0:T(8,128)(2,1)S(1)}, u32[]{:S(2)}, u32[]{:S(2)}) collective-permute-start(bf16[128,2688]{1,0:T(8,128)(2,1)S(1)} %add_convert_fusion.5), channel_id=1, source_target_pairs={{8,0},{10,2},{12,4},{14,6},{16,8},{18,10},{20,12},{22,14},{24,16},... | collective-permute-start | bytes 2064392 | tf_op jit(solution)/shard_map/ppermute | solution.py:29
  163.5 26.8 %collective-permute-start.13 = (bf16[128,2816]{1,0:T(8,128)(2,1)}, bf16[128,2816]{1,0:T(8,128)(2,1)}, u32[]{:S(2)}, u32[]{:S(2)}) collective-permute-start(bf16[128,2816]{1,0:T(8,128)(2,1)} %add_convert_fusion.4), channel_id=1, source_target_pairs={{0,8},{2,10},{4,12},{6,14},{8,16},{10,18},{12,20},{14,22},{1,9},{3... | collective-permute-start | bytes 2162696 | tf_op jit(solution)/shard_map/ppermute | solution.py:29
  180.8 147.5 %all-gather.3.cloned.1.call-start = ((), (), s32[]{:S(2)}) async-start(), calls=%async_computation | async-start | bytes 3604480 | tf_op jit(solution)/shard_map/all_gather | solution.py:37
  180.9 56.8 %copy-start.4 = (f32[512,2816]{1,0:T(8,128)S(1)}, f32[512,2816]{1,0:T(8,128)}, u32[]{:S(2)}) copy-start(f32[512,2816]{1,0:T(8,128)} %copy-done.3) | copy-start | bytes 17301508
  192.6 77.6 %copy-start.13 = (bf16[128,5504]{1,0:T(8,128)(2,1)S(1)}, bf16[128,5504]{1,0:T(8,128)(2,1)}, u32[]{:S(2)}) copy-start(bf16[128,5504]{1,0:T(8,128)(2,1)} %param.4) | copy-start | bytes 4227076
  192.6 77.6 %copy-start.14 = (bf16[128,5504]{1,0:T(8,128)(2,1)S(1)}, bf16[128,5504]{1,0:T(8,128)(2,1)}, u32[]{:S(2)}) copy-start(bf16[128,5504]{1,0:T(8,128)(2,1)} %param.5) | copy-start | bytes 4227076
  192.6 45.0 %collective-permute-start.16 = (bf16[128,2816]{1,0:T(8,128)(2,1)S(1)}, bf16[128,2816]{1,0:T(8,128)(2,1)S(1)}, u32[]{:S(2)}, u32[]{:S(2)}) collective-permute-start(bf16[128,2816]{1,0:T(8,128)(2,1)S(1)} %get-tuple-element.17), channel_id=1, source_target_pairs={{16,8},{18,10},{20,12},{22,14},{24,16},{26,18},{28,20},{30,22},{17... | collective-permute-start | bytes 2162696 | tf_op jit(solution)/shard_map/ppermute | solution.py:29
  194.2 49.9 %collective-permute-start.14 = (bf16[128,2816]{1,0:T(8,128)(2,1)S(1)}, bf16[128,2816]{1,0:T(8,128)(2,1)S(1)}, u32[]{:S(2)}, u32[]{:S(2)}) collective-permute-start(bf16[128,2816]{1,0:T(8,128)(2,1)S(1)} %get-tuple-element.16), channel_id=1, source_target_pairs={{0,8},{2,10},{4,12},{6,14},{8,16},{10,18},{12,20},{14,22},{16,24},... | collective-permute-start | bytes 2162696 | tf_op jit(solution)/shard_map/ppermute | solution.py:29
  237.8 32.4 %collective-permute-start.17 = (bf16[128,2816]{1,0:T(8,128)(2,1)S(1)}, bf16[128,2816]{1,0:T(8,128)(2,1)S(1)}, u32[]{:S(2)}, u32[]{:S(2)}) collective-permute-start(bf16[128,2816]{1,0:T(8,128)(2,1)S(1)} %add_convert_fusion.1), channel_id=1, source_target_pairs={{8,0},{10,2},{12,4},{14,6},{16,8},{18,10},{20,12},{22,14},{24,16},... | collective-permute-start | bytes 2162696 | tf_op jit(solution)/shard_map/ppermute | solution.py:29
  272.4 6.8 %copy-start.12 = (bf16[128,1,1024]{2,0,1:T(8,128)(2,1)S(1)}, bf16[128,1,1024]{2,0,1:T(8,128)(2,1)}, u32[]{:S(2)}) copy-start(bf16[128,1,1024]{2,0,1:T(8,128)(2,1)} %copy-done.11) | copy-start | bytes 786436
  272.4 7.5 %copy-start.19 = (bf16[128,1024]{1,0:T(8,128)(2,1)S(1)}, bf16[128,1024]{1,0:T(8,128)(2,1)}, u32[]{:S(2)}) copy-start(bf16[128,1024]{1,0:T(8,128)(2,1)} %copy-done.18) | copy-start | bytes 786436
  272.4 8.3 %copy-start.21 = (bf16[128,1024]{1,0:T(8,128)(2,1)S(1)}, bf16[128,1024]{1,0:T(8,128)(2,1)}, u32[]{:S(2)}) copy-start(bf16[128,1024]{1,0:T(8,128)(2,1)} %copy-done.20) | copy-start | bytes 786436
  292.6 77.4 %collective-permute-start.26 = (bf16[2688,512]{1,0:T(8,128)(2,1)}, bf16[2688,512]{1,0:T(8,128)(2,1)}, u32[]{:S(2)}, u32[]{:S(2)}) collective-permute-start(bf16[2688,512]{1,0:T(8,128)(2,1)} %slice.155), channel_id=1, source_target_pairs={{0,2},{2,0},{4,6},{6,4},{8,10},{10,8},{12,14},{14,12},{16,18},{18,... | collective-permute-start | bytes 8257544 | tf_op jit(solution)/shard_map/ppermute | solution.py:21
  328.3 11.6 %copy-start.24 = (bf16[512,2816]{1,0:T(8,128)(2,1)S(1)}, bf16[512,2816]{1,0:T(8,128)(2,1)}, u32[]{:S(2)}) copy-start(bf16[512,2816]{1,0:T(8,128)(2,1)} %all-gather.3.cloned.1.call-done) | copy-start | bytes 8650756
  336.1 26.4 %collective-permute-start.5 = (bf16[128,1024]{1,0:T(8,128)(2,1)S(1)}, bf16[128,1024]{1,0:T(8,128)(2,1)S(1)}, u32[]{:S(2)}, u32[]{:S(2)}) collective-permute-start(bf16[128,1024]{1,0:T(8,128)(2,1)S(1)} %get-tuple-element.40), channel_id=1, source_target_pairs={{0,16},{2,18},{4,20},{6,22},{8,24},{10,26},{12,28},{14,30},{16,0},... | collective-permute-start | bytes 786440 | tf_op jit(solution)/shard_map/ppermute | solution.py:25
  338.1 23.7 %collective-permute-start.4 = (bf16[128,1024]{1,0:T(8,128)(2,1)S(1)}, bf16[128,1024]{1,0:T(8,128)(2,1)S(1)}, u32[]{:S(2)}, u32[]{:S(2)}) collective-permute-start(bf16[128,1024]{1,0:T(8,128)(2,1)S(1)} %get-tuple-element.41), channel_id=1, source_target_pairs={{0,24},{2,26},{4,28},{6,30},{8,0},{10,2},{12,4},{14,6},{16,8},{18,... | collective-permute-start | bytes 786440 | tf_op jit(solution)/shard_map/ppermute | solution.py:25
  350.6 27.4 %collective-permute-start.24 = (bf16[2816,512]{1,0:T(8,128)(2,1)}, bf16[2816,512]{1,0:T(8,128)(2,1)}, u32[]{:S(2)}, u32[]{:S(2)}) collective-permute-start(bf16[2816,512]{1,0:T(8,128)(2,1)} %slice.154), channel_id=1, source_target_pairs={{0,2},{2,0},{4,6},{6,4},{8,10},{10,8},{12,14},{14,12},{16,18},{18,... | collective-permute-start | bytes 8650760 | tf_op jit(solution)/shard_map/ppermute | solution.py:21
  350.6 12.7 %collective-permute-start.6 = (bf16[128,1024]{1,0:T(8,128)(2,1)S(1)}, bf16[128,1024]{1,0:T(8,128)(2,1)S(1)}, u32[]{:S(2)}, u32[]{:S(2)}) collective-permute-start(bf16[128,1024]{1,0:T(8,128)(2,1)S(1)} %get-tuple-element.38), channel_id=1, source_target_pairs={{0,8},{2,10},{4,12},{6,14},{8,16},{10,18},{12,20},{14,22},{16,24},... | collective-permute-start | bytes 786440 | tf_op jit(solution)/shard_map/ppermute | solution.py:25
  368.1 9.9 %slice-start = ((s8[11534336]{0:T(1024)(128)(4,1)}), s8[4194304]{0:T(1024)(128)(4,1)S(1)}, s32[]{:S(2)}) async-start(s8[11534336]{0:T(1024)(128)(4,1)} %bitcast.19), calls=%async_computation.2 | async-start | bytes 8388608
  368.4 9.6 %slice-start.1 = ((s8[11534336]{0:T(1024)(128)(4,1)}), s8[4194304]{0:T(1024)(128)(4,1)S(1)}, s32[]{:S(2)}) async-start(s8[11534336]{0:T(1024)(128)(4,1)} %bitcast.19), calls=%async_computation.3 | async-start | bytes 8388608
  368.4 9.6 %slice-start.2 = ((s8[11534336]{0:T(1024)(128)(4,1)}), s8[3145728]{0:T(1024)(128)(4,1)S(1)}, s32[]{:S(2)}) async-start(s8[11534336]{0:T(1024)(128)(4,1)} %bitcast.19), calls=%async_computation.4 | async-start | bytes 6291456
  368.4 17.4 %collective-permute-start.7 = (bf16[128,2048]{0,1:T(8,128)(2,1)S(1)}, bf16[128,2048]{0,1:T(8,128)(2,1)S(1)}, u32[]{:S(2)}, u32[]{:S(2)}) collective-permute-start(bf16[128,2048]{0,1:T(8,128)(2,1)S(1)} %dynamic-slice_bitcast_fusion), channel_id=1, source_target_pairs={{0,1},{1,0},{2,3},{3,2},{4,5},{5,4},{6,7},{7,6},{8,9},{9,8},{10,11... | collective-permute-start | bytes 1572872 | tf_op jit(solution)/shard_map/ppermute | solution.py:32
  376.5 33.4 %collective-permute-start.27 = (bf16[2688,256]{1,0:T(8,128)(2,1)}, bf16[2688,256]{1,0:T(8,128)(2,1)}, u32[]{:S(2)}, u32[]{:S(2)}) collective-permute-start(bf16[2688,256]{1,0:T(8,128)(2,1)} %slice.157), channel_id=1, source_target_pairs={{0,4},{2,6},{4,0},{6,2},{8,12},{10,14},{12,8},{14,10},{16,20},{18,... | collective-permute-start | bytes 4128776 | tf_op jit(solution)/shard_map/ppermute | solution.py:21
  382.4 57.1 %collective-permute-start.25 = (bf16[2816,256]{1,0:T(8,128)(2,1)}, bf16[2816,256]{1,0:T(8,128)(2,1)}, u32[]{:S(2)}, u32[]{:S(2)}) collective-permute-start(bf16[2816,256]{1,0:T(8,128)(2,1)} %slice.156), channel_id=1, source_target_pairs={{0,4},{2,6},{4,0},{6,2},{8,12},{10,14},{12,8},{14,10},{16,20},{18,... | collective-permute-start | bytes 4325384 | tf_op jit(solution)/shard_map/ppermute | solution.py:21
  386.9 52.5 %copy-start.1 = (f32[2816,512]{1,0:T(8,128)S(1)}, f32[2816,512]{1,0:T(8,128)}, u32[]{:S(2)}) copy-start(f32[2816,512]{1,0:T(8,128)} %copy-done) | copy-start | bytes 17301508
  (11 other events, 37.4 us)
Sparse Core Ops, SparseCore 0:
  180.9 88.6 all-gather.4
  272.4 55.8 all-gather.2

commit v3 on v1

v3 whole, which is shorter than its diff:
```python
import jax
import jax.numpy as jnp
from jax import lax
from jax.sharding import PartitionSpec as P

QUAD = 4
STREAMS = 2
PER_STREAM = 2
ORDER = (0, 2, 1, 3)


def after(value, *others):
    return lax.optimization_barrier((value,) + others)[0]


def slot_of(near):
    result = []
    for block in range(QUAD):
        k = near ^ block
        result.append(((k & 1) << 1) | (k >> 1))
    return result


def solution(mesh):
    n_hst, n_local = mesh.shape["hst"], mesh.shape["local"]
    n_far = n_hst // QUAD

    def swap(value, bit):
        return lax.ppermute(value, "hst", [(h, h ^ bit) for h in range(n_hst)])

    def shift(value, step):
        pairs = [(h, (h + step * QUAD) % n_hst) for h in range(n_hst)]
        return lax.ppermute(value, "hst", pairs)

    def hop(value, way, sources):
        pairs = [(s * QUAD + q, (s + way) * QUAD + q) for s in sources for q in range(QUAD)]
        return lax.ppermute(value, "hst", pairs)

    def local_shift(value, step):
        return lax.ppermute(value, "local", [(i, (i + step) % n_local) for i in range(n_local)])

    def on_device(gate_act, up_act, cotangent, down_weight):
        h = lax.axis_index("hst")
        x = lax.axis_index("local")
        far, near = h // QUAD, h % QUAD
        tokens, half = cotangent.shape
        width = down_weight.shape[1]
        hidden_units = gate_act.shape[1]
        n_chunks = STREAMS * PER_STREAM
        lanes = -(-hidden_units // 128)
        chunk = 128 * -(-lanes // n_chunks)
        bounds = [(f * chunk, min(hidden_units, (f + 1) * chunk)) for f in range(n_chunks)]

        def padded(value, axis):
            missing = [(0, 0), (0, 0)]
            missing[axis] = (0, chunk - value.shape[axis])
            return jnp.pad(value, missing) if missing[axis][1] else value

        parts = [cotangent]
        for step in range(1, n_local):
            parts.append(local_shift(cotangent, n_local - step))
        twice = jnp.concatenate(parts + parts[:-1], axis=1)
        cot_full = lax.dynamic_slice_in_dim(
            twice, ((n_local - x) % n_local) * half, n_local * half, axis=1
        )
        cot_view = cot_full.reshape(tokens, n_far, QUAD, width)
        cot_view = jnp.concatenate(
            [lax.dynamic_slice_in_dim(cot_view, near ^ k, 1, axis=2) for k in ORDER], axis=2
        )
        cot_view = cot_view.reshape(tokens, n_far, QUAD * width)

        def cot_for(step):
            return lax.dynamic_index_in_dim(cot_view, (far + step) % n_far, axis=1, keepdims=False)

        cot_rows = jnp.concatenate(
            [cot_for(0)] + [shift(cot_for(n_far - e), n_far - e) for e in range(1, n_far)], axis=0
        )

        weights, last = [], []
        for f, (lo, hi) in enumerate(bounds):
            weight = after(padded(down_weight[lo:hi], 0), *last)
            other = swap(weight, 2)
            last = [other]
            if f == 0:
                last.append(parts[1])
            if f == 1:
                last.append(cot_rows)
            pair = jnp.concatenate([weight, other], axis=1)
            weights.append(jnp.concatenate([pair, swap(pair, 1)], axis=1))

        wide, hidden, terms = {}, {}, {}
        for f, (lo, hi) in enumerate(bounds):
            gate_wide = padded(gate_act[:, lo:hi], 1).astype(jnp.float32)
            up_wide = padded(up_act[:, lo:hi], 1).astype(jnp.float32)
            sigmoid_gate = jax.nn.sigmoid(gate_wide)
            wide[f] = gate_wide, up_wide, sigmoid_gate
            hidden[f] = (gate_wide * sigmoid_gate * up_wide).astype(jnp.bfloat16)

        gate_parts, up_parts, grad_parts, out_sums = {}, {}, {}, {}
        ready = []

        def gathered(f, above, below):
            slots = [hidden[f]]
            for e in range(1, n_far):
                slots.append(jnp.where(far + e < n_far, above[e], below[n_far - e]))
            hidden_rows = jnp.concatenate(slots, axis=0)
            out_sums[f] = jnp.dot(hidden_rows, weights[f], preferred_element_type=jnp.float32)
            grad = lax.dot_general(
                hidden_rows, cot_rows, (((0,), (0,)), ((), ())), preferred_element_type=jnp.float32
            )
            theirs = swap(grad[:, 2 * width :].astype(jnp.bfloat16), 1)
            grad = grad[:, : 2 * width] + theirs.astype(jnp.float32)
            theirs = swap(after(grad[:, width:].astype(jnp.bfloat16), *last), 2)
            last[:] = [theirs]
            ready.append(theirs)
            lo, hi = bounds[f]
            grad_parts[f] = (grad[:, :width] + theirs.astype(jnp.float32))[: hi - lo]

        def reduced(f, hidden_grad):
            gate_wide, up_wide, sigmoid_gate = wide[f]
            keep = bounds[f][1] - bounds[f][0]
            up_parts[f] = (hidden_grad * gate_wide * sigmoid_gate).astype(jnp.bfloat16)[:, :keep]
            gate_parts[f] = (
                hidden_grad * up_wide * sigmoid_gate * (1.0 + gate_wide * (1.0 - sigmoid_gate))
            ).astype(jnp.bfloat16)[:, :keep]

        def stream(chunks):
            recv = None
            for step in range(len(chunks) + 1):
                gather = chunks[step] if step < len(chunks) else None
                reduce = chunks[step - 1] if step else None
                if reduce is not None:
                    dots = lax.dot_general(
                        cot_rows,
                        weights[reduce],
                        (((1,), (1,)), ((), ())),
                        preferred_element_type=jnp.float32,
                    )
                    slots = [dots[e * tokens : (e + 1) * tokens] for e in range(n_far)]
                above, below = {}, {}
                first = 1 if gather is not None else 2
                end = n_far if reduce is not None else n_far - 1
                for j in range(first, end + 1):
                    lowest = 0 if reduce is not None and j > 1 else j - 1
                    highest = n_far - 2 if gather is not None and j < n_far else j - 2
                    sending = []
                    for which, place in ((0, far), (1, n_far - 1 - far)):
                        if j == 1:
                            if recv is None:
                                sending.append(hidden[gather])
                            else:
                                sending.append(after(hidden[gather], recv[which]))
                            continue
                        summed = None
                        if reduce is not None:
                            d = n_far - j + 1
                            summed = slots[d if which == 0 else n_far - d]
                            if j > 2:
                                summed = summed + recv[which].astype(jnp.float32)
                            summed = summed.astype(jnp.bfloat16)
                        if gather is None or j == n_far:
                            sending.append(summed)
                        elif reduce is None:
                            sending.append(recv[which])
                        else:
                            sending.append(jnp.where(place >= j - 1, recv[which], summed))
                    recv = yield sending, range(lowest, highest + 1)
                    if gather is not None and j < n_far:
                        below[j], above[j] = recv
                    if gather is not None and j == n_far - 1:
                        gathered(gather, above, below)
                if reduce is not None:
                    total = slots[0] + recv[0].astype(jnp.float32) + recv[1].astype(jnp.float32)
                    reduced(reduce, total)

        streams = [stream(range(s, n_chunks, STREAMS)) for s in range(STREAMS)]
        total_slots = STREAMS * (PER_STREAM + 1) * n_far - 2 * STREAMS
        recvs, history = [None] * STREAMS, []
        alive = list(range(STREAMS))
        awaited = 0
        while alive:
            for s in list(alive):
                try:
                    (up, down), sources = streams[s].send(recvs[s])
                except StopIteration:
                    alive.remove(s)
                    continue
                slot = len(history)
                others = history[-STREAMS - 1] if slot > STREAMS else ()
                if awaited < len(ready) and 10 * slot >= total_slots * (6 + awaited):
                    others += (ready[awaited],)
                    awaited += 1
                if others:
                    up, down = lax.optimization_barrier((up, down) + others)[:2]
                downs = [n_far - 1 - z for z in sources]
                recvs[s] = hop(up, 1, sources), hop(down, -1, downs)
                history.append(recvs[s])

        out_terms = sum(out_sums[f] for f in range(n_chunks)).astype(jnp.bfloat16)
        slots = [out_terms[:tokens]]
        for e in range(1, n_far):
            slots.append(shift(out_terms[e * tokens : (e + 1) * tokens], e))
        back = [slots[0]] + slots[:0:-1]
        twice = jnp.concatenate(back + back[:-1], axis=1)
        columns = QUAD * width
        mine = lax.dynamic_slice_in_dim(
            twice, ((n_far - far) % n_far) * columns, n_far * columns, axis=1
        )
        mine = mine.reshape(tokens, n_far, QUAD, width)
        mine = jnp.concatenate(
            [lax.dynamic_slice_in_dim(mine, slot, 1, axis=2) for slot in slot_of(near)], axis=2
        )
        mine = mine.reshape(tokens, n_local, half)

        def half_of(step):
            return lax.dynamic_index_in_dim(mine, (x + step) % n_local, axis=1, keepdims=False)

        output = half_of(0).astype(jnp.float32)
        for step in range(1, n_local):
            output = output + local_shift(half_of(step), step).astype(jnp.float32)
        chunks = range(n_chunks)
        return (
            output.astype(jnp.bfloat16),
            jnp.concatenate([gate_parts[f] for f in chunks], axis=1),
            jnp.concatenate([up_parts[f] for f in chunks], axis=1),
            jnp.concatenate([grad_parts[f] for f in chunks], axis=0),
        )

    specs = (P("hst", "local"), P("hst", "local"), P("hst", "local"), P("local", "hst"))
    return jax.shard_map(
        on_device, mesh=mesh, in_specs=specs, out_specs=specs, check_vma=False
    )
```

time: 427 us -> 341 us (0.80); the launches traced: 425 us -> 335 us
  waiting for transfers between devices: 267 us -> 76.5 us
  starting transfers between devices: 62.5 us -> 144 us
  local copies, waits for them, and re-layouts: 27.5 us -> 35.3 us
  other arithmetic: 36.8 us -> 43.2 us
    ppermute x24 -> x40, waiting for transfers between devices: 129 us -> 33 us  [hop(): return lax.ppermute(value, 'hst', pairs)]
    ppermute x24 -> x40, starting transfers between devices: 47.1 us -> 120 us  [hop(): return lax.ppermute(value, 'hst', pairs)]
    ppermute x8 -> x16, waiting for transfers between devices: 104 us -> 32.9 us  [swap(): return lax.ppermute(value, 'hst', [(h, h ^ bit) for h in range(n_hst)])]
    ppermute x6, waiting for transfers between devices: 33 us -> 10.6 us  [shift(): return lax.ppermute(value, 'hst', pairs)]
    convert_element_type x8 -> x12, other arithmetic: 5.29 us -> 16.4 us  [the longest x6 6.55 us: stream(): summed = summed.astype(jnp.bfloat16)]
    ppermute x8 -> x16, starting transfers between devices: 5.08 us -> 11.2 us  [swap(): return lax.ppermute(value, 'hst', [(h, h ^ bit) for h in range(n_hst)])]
    concatenate x4 -> x6, other arithmetic: 9.72 us -> 5.99 us  [the longest x1 2.7 us: on_device(): jnp.concatenate([grad_parts[f] for f in chunks], axis=0)]
    dot_general x6 -> x12, matrix products: 30.5 us -> 33.3 us  [the longest x4 14.3 us: gathered(): jnp.dot(hidden_rows, weights[f], preferred_element_type=jnp.float32)]
  transfers between devices with their start and end apart: 40 -> 64, of which waited for: 22 -> 17; matrix products, arithmetic and copies ran while one was open for 19% -> 30% of each run, Pallas kernels for 0% -> 0%
where the time goes in v3:
time: 341 us; the launch traced here: 335 us
  starting transfers between devices  144 us (42%)
  waiting for transfers between devices  76.5 us (22%)
  other arithmetic  43.2 us (13%)
  local copies, waits for them, and re-layouts  35.3 us (10%)
  matrix products  33.3 us (10%)
    ppermute x40, starting transfers between devices, hop(): return lax.ppermute(value, 'hst', pairs)  120 us
    ppermute x40, waiting for transfers between devices, hop(): return lax.ppermute(value, 'hst', pairs)  33 us
    ppermute x16, waiting for transfers between devices, swap(): return lax.ppermute(value, 'hst', [(h, h ^ bit) for h in range(n_hst)])  32.9 us
    unnamed x109, local copies, waits for them, and re-layouts  14.7 us
    dot_general x4, matrix products, gathered(): jnp.dot(hidden_rows, weights[f], preferred_element_type=jnp.float32)  14.3 us
    ppermute x16, starting transfers between devices, swap(): return lax.ppermute(value, 'hst', [(h, h ^ bit) for h in range(n_hst)])  11.2 us
    ppermute x6, starting transfers between devices, shift(): return lax.ppermute(value, 'hst', pairs)  10.8 us
    ppermute x6, waiting for transfers between devices, shift(): return lax.ppermute(value, 'hst', pairs)  10.6 us
  transfers between devices with their start and end apart: 64, of which 17 were waited for; matrix products, arithmetic and copies ran while one was open for 30% of the time, Pallas kernels for 0%

profile of v3, /device:TPU:8, one launch (start us, length us, event | category | flops | bytes accessed | tf_op | source)
XLA Modules:
  0.0 334.6 jit_solution(805883371079943321)
XLA Ops:
  0.6 3.1 fusion.9
  5.7 3.9 %collective-permute-start.4 = (bf16[128,1408]{1,0:T(8,128)(2,1)}, bf16[128,1408]{1,0:T(8,128)(2,1)}, u32[]{:S(2)}, u32[]{:S(2)}) collective-permute-start(bf16[128,1408]{1,0:T(8,128)(2,1)} %get-tuple-element.134), channel_id=1, source_target_pairs={{0,8},{2,10},{4,12},{6,14},{8,16},{10,18},{12,20},{14,22},{16,24},... | collective-permute-start | bytes 1081352 | tf_op jit(solution)/shard_map/ppermute | solution.py:37
  9.6 4.2 %collective-permute-start.1 = (bf16[128,1408]{1,0:T(8,128)(2,1)}, bf16[128,1408]{1,0:T(8,128)(2,1)}, u32[]{:S(2)}, u32[]{:S(2)}) collective-permute-start(bf16[128,1408]{1,0:T(8,128)(2,1)} %get-tuple-element.135), channel_id=1, source_target_pairs={{0,8},{2,10},{4,12},{6,14},{8,16},{10,18},{12,20},{14,22},{16,24},... | collective-permute-start | bytes 1081352 | tf_op jit(solution)/shard_map/ppermute | solution.py:37
  13.8 2.4 collective-permute-start
  30.1 4.3 %collective-permute-start.10 = (bf16[128,1408]{1,0:T(8,128)(2,1)}, bf16[128,1408]{1,0:T(8,128)(2,1)}, u32[]{:S(2)}, u32[]{:S(2)}) collective-permute-start(bf16[128,1408]{1,0:T(8,128)(2,1)} %collective-permute-done.4), channel_id=1, source_target_pairs={{8,16},{10,18},{12,20},{14,22},{16,24},{18,26},{20,28},{22,30},{9,... | collective-permute-start | bytes 1081352 | tf_op jit(solution)/shard_map/ppermute | solution.py:37
  36.3 5.5 %collective-permute-start.2 = (bf16[128,1408]{1,0:T(8,128)(2,1)}, bf16[128,1408]{1,0:T(8,128)(2,1)}, u32[]{:S(2)}, u32[]{:S(2)}) collective-permute-start(bf16[128,1408]{1,0:T(8,128)(2,1)} %collective-permute-done.1), channel_id=1, source_target_pairs={{8,16},{10,18},{12,20},{14,22},{16,24},{18,26},{20,28},{22,30},{9,... | collective-permute-start | bytes 1081352 | tf_op jit(solution)/shard_map/ppermute | solution.py:37
  52.2 2.7 collective-permute-start.21
  54.9 3.2 collective-permute-done.3
  58.8 3.1 collective-permute-start.7
  68.5 4.6 %collective-permute-done.7 = bf16[128,1408]{1,0:T(8,128)(2,1)S(1)} collective-permute-done((bf16[128,1408]{1,0:T(8,128)(2,1)}, bf16[128,1408]{1,0:T(8,128)(2,1)S(1)}, u32[]{:S(2)}, u32[]{:S(2)}) %collective-permute-start.7) | collective-permute-done | bytes 360480 | tf_op jit(solution)/shard_map/ppermute | solution.py:37
  73.1 4.1 %collective-permute-start.20 = (bf16[128,1024]{1,0:T(8,128)(2,1)S(1)}, bf16[128,1024]{1,0:T(8,128)(2,1)S(1)}, u32[]{:S(2)}, u32[]{:S(2)}) collective-permute-start(bf16[128,1024]{1,0:T(8,128)(2,1)S(1)} %bitcast.32), channel_id=1, source_target_pairs={{0,16},{2,18},{4,20},{6,22},{8,24},{10,26},{12,28},{14,30},{16,0},... | collective-permute-start | bytes 786440 | tf_op jit(solution)/shard_map/ppermute | solution.py:33
  80.0 2.4 collective-permute-start.17
  82.5 4.3 %collective-permute-start.18 = (bf16[128,1408]{1,0:T(8,128)(2,1)S(1)}, bf16[128,1408]{1,0:T(8,128)(2,1)S(1)}, u32[]{:S(2)}, u32[]{:S(2)}) collective-permute-start(bf16[128,1408]{1,0:T(8,128)(2,1)S(1)} %copy-done.17), channel_id=1, source_target_pairs={{0,8},{2,10},{4,12},{6,14},{8,16},{10,18},{12,20},{14,22},{16,24},... | collective-permute-start | bytes 1081352 | tf_op jit(solution)/shard_map/ppermute | solution.py:37
  86.8 3.9 %collective-permute-start.24 = (bf16[128,1408]{1,0:T(8,128)(2,1)S(1)}, bf16[128,1408]{1,0:T(8,128)(2,1)S(1)}, u32[]{:S(2)}, u32[]{:S(2)}) collective-permute-start(bf16[128,1408]{1,0:T(8,128)(2,1)S(1)} %copy-done.18), channel_id=1, source_target_pairs={{0,8},{2,10},{4,12},{6,14},{8,16},{10,18},{12,20},{14,22},{16,24},... | collective-permute-start | bytes 1081352 | tf_op jit(solution)/shard_map/ppermute | solution.py:37
  90.7 2.7 fusion.54
  95.7 2.7 fusion.56
  101.4 15.0 %collective-permute-done.28 = bf16[1408,256]{1,0:T(8,128)(2,1)S(1)} collective-permute-done((bf16[1408,256]{1,0:T(8,128)(2,1)S(1)}, bf16[1408,256]{1,0:T(8,128)(2,1)S(1)}, u32[]{:S(2)}, u32[]{:S(2)}) %collective-permute-start.28) | collective-permute-done | bytes 720928 | tf_op jit(solution)/shard_map/ppermute | solution.py:29
  117.0 2.9 fusion
  122.3 3.9 %collective-permute-start.23 = (bf16[128,1408]{1,0:T(8,128)(2,1)S(1)}, bf16[128,1408]{1,0:T(8,128)(2,1)S(1)}, u32[]{:S(2)}, u32[]{:S(2)}) collective-permute-start(bf16[128,1408]{1,0:T(8,128)(2,1)S(1)} %get-tuple-element.61), channel_id=1, source_target_pairs={{24,16},{26,18},{28,20},{30,22},{16,8},{18,10},{20,12},{22,14},{8,... | collective-permute-start | bytes 1081352 | tf_op jit(solution)/shard_map/ppermute | solution.py:37
  126.3 4.3 %fusion.1 = f32[512,1024]{1,0:T(8,128)} fusion(bf16[1408,512]{1,0:T(8,128)(2,1)S(1)} %collective-permute-done.9, bf16[1408,256]{1,0:T(8,128)(2,1)} %collective-permute-done.8, bf16[1408,256]{1,0:T(8,128)(2,1)S(1)} %get-tuple-element.137, bf16[128,1408]{1,0:T(8,128)(2,1)S(1)} %broadcast_select_fusion.3, bf16[128,1408]{1,0:T(8,128)(2,1)S(1)} %broadcast_select_fusion.7, ...), kind=kOutput, calls=%fused_computation.45 | convolution fusion | flops 1490812928 | bytes 6422528 | tf_op jit(solution)/shard_map/dot_general | solution.py:107
  136.1 7.6 %collective-permute-done.25 = bf16[128,1408]{1,0:T(8,128)(2,1)S(1)} collective-permute-done((bf16[128,1408]{1,0:T(8,128)(2,1)S(1)}, bf16[128,1408]{1,0:T(8,128)(2,1)S(1)}, u32[]{:S(2)}, u32[]{:S(2)}) %collective-permute-start.25) | collective-permute-done | bytes 360480 | tf_op jit(solution)/shard_map/ppermute | solution.py:37
  146.6 3.7 %collective-permute-start.27 = (bf16[128,1408]{1,0:T(8,128)(2,1)S(1)}, bf16[128,1408]{1,0:T(8,128)(2,1)S(1)}, u32[]{:S(2)}, u32[]{:S(2)}) collective-permute-start(bf16[128,1408]{1,0:T(8,128)(2,1)S(1)} %get-tuple-element.67), channel_id=1, source_target_pairs={{24,16},{26,18},{28,20},{30,22},{16,8},{18,10},{20,12},{22,14},{8,... | collective-permute-start | bytes 1081352 | tf_op jit(solution)/shard_map/ppermute | solution.py:37
  150.8 2.3 collective-permute-done.34
  154.6 3.7 %fusion.68 = f32[512,1408]{1,0:T(8,128)S(1)} fusion(bf16[1408,1024]{1,0:T(8,128)(2,1)} %constant_dynamic-update-slice_fusion, bf16[128,1024]{1,0:T(8,128)(2,1)S(1)} %collective-permute-done.21, bf16[128,1024]{1,0:T(8,128)(2,1)S(1)} %copy-done.41, bf16[128,1024]{1,0:T(8,128)(2,1)S(1)} %copy-done.39, bf16[128,1024]{1,0:T(8,128)(2,1)S(1)} %bitcast.27), kind=kOutput, calls=%fused_computation.198 | convolution fusion | flops 1480589312 | bytes 6815744 | tf_op jit(solution)/shard_map/dot_general | solution.py:133
  158.3 3.9 %collective-permute-start.30 = (bf16[128,1408]{1,0:T(8,128)(2,1)S(1)}, bf16[128,1408]{1,0:T(8,128)(2,1)S(1)}, u32[]{:S(2)}, u32[]{:S(2)}) collective-permute-start(bf16[128,1408]{1,0:T(8,128)(2,1)S(1)} %get-tuple-element.69), channel_id=1, source_target_pairs={{0,8},{2,10},{4,12},{6,14},{8,16},{10,18},{12,20},{14,22},{16,24},... | collective-permute-start | bytes 1081352 | tf_op jit(solution)/shard_map/ppermute | solution.py:37
  167.3 5.0 %fusion.55 = f32[512,1024]{1,0:T(8,128)} fusion(bf16[1408,1024]{1,0:T(8,128)(2,1)} %constant_dynamic-update-slice_fusion, bf16[128,1408]{1,0:T(8,128)(2,1)S(1)} %copy-done.29, bf16[128,1408]{1,0:T(8,128)(2,1)S(1)} %copy-done.25, bf16[128,1408]{1,0:T(8,128)(2,1)S(1)} %copy-done.27, bf16[128,1408]{1,0:T(8,128)(2,1)} %get-tuple-element.134), kind=kOutput, calls=%fused_computation.156 | convolution fusion | flops 1482162176 | bytes 6422528 | tf_op jit(solution)/shard_map/dot_general | solution.py:107
  172.3 2.4 collective-permute-done.31
  174.9 2.2 collective-permute-start.32
  177.1 3.6 %collective-permute-start.33 = (bf16[128,1408]{1,0:T(8,128)(2,1)S(1)}, bf16[128,1408]{1,0:T(8,128)(2,1)S(1)}, u32[]{:S(2)}, u32[]{:S(2)}) collective-permute-start(bf16[128,1408]{1,0:T(8,128)(2,1)S(1)} %get-tuple-element.72), channel_id=1, source_target_pairs={{24,16},{26,18},{28,20},{30,22},{16,8},{18,10},{20,12},{22,14},{8,... | collective-permute-start | bytes 1081352 | tf_op jit(solution)/shard_map/ppermute | solution.py:37
  181.9 4.6 %collective-permute-done.32 = bf16[128,1408]{1,0:T(8,128)(2,1)S(1)} collective-permute-done((bf16[128,1408]{1,0:T(8,128)(2,1)S(1)}, bf16[128,1408]{1,0:T(8,128)(2,1)S(1)}, u32[]{:S(2)}, u32[]{:S(2)}) %collective-permute-start.32) | collective-permute-done | bytes 360480 | tf_op jit(solution)/shard_map/ppermute | solution.py:37
  194.2 8.8 %collective-permute-done.41 = bf16[1408,256]{1,0:T(8,128)(2,1)S(1)} collective-permute-done((bf16[1408,256]{1,0:T(8,128)(2,1)S(1)}, bf16[1408,256]{1,0:T(8,128)(2,1)S(1)}, u32[]{:S(2)}, u32[]{:S(2)}) %collective-permute-start.41) | collective-permute-done | bytes 720928 | tf_op jit(solution)/shard_map/ppermute | solution.py:29
  203.0 11.8 %collective-permute-start.45 = (bf16[128,1408]{1,0:T(8,128)(2,1)S(1)}, bf16[128,1408]{1,0:T(8,128)(2,1)S(1)}, u32[]{:S(2)}, u32[]{:S(2)}) collective-permute-start(bf16[128,1408]{1,0:T(8,128)(2,1)S(1)} %get-tuple-element.78), channel_id=1, source_target_pairs={{24,16},{26,18},{28,20},{30,22},{16,8},{18,10},{20,12},{22,14},{8,... | collective-permute-start | bytes 1081352 | tf_op jit(solution)/shard_map/ppermute | solution.py:37
  219.3 3.1 fusion.53
  222.4 4.2 %collective-permute-start.42 = (bf16[128,1408]{1,0:T(8,128)(2,1)S(1)}, bf16[128,1408]{1,0:T(8,128)(2,1)S(1)}, u32[]{:S(2)}, u32[]{:S(2)}) collective-permute-start(bf16[128,1408]{1,0:T(8,128)(2,1)S(1)} %get-tuple-element.75), channel_id=1, source_target_pairs={{0,8},{2,10},{4,12},{6,14},{8,16},{10,18},{12,20},{14,22},{16,24},... | collective-permute-start | bytes 1081352 | tf_op jit(solution)/shard_map/ppermute | solution.py:37
  228.5 2.3 fusion.28
  243.1 6.0 %collective-permute-done.47 = bf16[1408,256]{1,0:T(8,128)(2,1)S(1)} collective-permute-done((bf16[1408,256]{1,0:T(8,128)(2,1)S(1)}, bf16[1408,256]{1,0:T(8,128)(2,1)S(1)}, u32[]{:S(2)}, u32[]{:S(2)}) %collective-permute-start.47) | collective-permute-done | bytes 720928 | tf_op jit(solution)/shard_map/ppermute | solution.py:29
  252.7 10.6 %collective-permute-done.36 = bf16[128,1024]{1,0:T(8,128)(2,1)S(1)} collective-permute-done((bf16[128,1024]{1,0:T(8,128)(2,1)S(1)}, bf16[128,1024]{1,0:T(8,128)(2,1)S(1)}, u32[]{:S(2)}, u32[]{:S(2)}) %collective-permute-start.36) | collective-permute-done | bytes 262176 | tf_op jit(solution)/shard_map/ppermute | solution.py:33
  268.6 2.3 copy.16
  277.3 7.6 %collective-permute-start.60 = (bf16[128,1408]{1,0:T(8,128)(2,1)S(1)}, bf16[128,1408]{1,0:T(8,128)(2,1)S(1)}, u32[]{:S(2)}, u32[]{:S(2)}) collective-permute-start(bf16[128,1408]{1,0:T(8,128)(2,1)S(1)} %get-tuple-element.90), channel_id=1, source_target_pairs={{0,8},{2,10},{4,12},{6,14},{8,16},{10,18},{12,20},{14,22},{1,9},{3... | collective-permute-start | bytes 1081352 | tf_op jit(solution)/shard_map/ppermute | solution.py:37
  286.2 2.3 add_convert_fusion.7
  288.5 2.7 slice_add_fusion
  293.1 4.5 %collective-permute-start.52 = (bf16[128,1408]{1,0:T(8,128)(2,1)}, bf16[128,1408]{1,0:T(8,128)(2,1)}, u32[]{:S(2)}, u32[]{:S(2)}) collective-permute-start(bf16[128,1408]{1,0:T(8,128)(2,1)} %get-tuple-element.83), channel_id=1, source_target_pairs={{0,8},{2,10},{4,12},{6,14},{8,16},{10,18},{12,20},{14,22},{1,9},{3... | collective-permute-start | bytes 1081352 | tf_op jit(solution)/shard_map/ppermute | solution.py:37
  304.5 4.0 %collective-permute-done.53 = bf16[128,1408]{1,0:T(8,128)(2,1)} collective-permute-done((bf16[128,1408]{1,0:T(8,128)(2,1)}, bf16[128,1408]{1,0:T(8,128)(2,1)}, u32[]{:S(2)}, u32[]{:S(2)}) %collective-permute-start.53) | collective-permute-done | bytes 360480 | tf_op jit(solution)/shard_map/ppermute | solution.py:37
  310.4 3.9 %collective-permute-start.63 = (bf16[128,1408]{1,0:T(8,128)(2,1)}, bf16[128,1408]{1,0:T(8,128)(2,1)S(1)}, u32[]{:S(2)}, u32[]{:S(2)}) collective-permute-start(bf16[128,1408]{1,0:T(8,128)(2,1)} %get-tuple-element.93), channel_id=1, source_target_pairs={{24,16},{26,18},{28,20},{30,22},{16,8},{18,10},{20,12},{22,14},{8,... | collective-permute-start | bytes 1081352 | tf_op jit(solution)/shard_map/ppermute | solution.py:37
  316.9 4.3 %collective-permute-start.58 = (bf16[128,1408]{1,0:T(8,128)(2,1)S(1)}, bf16[128,1408]{1,0:T(8,128)(2,1)S(1)}, u32[]{:S(2)}, u32[]{:S(2)}) collective-permute-start(bf16[128,1408]{1,0:T(8,128)(2,1)S(1)} %get-tuple-element.88), channel_id=1, source_target_pairs={{0,8},{2,10},{4,12},{6,14},{8,16},{10,18},{12,20},{14,22},{16,24},... | collective-permute-start | bytes 1081352 | tf_op jit(solution)/shard_map/ppermute | solution.py:37
  323.3 2.7 pad_maximum_fusion
  328.0 2.5 collective-permute-done.59
  330.5 2.3 fusion.34
  (275 shorter events, 124.5 us)
Async XLA Ops:
  3.7 24.9 %collective-permute-start.5 = (bf16[128,1408]{1,0:T(8,128)(2,1)}, bf16[128,1408]{1,0:T(8,128)(2,1)}, u32[]{:S(2)}, u32[]{:S(2)}) collective-permute-start(bf16[128,1408]{1,0:T(8,128)(2,1)} %get-tuple-element.134), channel_id=1, source_target_pairs={{24,16},{26,18},{28,20},{30,22},{16,8},{18,10},{20,12},{22,14},{8,... | collective-permute-start | bytes 1081352 | tf_op jit(solution)/shard_map/ppermute | solution.py:37
  5.7 24.5 %collective-permute-start.4 = (bf16[128,1408]{1,0:T(8,128)(2,1)}, bf16[128,1408]{1,0:T(8,128)(2,1)}, u32[]{:S(2)}, u32[]{:S(2)}) collective-permute-start(bf16[128,1408]{1,0:T(8,128)(2,1)} %get-tuple-element.134), channel_id=1, source_target_pairs={{0,8},{2,10},{4,12},{6,14},{8,16},{10,18},{12,20},{14,22},{16,24},... | collective-permute-start | bytes 1081352 | tf_op jit(solution)/shard_map/ppermute | solution.py:37
  9.6 20.5 %collective-permute-start.1 = (bf16[128,1408]{1,0:T(8,128)(2,1)}, bf16[128,1408]{1,0:T(8,128)(2,1)}, u32[]{:S(2)}, u32[]{:S(2)}) collective-permute-start(bf16[128,1408]{1,0:T(8,128)(2,1)} %get-tuple-element.135), channel_id=1, source_target_pairs={{0,8},{2,10},{4,12},{6,14},{8,16},{10,18},{12,20},{14,22},{16,24},... | collective-permute-start | bytes 1081352 | tf_op jit(solution)/shard_map/ppermute | solution.py:37
  13.8 16.3 %collective-permute-start = (bf16[128,1408]{1,0:T(8,128)(2,1)}, bf16[128,1408]{1,0:T(8,128)(2,1)}, u32[]{:S(2)}, u32[]{:S(2)}) collective-permute-start(bf16[128,1408]{1,0:T(8,128)(2,1)} %get-tuple-element.135), channel_id=1, source_target_pairs={{24,16},{26,18},{28,20},{30,22},{16,8},{18,10},{20,12},{22,14},{8,... | collective-permute-start | bytes 1081352 | tf_op jit(solution)/shard_map/ppermute | solution.py:37
  17.2 24.6 %collective-permute-start.14 = (bf16[128,2048]{0,1:T(8,128)(2,1)}, bf16[128,2048]{0,1:T(8,128)(2,1)}, u32[]{:S(2)}, u32[]{:S(2)}) collective-permute-start(bf16[128,2048]{0,1:T(8,128)(2,1)} %copy.9), channel_id=1, source_target_pairs={{0,1},{1,0},{2,3},{3,2},{4,5},{5,4},{6,7},{7,6},{8,9},{9,8},{10,11... | collective-permute-start | bytes 1572872 | tf_op jit(solution)/shard_map/ppermute | solution.py:40
  28.6 34.0 %collective-permute-start.8 = (bf16[1408,256]{1,0:T(8,128)(2,1)S(1)}, bf16[1408,256]{1,0:T(8,128)(2,1)}, u32[]{:S(2)}, u32[]{:S(2)}) collective-permute-start(bf16[1408,256]{1,0:T(8,128)(2,1)S(1)} %get-tuple-element.137), channel_id=1, source_target_pairs={{0,4},{2,6},{4,0},{6,2},{8,12},{10,14},{12,8},{14,10},{16,20},{18,... | collective-permute-start | bytes 2162696 | tf_op jit(solution)/shard_map/ppermute | solution.py:29
  30.1 24.8 %collective-permute-start.10 = (bf16[128,1408]{1,0:T(8,128)(2,1)}, bf16[128,1408]{1,0:T(8,128)(2,1)}, u32[]{:S(2)}, u32[]{:S(2)}) collective-permute-start(bf16[128,1408]{1,0:T(8,128)(2,1)} %collective-permute-done.4), channel_id=1, source_target_pairs={{8,16},{10,18},{12,20},{14,22},{16,24},{18,26},{20,28},{22,30},{9,... | collective-permute-start | bytes 1081352 | tf_op jit(solution)/shard_map/ppermute | solution.py:37
  34.4 20.5 %collective-permute-start.11 = (bf16[128,1408]{1,0:T(8,128)(2,1)}, bf16[128,1408]{1,0:T(8,128)(2,1)}, u32[]{:S(2)}, u32[]{:S(2)}) collective-permute-start(bf16[128,1408]{1,0:T(8,128)(2,1)} %collective-permute-done.5), channel_id=1, source_target_pairs={{16,8},{18,10},{20,12},{22,14},{8,0},{10,2},{12,4},{14,6},{17,9},{... | collective-permute-start | bytes 1081352 | tf_op jit(solution)/shard_map/ppermute | solution.py:37
  36.3 15.9 %collective-permute-start.2 = (bf16[128,1408]{1,0:T(8,128)(2,1)}, bf16[128,1408]{1,0:T(8,128)(2,1)}, u32[]{:S(2)}, u32[]{:S(2)}) collective-permute-start(bf16[128,1408]{1,0:T(8,128)(2,1)} %collective-permute-done.1), channel_id=1, source_target_pairs={{8,16},{10,18},{12,20},{14,22},{16,24},{18,26},{20,28},{22,30},{9,... | collective-permute-start | bytes 1081352 | tf_op jit(solution)/shard_map/ppermute | solution.py:37
  41.8 16.4 %collective-permute-start.3 = (bf16[128,1408]{1,0:T(8,128)(2,1)}, bf16[128,1408]{1,0:T(8,128)(2,1)}, u32[]{:S(2)}, u32[]{:S(2)}) collective-permute-start(bf16[128,1408]{1,0:T(8,128)(2,1)} %collective-permute-done), channel_id=1, source_target_pairs={{16,8},{18,10},{20,12},{22,14},{8,0},{10,2},{12,4},{14,6},{17,9},{... | collective-permute-start | bytes 1081352 | tf_op jit(solution)/shard_map/ppermute | solution.py:37
  52.2 27.8 %collective-permute-start.21 = (bf16[128,1024]{1,0:T(8,128)(2,1)}, bf16[128,1024]{1,0:T(8,128)(2,1)S(1)}, u32[]{:S(2)}, u32[]{:S(2)}) collective-permute-start(bf16[128,1024]{1,0:T(8,128)(2,1)} %bitcast.5), channel_id=1, source_target_pairs={{0,8},{2,10},{4,12},{6,14},{8,16},{10,18},{12,20},{14,22},{16,24},... | collective-permute-start | bytes 786440 | tf_op jit(solution)/shard_map/ppermute | solution.py:33
  58.8 14.3 %collective-permute-start.7 = (bf16[128,1408]{1,0:T(8,128)(2,1)}, bf16[128,1408]{1,0:T(8,128)(2,1)S(1)}, u32[]{:S(2)}, u32[]{:S(2)}) collective-permute-start(bf16[128,1408]{1,0:T(8,128)(2,1)} %collective-permute-done.3), channel_id=1, source_target_pairs={{8,0},{10,2},{12,4},{14,6},{9,1},{11,3},{13,5},{15,7}} | collective-permute-start | bytes 1081352 | tf_op jit(solution)/shard_map/ppermute | solution.py:37
  61.9 15.4 %collective-permute-start.12 = (bf16[128,1408]{1,0:T(8,128)(2,1)}, bf16[128,1408]{1,0:T(8,128)(2,1)S(1)}, u32[]{:S(2)}, u32[]{:S(2)}) collective-permute-start(bf16[128,1408]{1,0:T(8,128)(2,1)} %collective-permute-done.10), channel_id=1, source_target_pairs={{16,24},{18,26},{20,28},{22,30},{17,25},{19,27},{21,29},{23,31}} | collective-permute-start | bytes 1081352 | tf_op jit(solution)/shard_map/ppermute | solution.py:37
  62.6 15.2 %collective-permute-start.13 = (bf16[128,1408]{1,0:T(8,128)(2,1)}, bf16[128,1408]{1,0:T(8,128)(2,1)S(1)}, u32[]{:S(2)}, u32[]{:S(2)}) collective-permute-start(bf16[128,1408]{1,0:T(8,128)(2,1)} %collective-permute-done.11), channel_id=1, source_target_pairs={{8,0},{10,2},{12,4},{14,6},{9,1},{11,3},{13,5},{15,7}} | collective-permute-start | bytes 1081352 | tf_op jit(solution)/shard_map/ppermute | solution.py:37
  68.5 14.0 %collective-permute-start.19 = (bf16[128,1024]{1,0:T(8,128)(2,1)S(1)}, bf16[128,1024]{1,0:T(8,128)(2,1)S(1)}, u32[]{:S(2)}, u32[]{:S(2)}) collective-permute-start(bf16[128,1024]{1,0:T(8,128)(2,1)S(1)} %bitcast.33), channel_id=1, source_target_pairs={{0,24},{2,26},{4,28},{6,30},{8,0},{10,2},{12,4},{14,6},{16,8},{18,... | collective-permute-start | bytes 786440 | tf_op jit(solution)/shard_map/ppermute | solution.py:33
  77.3 21.4 %collective-permute-start.15 = (bf16[1408,256]{1,0:T(8,128)(2,1)S(1)}, bf16[1408,256]{1,0:T(8,128)(2,1)S(1)}, u32[]{:S(2)}, u32[]{:S(2)}) collective-permute-start(bf16[1408,256]{1,0:T(8,128)(2,1)S(1)} %get-tuple-element.55), channel_id=1, source_target_pairs={{0,4},{2,6},{4,0},{6,2},{8,12},{10,14},{12,8},{14,10},{16,20},{18,... | collective-permute-start | bytes 2162696 | tf_op jit(solution)/shard_map/ppermute | solution.py:29
  77.8 38.7 %collective-permute-start.9 = (bf16[1408,512]{1,0:T(8,128)(2,1)S(1)}, bf16[1408,512]{1,0:T(8,128)(2,1)S(1)}, u32[]{:S(2)}, u32[]{:S(2)}) collective-permute-start(bf16[1408,512]{1,0:T(8,128)(2,1)S(1)} %pad_maximum_fusion.3), channel_id=1, source_target_pairs={{0,2},{2,0},{4,6},{6,4},{8,10},{10,8},{12,14},{14,12},{16,18},{18,... | collective-permute-start | bytes 4325384 | tf_op jit(solution)/shard_map/ppermute | solution.py:29
  80.0 39.9 %collective-permute-start.17 = (bf16[128,1408]{1,0:T(8,128)(2,1)S(1)}, bf16[128,1408]{1,0:T(8,128)(2,1)S(1)}, u32[]{:S(2)}, u32[]{:S(2)}) collective-permute-start(bf16[128,1408]{1,0:T(8,128)(2,1)S(1)} %copy-done.17), channel_id=1, source_target_pairs={{24,16},{26,18},{28,20},{30,22},{16,8},{18,10},{20,12},{22,14},{8,... | collective-permute-start | bytes 1081352 | tf_op jit(solution)/shard_map/ppermute | solution.py:37
  82.5 37.5 %collective-permute-start.18 = (bf16[128,1408]{1,0:T(8,128)(2,1)S(1)}, bf16[128,1408]{1,0:T(8,128)(2,1)S(1)}, u32[]{:S(2)}, u32[]{:S(2)}) collective-permute-start(bf16[128,1408]{1,0:T(8,128)(2,1)S(1)} %copy-done.17), channel_id=1, source_target_pairs={{0,8},{2,10},{4,12},{6,14},{8,16},{10,18},{12,20},{14,22},{16,24},... | collective-permute-start | bytes 1081352 | tf_op jit(solution)/shard_map/ppermute | solution.py:37
  86.8 47.7 %collective-permute-start.24 = (bf16[128,1408]{1,0:T(8,128)(2,1)S(1)}, bf16[128,1408]{1,0:T(8,128)(2,1)S(1)}, u32[]{:S(2)}, u32[]{:S(2)}) collective-permute-start(bf16[128,1408]{1,0:T(8,128)(2,1)S(1)} %copy-done.18), channel_id=1, source_target_pairs={{0,8},{2,10},{4,12},{6,14},{8,16},{10,18},{12,20},{14,22},{16,24},... | collective-permute-start | bytes 1081352 | tf_op jit(solution)/shard_map/ppermute | solution.py:37
  98.7 17.8 %collective-permute-start.28 = (bf16[1408,256]{1,0:T(8,128)(2,1)S(1)}, bf16[1408,256]{1,0:T(8,128)(2,1)S(1)}, u32[]{:S(2)}, u32[]{:S(2)}) collective-permute-start(bf16[1408,256]{1,0:T(8,128)(2,1)S(1)} %get-tuple-element.68), channel_id=1, source_target_pairs={{0,4},{2,6},{4,0},{6,2},{8,12},{10,14},{12,8},{14,10},{16,20},{18,... | collective-permute-start | bytes 2162696 | tf_op jit(solution)/shard_map/ppermute | solution.py:29
  116.4 27.2 %collective-permute-start.46 = (bf16[1408,512]{1,0:T(8,128)(2,1)S(1)}, bf16[1408,512]{1,0:T(8,128)(2,1)S(1)}, u32[]{:S(2)}, u32[]{:S(2)}) collective-permute-start(bf16[1408,512]{1,0:T(8,128)(2,1)S(1)} %slice.370), channel_id=1, source_target_pairs={{0,2},{2,0},{4,6},{6,4},{8,10},{10,8},{12,14},{14,12},{16,18},{18,... | collective-permute-start | bytes 4325384 | tf_op jit(solution)/shard_map/ppermute | solution.py:29
  116.4 30.1 %collective-permute-start.40 = (bf16[1408,512]{1,0:T(8,128)(2,1)S(1)}, bf16[1408,512]{1,0:T(8,128)(2,1)S(1)}, u32[]{:S(2)}, u32[]{:S(2)}) collective-permute-start(bf16[1408,512]{1,0:T(8,128)(2,1)S(1)} %slice.371), channel_id=1, source_target_pairs={{0,2},{2,0},{4,6},{6,4},{8,10},{10,8},{12,14},{14,12},{16,18},{18,... | collective-permute-start | bytes 4325384 | tf_op jit(solution)/shard_map/ppermute | solution.py:29
  134.2 19.1 %collective-permute-start.16 = (bf16[1408,512]{1,0:T(8,128)(2,1)S(1)}, bf16[1408,512]{1,0:T(8,128)(2,1)S(1)}, u32[]{:S(2)}, u32[]{:S(2)}) collective-permute-start(bf16[1408,512]{1,0:T(8,128)(2,1)S(1)} %pad_maximum_fusion.5), channel_id=1, source_target_pairs={{0,2},{2,0},{4,6},{6,4},{8,10},{10,8},{12,14},{14,12},{16,18},{18,... | collective-permute-start | bytes 4325384 | tf_op jit(solution)/shard_map/ppermute | solution.py:29
  134.5 18.6 %collective-permute-start.34 = (bf16[1408,256]{1,0:T(8,128)(2,1)S(1)}, bf16[1408,256]{1,0:T(8,128)(2,1)S(1)}, u32[]{:S(2)}, u32[]{:S(2)}) collective-permute-start(bf16[1408,256]{1,0:T(8,128)(2,1)S(1)} %pad.13), channel_id=1, source_target_pairs={{0,4},{2,6},{4,0},{6,2},{8,12},{10,14},{12,8},{14,10},{16,20},{18,... | collective-permute-start | bytes 2162696 | tf_op jit(solution)/shard_map/ppermute | solution.py:29
  143.6 72.5 %collective-permute-start.29 = (bf16[1408,512]{1,0:T(8,128)(2,1)S(1)}, bf16[1408,512]{1,0:T(8,128)(2,1)S(1)}, u32[]{:S(2)}, u32[]{:S(2)}) collective-permute-start(bf16[1408,512]{1,0:T(8,128)(2,1)S(1)} %pad_maximum_fusion.7), channel_id=1, source_target_pairs={{0,2},{2,0},{4,6},{6,4},{8,10},{10,8},{12,14},{14,12},{16,18},{18,... | collective-permute-start | bytes 4325384 | tf_op jit(solution)/shard_map/ppermute | solution.py:29
  143.7 18.6 %collective-permute-start.26 = (bf16[128,1408]{1,0:T(8,128)(2,1)S(1)}, bf16[128,1408]{1,0:T(8,128)(2,1)S(1)}, u32[]{:S(2)}, u32[]{:S(2)}) collective-permute-start(bf16[128,1408]{1,0:T(8,128)(2,1)S(1)} %get-tuple-element.66), channel_id=1, source_target_pairs={{0,8},{2,10},{4,12},{6,14},{8,16},{10,18},{12,20},{14,22},{16,24},... | collective-permute-start | bytes 1081352 | tf_op jit(solution)/shard_map/ppermute | solution.py:37
  146.6 17.7 %collective-permute-start.27 = (bf16[128,1408]{1,0:T(8,128)(2,1)S(1)}, bf16[128,1408]{1,0:T(8,128)(2,1)S(1)}, u32[]{:S(2)}, u32[]{:S(2)}) collective-permute-start(bf16[128,1408]{1,0:T(8,128)(2,1)S(1)} %get-tuple-element.67), channel_id=1, source_target_pairs={{24,16},{26,18},{28,20},{30,22},{16,8},{18,10},{20,12},{22,14},{8,... | collective-permute-start | bytes 1081352 | tf_op jit(solution)/shard_map/ppermute | solution.py:37
  153.2 77.6 %collective-permute-start.35 = (bf16[1408,512]{1,0:T(8,128)(2,1)S(1)}, bf16[1408,512]{1,0:T(8,128)(2,1)S(1)}, u32[]{:S(2)}, u32[]{:S(2)}) collective-permute-start(bf16[1408,512]{1,0:T(8,128)(2,1)S(1)} %pad_maximum_fusion.9), channel_id=1, source_target_pairs={{0,2},{2,0},{4,6},{6,4},{8,10},{10,8},{12,14},{14,12},{16,18},{18,... | collective-permute-start | bytes 4325384 | tf_op jit(solution)/shard_map/ppermute | solution.py:29
  158.3 14.0 %collective-permute-start.30 = (bf16[128,1408]{1,0:T(8,128)(2,1)S(1)}, bf16[128,1408]{1,0:T(8,128)(2,1)S(1)}, u32[]{:S(2)}, u32[]{:S(2)}) collective-permute-start(bf16[128,1408]{1,0:T(8,128)(2,1)S(1)} %get-tuple-element.69), channel_id=1, source_target_pairs={{0,8},{2,10},{4,12},{6,14},{8,16},{10,18},{12,20},{14,22},{16,24},... | collective-permute-start | bytes 1081352 | tf_op jit(solution)/shard_map/ppermute | solution.py:37
  166.3 74.6 %collective-permute-start.50 = (bf16[1408,512]{1,0:T(8,128)(2,1)S(1)}, bf16[1408,512]{1,0:T(8,128)(2,1)S(1)}, u32[]{:S(2)}, u32[]{:S(2)}) collective-permute-start(bf16[1408,512]{1,0:T(8,128)(2,1)S(1)} %slice.369), channel_id=1, source_target_pairs={{0,2},{2,0},{4,6},{6,4},{8,10},{10,8},{12,14},{14,12},{16,18},{18,... | collective-permute-start | bytes 4325384 | tf_op jit(solution)/shard_map/ppermute | solution.py:29
  186.5 16.5 %collective-permute-start.41 = (bf16[1408,256]{1,0:T(8,128)(2,1)S(1)}, bf16[1408,256]{1,0:T(8,128)(2,1)S(1)}, u32[]{:S(2)}, u32[]{:S(2)}) collective-permute-start(bf16[1408,256]{1,0:T(8,128)(2,1)S(1)} %slice.375), channel_id=1, source_target_pairs={{0,4},{2,6},{4,0},{6,2},{8,12},{10,14},{12,8},{14,10},{16,20},{18,... | collective-permute-start | bytes 2162696 | tf_op jit(solution)/shard_map/ppermute | solution.py:29
  188.6 33.8 %collective-permute-start.44 = (bf16[128,1408]{1,0:T(8,128)(2,1)S(1)}, bf16[128,1408]{1,0:T(8,128)(2,1)S(1)}, u32[]{:S(2)}, u32[]{:S(2)}) collective-permute-start(bf16[128,1408]{1,0:T(8,128)(2,1)S(1)} %get-tuple-element.77), channel_id=1, source_target_pairs={{0,8},{2,10},{4,12},{6,14},{8,16},{10,18},{12,20},{14,22},{16,24},... | collective-permute-start | bytes 1081352 | tf_op jit(solution)/shard_map/ppermute | solution.py:37
  203.0 23.6 %collective-permute-start.45 = (bf16[128,1408]{1,0:T(8,128)(2,1)S(1)}, bf16[128,1408]{1,0:T(8,128)(2,1)S(1)}, u32[]{:S(2)}, u32[]{:S(2)}) collective-permute-start(bf16[128,1408]{1,0:T(8,128)(2,1)S(1)} %get-tuple-element.78), channel_id=1, source_target_pairs={{24,16},{26,18},{28,20},{30,22},{16,8},{18,10},{20,12},{22,14},{8,... | collective-permute-start | bytes 1081352 | tf_op jit(solution)/shard_map/ppermute | solution.py:37
  216.1 72.4 %collective-permute-start.56 = (bf16[1408,512]{1,0:T(8,128)(2,1)}, bf16[1408,512]{1,0:T(8,128)(2,1)}, u32[]{:S(2)}, u32[]{:S(2)}) collective-permute-start(bf16[1408,512]{1,0:T(8,128)(2,1)} %slice.368), channel_id=1, source_target_pairs={{0,2},{2,0},{4,6},{6,4},{8,10},{10,8},{12,14},{14,12},{16,18},{18,... | collective-permute-start | bytes 4325384 | tf_op jit(solution)/shard_map/ppermute | solution.py:29
  222.4 16.0 %collective-permute-start.42 = (bf16[128,1408]{1,0:T(8,128)(2,1)S(1)}, bf16[128,1408]{1,0:T(8,128)(2,1)S(1)}, u32[]{:S(2)}, u32[]{:S(2)}) collective-permute-start(bf16[128,1408]{1,0:T(8,128)(2,1)S(1)} %get-tuple-element.75), channel_id=1, source_target_pairs={{0,8},{2,10},{4,12},{6,14},{8,16},{10,18},{12,20},{14,22},{16,24},... | collective-permute-start | bytes 1081352 | tf_op jit(solution)/shard_map/ppermute | solution.py:37
  230.8 18.2 %collective-permute-start.47 = (bf16[1408,256]{1,0:T(8,128)(2,1)S(1)}, bf16[1408,256]{1,0:T(8,128)(2,1)S(1)}, u32[]{:S(2)}, u32[]{:S(2)}) collective-permute-start(bf16[1408,256]{1,0:T(8,128)(2,1)S(1)} %slice.374), channel_id=1, source_target_pairs={{0,4},{2,6},{4,0},{6,2},{8,12},{10,14},{12,8},{14,10},{16,20},{18,... | collective-permute-start | bytes 2162696 | tf_op jit(solution)/shard_map/ppermute | solution.py:29
  238.4 27.6 %collective-permute-start.38 = (bf16[128,1024]{1,0:T(8,128)(2,1)S(1)}, bf16[128,1024]{1,0:T(8,128)(2,1)S(1)}, u32[]{:S(2)}, u32[]{:S(2)}) collective-permute-start(bf16[128,1024]{1,0:T(8,128)(2,1)S(1)} %get-tuple-element.146), channel_id=1, source_target_pairs={{0,8},{2,10},{4,12},{6,14},{8,16},{10,18},{12,20},{14,22},{16,24},... | collective-permute-start | bytes 786440 | tf_op jit(solution)/shard_map/ppermute | solution.py:33
  240.4 24.2 %collective-permute-start.37 = (bf16[128,1024]{1,0:T(8,128)(2,1)S(1)}, bf16[128,1024]{1,0:T(8,128)(2,1)S(1)}, u32[]{:S(2)}, u32[]{:S(2)}) collective-permute-start(bf16[128,1024]{1,0:T(8,128)(2,1)S(1)} %get-tuple-element.148), channel_id=1, source_target_pairs={{0,16},{2,18},{4,20},{6,22},{8,24},{10,26},{12,28},{14,30},{16,0},... | collective-permute-start | bytes 786440 | tf_op jit(solution)/shard_map/ppermute | solution.py:33
  241.2 22.0 %collective-permute-start.36 = (bf16[128,1024]{1,0:T(8,128)(2,1)S(1)}, bf16[128,1024]{1,0:T(8,128)(2,1)S(1)}, u32[]{:S(2)}, u32[]{:S(2)}) collective-permute-start(bf16[128,1024]{1,0:T(8,128)(2,1)S(1)} %get-tuple-element.149), channel_id=1, source_target_pairs={{0,24},{2,26},{4,28},{6,30},{8,0},{10,2},{12,4},{14,6},{16,8},{18,... | collective-permute-start | bytes 786440 | tf_op jit(solution)/shard_map/ppermute | solution.py:33
  249.1 23.3 %collective-permute-start.54 = (bf16[128,1408]{1,0:T(8,128)(2,1)}, bf16[128,1408]{1,0:T(8,128)(2,1)}, u32[]{:S(2)}, u32[]{:S(2)}) collective-permute-start(bf16[128,1408]{1,0:T(8,128)(2,1)} %get-tuple-element.85), channel_id=1, source_target_pairs={{0,8},{2,10},{4,12},{6,14},{1,9},{3,11},{5,13},{7,15}} | collective-permute-start | bytes 1081352 | tf_op jit(solution)/shard_map/ppermute | solution.py:37
  272.4 20.7 %collective-permute-start.51 = (bf16[1408,256]{1,0:T(8,128)(2,1)S(1)}, bf16[1408,256]{1,0:T(8,128)(2,1)S(1)}, u32[]{:S(2)}, u32[]{:S(2)}) collective-permute-start(bf16[1408,256]{1,0:T(8,128)(2,1)S(1)} %copy-done.15), channel_id=1, source_target_pairs={{0,4},{2,6},{4,0},{6,2},{8,12},{10,14},{12,8},{14,10},{16,20},{18,... | collective-permute-start | bytes 2162696 | tf_op jit(solution)/shard_map/ppermute | solution.py:29
  273.4 28.9 %collective-permute-start.39 = (bf16[128,2048]{0,1:T(8,128)(2,1)S(1)}, bf16[128,2048]{0,1:T(8,128)(2,1)S(1)}, u32[]{:S(2)}, u32[]{:S(2)}) collective-permute-start(bf16[128,2048]{0,1:T(8,128)(2,1)S(1)} %dynamic-slice_bitcast_fusion), channel_id=1, source_target_pairs={{0,1},{1,0},{2,3},{3,2},{4,5},{5,4},{6,7},{7,6},{8,9},{9,8},{10,11... | collective-permute-start | bytes 1572872 | tf_op jit(solution)/shard_map/ppermute | solution.py:40
  277.3 23.0 %collective-permute-start.60 = (bf16[128,1408]{1,0:T(8,128)(2,1)S(1)}, bf16[128,1408]{1,0:T(8,128)(2,1)S(1)}, u32[]{:S(2)}, u32[]{:S(2)}) collective-permute-start(bf16[128,1408]{1,0:T(8,128)(2,1)S(1)} %get-tuple-element.90), channel_id=1, source_target_pairs={{0,8},{2,10},{4,12},{6,14},{8,16},{10,18},{12,20},{14,22},{1,9},{3... | collective-permute-start | bytes 1081352 | tf_op jit(solution)/shard_map/ppermute | solution.py:37
  284.9 16.4 %collective-permute-start.61 = (bf16[128,1408]{1,0:T(8,128)(2,1)S(1)}, bf16[128,1408]{1,0:T(8,128)(2,1)S(1)}, u32[]{:S(2)}, u32[]{:S(2)}) collective-permute-start(bf16[128,1408]{1,0:T(8,128)(2,1)S(1)} %get-tuple-element.91), channel_id=1, source_target_pairs={{24,16},{26,18},{28,20},{30,22},{16,8},{18,10},{20,12},{22,14},{25... | collective-permute-start | bytes 1081352 | tf_op jit(solution)/shard_map/ppermute | solution.py:37
  300.3 16.6 %collective-permute-start.57 = (bf16[1408,256]{1,0:T(8,128)(2,1)}, bf16[1408,256]{1,0:T(8,128)(2,1)S(1)}, u32[]{:S(2)}, u32[]{:S(2)}) collective-permute-start(bf16[1408,256]{1,0:T(8,128)(2,1)} %slice.372), channel_id=1, source_target_pairs={{0,4},{2,6},{4,0},{6,2},{8,12},{10,14},{12,8},{14,10},{16,20},{18,... | collective-permute-start | bytes 2162696 | tf_op jit(solution)/shard_map/ppermute | solution.py:29
  308.5 17.5 %collective-permute-start.62 = (bf16[128,1408]{1,0:T(8,128)(2,1)}, bf16[128,1408]{1,0:T(8,128)(2,1)S(1)}, u32[]{:S(2)}, u32[]{:S(2)}) collective-permute-start(bf16[128,1408]{1,0:T(8,128)(2,1)} %get-tuple-element.92), channel_id=1, source_target_pairs={{0,8},{2,10},{4,12},{6,14},{8,16},{10,18},{12,20},{14,22},{16,24},... | collective-permute-start | bytes 1081352 | tf_op jit(solution)/shard_map/ppermute | solution.py:37
  310.4 15.6 %collective-permute-start.63 = (bf16[128,1408]{1,0:T(8,128)(2,1)}, bf16[128,1408]{1,0:T(8,128)(2,1)S(1)}, u32[]{:S(2)}, u32[]{:S(2)}) collective-permute-start(bf16[128,1408]{1,0:T(8,128)(2,1)} %get-tuple-element.93), channel_id=1, source_target_pairs={{24,16},{26,18},{28,20},{30,22},{16,8},{18,10},{20,12},{22,14},{8,... | collective-permute-start | bytes 1081352 | tf_op jit(solution)/shard_map/ppermute | solution.py:37
  (63 other events, 714.1 us)

commit v4 on v3

v4 whole, which is shorter than its diff:
```python
import jax
import jax.numpy as jnp
from jax import lax
from jax.sharding import PartitionSpec as P

QUAD = 4
CHUNKS = 2
ORDER = (0, 2, 1, 3)


def after(value, *others):
    return lax.optimization_barrier((value,) + others)[0]


def slot_of(near):
    result = []
    for block in range(QUAD):
        k = near ^ block
        result.append(((k & 1) << 1) | (k >> 1))
    return result


def solution(mesh):
    n_hst, n_local = mesh.shape["hst"], mesh.shape["local"]
    n_far = n_hst // QUAD

    def swap(value, bit):
        return lax.ppermute(value, "hst", [(h, h ^ bit) for h in range(n_hst)])

    def shift(value, step):
        pairs = [(h, (h + step * QUAD) % n_hst) for h in range(n_hst)]
        return lax.ppermute(value, "hst", pairs)

    def hop(value, way, sources):
        pairs = [(s * QUAD + q, (s + way) * QUAD + q) for s in sources for q in range(QUAD)]
        return lax.ppermute(value, "hst", pairs)

    def local_shift(value, step):
        return lax.ppermute(value, "local", [(i, (i + step) % n_local) for i in range(n_local)])

    def on_device(gate_act, up_act, cotangent, down_weight):
        h = lax.axis_index("hst")
        x = lax.axis_index("local")
        far, near = h // QUAD, h % QUAD
        tokens, half = cotangent.shape
        width = down_weight.shape[1]
        hidden_units = gate_act.shape[1]
        n_chunks = CHUNKS
        lanes = -(-hidden_units // 128)
        chunk = 128 * -(-lanes // n_chunks)
        bounds = [(f * chunk, min(hidden_units, (f + 1) * chunk)) for f in range(n_chunks)]

        parts = [cotangent]
        for step in range(1, n_local):
            parts.append(local_shift(cotangent, n_local - step))
        twice = jnp.concatenate(parts + parts[:-1], axis=1)
        cot_full = lax.dynamic_slice_in_dim(
            twice, ((n_local - x) % n_local) * half, n_local * half, axis=1
        )
        cot_view = cot_full.reshape(tokens, n_far, QUAD, width)
        cot_view = jnp.concatenate(
            [lax.dynamic_slice_in_dim(cot_view, near ^ k, 1, axis=2) for k in ORDER], axis=2
        )
        cot_view = cot_view.reshape(tokens, n_far, QUAD * width)

        def cot_for(step):
            return lax.dynamic_index_in_dim(cot_view, (far + step) % n_far, axis=1, keepdims=False)

        cot_rows = jnp.concatenate(
            [cot_for(0)] + [shift(cot_for(n_far - e), n_far - e) for e in range(1, n_far)], axis=0
        )

        weights, last = [], []
        for f, (lo, hi) in enumerate(bounds):
            weight = after(down_weight[lo:hi], *last)
            other = swap(weight, 2)
            last = [other]
            if f == 0:
                last.append(parts[1])
            if f == 1:
                last.append(cot_rows)
            pair = jnp.concatenate([weight, other], axis=1)
            weights.append(jnp.concatenate([pair, swap(pair, 1)], axis=1))

        wide, hidden, terms = {}, {}, {}
        for f, (lo, hi) in enumerate(bounds):
            gate_wide = gate_act[:, lo:hi].astype(jnp.float32)
            up_wide = up_act[:, lo:hi].astype(jnp.float32)
            sigmoid_gate = jax.nn.sigmoid(gate_wide)
            wide[f] = gate_wide, up_wide, sigmoid_gate
            hidden[f] = (gate_wide * sigmoid_gate * up_wide).astype(jnp.bfloat16)

        gate_parts, up_parts, grad_parts, out_sums = {}, {}, {}, {}
        ready = []

        def gathered(f, above, below):
            slots = [hidden[f]]
            for e in range(1, n_far):
                slots.append(jnp.where(far + e < n_far, above[e], below[n_far - e]))
            hidden_rows = jnp.concatenate(slots, axis=0)
            out_sums[f] = jnp.dot(hidden_rows, weights[f], preferred_element_type=jnp.float32)
            grad = lax.dot_general(
                hidden_rows, cot_rows, (((0,), (0,)), ((), ())), preferred_element_type=jnp.float32
            )
            theirs = swap(grad[:, 2 * width :].astype(jnp.bfloat16), 1)
            ready.append(theirs)
            grad = grad[:, : 2 * width] + theirs.astype(jnp.float32)
            theirs = swap(after(grad[:, width:].astype(jnp.bfloat16), *last), 2)
            last[:] = [theirs]
            grad_parts[f] = grad[:, :width] + theirs.astype(jnp.float32)

        def reduced(f, hidden_grad):
            gate_wide, up_wide, sigmoid_gate = wide[f]
            up_parts[f] = (hidden_grad * gate_wide * sigmoid_gate).astype(jnp.bfloat16)
            gate_parts[f] = (
                hidden_grad * up_wide * sigmoid_gate * (1.0 + gate_wide * (1.0 - sigmoid_gate))
            ).astype(jnp.bfloat16)

        history = []

        def both_ways(up, down, sources, *awaited):
            if len(history) > 2:
                awaited += history[-3]
            if awaited:
                up, down = lax.optimization_barrier((up, down) + awaited)[:2]
            downs = [n_far - 1 - z for z in sources]
            history.append((hop(up, 1, sources), hop(down, -1, downs)))
            return history[-1]

        def gather_rounds(f):
            above, below = {}, {}
            up = down = hidden[f]
            for j in range(1, n_far):
                up, down = both_ways(
                    up, down, range(j - 1, n_far - 1), *([cot_rows] if j == n_far - 1 else [])
                )
                below[j], above[j] = up, down
                if j == n_far - 1:
                    gathered(f, above, below)
                yield

        def reduce_rounds(f):
            terms = lax.dot_general(
                cot_rows, weights[f], (((1,), (1,)), ((), ())), preferred_element_type=jnp.float32
            )
            slots = [terms[e * tokens : (e + 1) * tokens] for e in range(n_far)]
            up = down = None
            for d in range(n_far - 1, 0, -1):
                up_term, down_term = slots[d], slots[n_far - d]
                if up is not None:
                    up_term = up_term + up.astype(jnp.float32)
                    down_term = down_term + down.astype(jnp.float32)
                up, down = both_ways(
                    up_term.astype(jnp.bfloat16),
                    down_term.astype(jnp.bfloat16),
                    range(0, n_far - d),
                    *(ready[f : f + 1] if d == 1 else []),
                )
                if d == 1:
                    reduced(f, slots[0] + up.astype(jnp.float32) + down.astype(jnp.float32))
                yield

        gathers = [gather_rounds(f) for f in range(n_chunks)]
        reduces = [reduce_rounds(f) for f in range(n_chunks)]
        gather_order = [gathers[f] for j in range(1, n_far) for f in range(n_chunks)]
        reduce_order = [reduces[f] for j in range(1, n_far) for f in range(n_chunks)]
        lag = len(gather_order) - n_chunks + 1
        order = gather_order[:lag]
        for i, rounds in enumerate(reduce_order):
            order += [rounds] + gather_order[lag + i : lag + i + 1]
        for rounds in order:
            next(rounds)

        out_terms = sum(out_sums[f] for f in range(n_chunks)).astype(jnp.bfloat16)
        slots = [out_terms[:tokens]]
        for e in range(1, n_far):
            slots.append(shift(out_terms[e * tokens : (e + 1) * tokens], e))
        back = [slots[0]] + slots[:0:-1]
        twice = jnp.concatenate(back + back[:-1], axis=1)
        columns = QUAD * width
        mine = lax.dynamic_slice_in_dim(
            twice, ((n_far - far) % n_far) * columns, n_far * columns, axis=1
        )
        mine = mine.reshape(tokens, n_far, QUAD, width)
        mine = jnp.concatenate(
            [lax.dynamic_slice_in_dim(mine, slot, 1, axis=2) for slot in slot_of(near)], axis=2
        )
        mine = mine.reshape(tokens, n_local, half)

        def half_of(step):
            return lax.dynamic_index_in_dim(mine, (x + step) % n_local, axis=1, keepdims=False)

        output = half_of(0).astype(jnp.float32)
        for step in range(1, n_local):
            output = output + local_shift(half_of(step), step).astype(jnp.float32)
        chunks = range(n_chunks)
        return (
            output.astype(jnp.bfloat16),
            jnp.concatenate([gate_parts[f] for f in chunks], axis=1),
            jnp.concatenate([up_parts[f] for f in chunks], axis=1),
            jnp.concatenate([grad_parts[f] for f in chunks], axis=0),
        )

    specs = (P("hst", "local"), P("hst", "local"), P("hst", "local"), P("local", "hst"))
    return jax.shard_map(
        on_device, mesh=mesh, in_specs=specs, out_specs=specs, check_vma=False
    )
```

time: 341 us -> 313 us (0.918); the launches traced: 335 us -> 312 us
  starting transfers between devices: 144 us -> 96.5 us
  waiting for transfers between devices: 76.5 us -> 112 us
  local copies, waits for them, and re-layouts: 35.3 us -> 21.8 us
  other arithmetic: 43.2 us -> 48 us
    ppermute x40 -> x24, starting transfers between devices: 120 us -> 73.6 us  [hop(): return lax.ppermute(value, 'hst', pairs)]
    ppermute x40 -> x24, waiting for transfers between devices: 33 us -> 67.1 us  [hop(): return lax.ppermute(value, 'hst', pairs)]
    ppermute x16 -> x8, waiting for transfers between devices: 32.9 us -> 0.02 us  [swap(): return lax.ppermute(value, 'hst', [(h, h ^ bit) for h in range(n_hst)])]
    ppermute x6, waiting for transfers between devices: 10.6 us -> 42.3 us  [shift(): return lax.ppermute(value, 'hst', pairs)]
    unnamed x109 -> x87, local copies, waits for them, and re-layouts: 14.7 us -> 7.15 us
    ppermute x16 -> x8, starting transfers between devices: 11.2 us -> 6.14 us  [swap(): return lax.ppermute(value, 'hst', [(h, h ^ bit) for h in range(n_hst)])]
    add x4 -> x2, other arithmetic: 4.3 us -> 8.27 us  [gathered(): grad = grad[:, :2 * width] + theirs.astype(jnp.float32)]
    slice x8 -> x4, local copies, waits for them, and re-layouts: 7.64 us -> 4.3 us  [the longest x2 2.89 us: on_device(): weight = after(down_weight[lo:hi], *last)]
  transfers between devices with their start and end apart: 64 -> 40, of which waited for: 17 -> 17; matrix products, arithmetic and copies ran while one was open for 30% -> 31% of each run, Pallas kernels for 0% -> 0%
where the time goes in v4:
time: 313 us; the launch traced here: 312 us
  waiting for transfers between devices  112 us (36%)
  starting transfers between devices  96.5 us (31%)
  other arithmetic  48 us (15%)
  matrix products  31.5 us (10%)
  local copies, waits for them, and re-layouts  21.8 us (7%)
    ppermute x24, starting transfers between devices, hop(): return lax.ppermute(value, 'hst', pairs)  73.6 us
    ppermute x24, waiting for transfers between devices, hop(): return lax.ppermute(value, 'hst', pairs)  67.1 us
    ppermute x6, waiting for transfers between devices, shift(): return lax.ppermute(value, 'hst', pairs)  42.3 us
    ppermute x6, starting transfers between devices, shift(): return lax.ppermute(value, 'hst', pairs)  13.6 us
    dot_general x2, matrix products, gathered(): jnp.dot(hidden_rows, weights[f], preferred_element_type=jnp.float32)  12.1 us
    dot_general x2, matrix products, reduce_rounds(): lax.dot_general(cot_rows, weights[f], (((1,), (1,)), ((), ())), preferred...  10.1 us
    dot_general x2, matrix products, gathered(): lax.dot_general(hidden_rows, cot_rows, (((0,), (0,)), ((), ())), preferre...  9.31 us
    convert_element_type x4, other arithmetic, reduce_rounds(): down_term.astype(jnp.bfloat16)  8.38 us
  transfers between devices with their start and end apart: 40, of which 17 were waited for; matrix products, arithmetic and copies ran while one was open for 31% of the time, Pallas kernels for 0%

profile of v4, /device:TPU:8, one launch (start us, length us, event | category | flops | bytes accessed | tf_op | source)
XLA Modules:
  0.0 311.6 jit_solution(6603359071488264789)
XLA Ops:
  0.7 2.7 fusion.13
  5.3 3.9 %collective-permute-start.8 = (bf16[128,2688]{1,0:T(8,128)(2,1)}, bf16[128,2688]{1,0:T(8,128)(2,1)}, u32[]{:S(2)}, u32[]{:S(2)}) collective-permute-start(bf16[128,2688]{1,0:T(8,128)(2,1)} %fusion.13), channel_id=1, source_target_pairs={{0,8},{2,10},{4,12},{6,14},{8,16},{10,18},{12,20},{14,22},{16,24},... | collective-permute-start | bytes 2064392 | tf_op jit(solution)/shard_map/ppermute | solution.py:36
  13.4 4.3 %collective-permute-start.1 = (bf16[128,2816]{1,0:T(8,128)(2,1)}, bf16[128,2816]{1,0:T(8,128)(2,1)S(1)}, u32[]{:S(2)}, u32[]{:S(2)}) collective-permute-start(bf16[128,2816]{1,0:T(8,128)(2,1)} %fusion.2), channel_id=1, source_target_pairs={{0,8},{2,10},{4,12},{6,14},{8,16},{10,18},{12,20},{14,22},{16,24},... | collective-permute-start | bytes 2162696 | tf_op jit(solution)/shard_map/ppermute | solution.py:36
  21.3 2.5 collective-permute-done.4
  25.4 4.2 %fusion.25 = bf16[128,4096]{0,1:T(8,128)(2,1)S(1)} fusion(s32[]{:T(128)S(6)} %select_n.136, bf16[128,2048]{0,1:T(8,128)(2,1)S(1)} %copy.10, bf16[128,2048]{0,1:T(8,128)(2,1)} %collective-permute-done.4), kind=kLoop, calls=%fused_computation.71 | loop fusion | flops 3145728 | bytes 2097156 | tf_op jit(solution)/shard_map/concatenate | solution.py:56
  29.8 10.2 %collective-permute-done.1 = bf16[128,2816]{1,0:T(8,128)(2,1)S(1)} collective-permute-done((bf16[128,2816]{1,0:T(8,128)(2,1)}, bf16[128,2816]{1,0:T(8,128)(2,1)S(1)}, u32[]{:S(2)}, u32[]{:S(2)}) %collective-permute-start.1) | collective-permute-done | bytes 720928 | tf_op jit(solution)/shard_map/ppermute | solution.py:36
  40.1 4.5 %collective-permute-start.14 = (bf16[128,2688]{1,0:T(8,128)(2,1)}, bf16[128,2688]{1,0:T(8,128)(2,1)}, u32[]{:S(2)}, u32[]{:S(2)}) collective-permute-start(bf16[128,2688]{1,0:T(8,128)(2,1)} %collective-permute-done.8), channel_id=1, source_target_pairs={{8,16},{10,18},{12,20},{14,22},{16,24},{18,26},{20,28},{22,30},{9,... | collective-permute-start | bytes 2064392 | tf_op jit(solution)/shard_map/ppermute | solution.py:36
  46.8 2.9 collective-permute-start.7
  50.7 18.0 %collective-permute-done.7 = bf16[128,1024]{1,0:T(8,128)(2,1)S(1)} collective-permute-done((bf16[128,1024]{1,0:T(8,128)(2,1)S(1)}, bf16[128,1024]{1,0:T(8,128)(2,1)S(1)}, u32[]{:S(2)}, u32[]{:S(2)}) %collective-permute-start.7) | collective-permute-done | bytes 262176 | tf_op jit(solution)/shard_map/ppermute | solution.py:32
  68.7 4.3 %collective-permute-start.6 = (bf16[128,1024]{1,0:T(8,128)(2,1)S(1)}, bf16[128,1024]{1,0:T(8,128)(2,1)}, u32[]{:S(2)}, u32[]{:S(2)}) collective-permute-start(bf16[128,1024]{1,0:T(8,128)(2,1)S(1)} %bitcast.28), channel_id=1, source_target_pairs={{0,16},{2,18},{4,20},{6,22},{8,24},{10,26},{12,28},{14,30},{16,0},... | collective-permute-start | bytes 786440 | tf_op jit(solution)/shard_map/ppermute | solution.py:32
  75.4 2.8 collective-permute-done.5
  81.7 5.3 %collective-permute-start.3 = (bf16[128,2816]{1,0:T(8,128)(2,1)}, bf16[128,2816]{1,0:T(8,128)(2,1)S(1)}, u32[]{:S(2)}, u32[]{:S(2)}) collective-permute-start(bf16[128,2816]{1,0:T(8,128)(2,1)} %collective-permute-done), channel_id=1, source_target_pairs={{16,8},{18,10},{20,12},{22,14},{8,0},{10,2},{12,4},{14,6},{17,9},{... | collective-permute-start | bytes 2162696 | tf_op jit(solution)/shard_map/ppermute | solution.py:36
  93.1 3.7 %collective-permute-done.2 = bf16[128,2816]{1,0:T(8,128)(2,1)S(1)} collective-permute-done((bf16[128,2816]{1,0:T(8,128)(2,1)}, bf16[128,2816]{1,0:T(8,128)(2,1)S(1)}, u32[]{:S(2)}, u32[]{:S(2)}) %collective-permute-start.2) | collective-permute-done | bytes 720928 | tf_op jit(solution)/shard_map/ppermute | solution.py:36
  96.8 7.0 %collective-permute-done.3 = bf16[128,2816]{1,0:T(8,128)(2,1)S(1)} collective-permute-done((bf16[128,2816]{1,0:T(8,128)(2,1)}, bf16[128,2816]{1,0:T(8,128)(2,1)S(1)}, u32[]{:S(2)}, u32[]{:S(2)}) %collective-permute-start.3) | collective-permute-done | bytes 720928 | tf_op jit(solution)/shard_map/ppermute | solution.py:36
  104.6 4.5 %collective-permute-start.11 = (bf16[128,2816]{1,0:T(8,128)(2,1)S(1)}, bf16[128,2816]{1,0:T(8,128)(2,1)S(1)}, u32[]{:S(2)}, u32[]{:S(2)}) collective-permute-start(bf16[128,2816]{1,0:T(8,128)(2,1)S(1)} %collective-permute-done.3), channel_id=1, source_target_pairs={{8,0},{10,2},{12,4},{14,6},{9,1},{11,3},{13,5},{15,7}} | collective-permute-start | bytes 2162696 | tf_op jit(solution)/shard_map/ppermute | solution.py:36
  112.1 6.5 %collective-permute-done.17 = bf16[128,2688]{1,0:T(8,128)(2,1)S(1)} collective-permute-done((bf16[128,2688]{1,0:T(8,128)(2,1)}, bf16[128,2688]{1,0:T(8,128)(2,1)S(1)}, u32[]{:S(2)}, u32[]{:S(2)}) %collective-permute-start.17) | collective-permute-done | bytes 688160 | tf_op jit(solution)/shard_map/ppermute | solution.py:36
  119.9 4.6 %fusion.28 = f32[2688,1024]{1,0:T(8,128)S(1)} fusion(bf16[128,2688]{1,0:T(8,128)(2,1)S(1)} %broadcast_select_fusion.3, bf16[128,2688]{1,0:T(8,128)(2,1)S(1)} %broadcast_select_fusion.4, bf16[128,2688]{1,0:T(8,128)(2,1)S(1)} %broadcast_select_fusion.5, bf16[128,2688]{1,0:T(8,128)(2,1)} %fusion.13, bf16[128,1024]{1,0:T(8,128)(2,1)S(1)} %copy-done.29, ...), kind=kOutput, calls=%fused_computation.85 | convolution fusion | flops 2833776640 | bytes 14811136 | tf_op jit(solution)/shard_map/dot_general | solution.py:102
  125.0 2.2 broadcast_select_fusion.2
  127.2 5.8 %collective-permute-done.11 = bf16[128,2816]{1,0:T(8,128)(2,1)S(1)} collective-permute-done((bf16[128,2816]{1,0:T(8,128)(2,1)S(1)}, bf16[128,2816]{1,0:T(8,128)(2,1)S(1)}, u32[]{:S(2)}, u32[]{:S(2)}) %collective-permute-start.11) | collective-permute-done | bytes 720928 | tf_op jit(solution)/shard_map/ppermute | solution.py:36
  133.1 4.8 %fusion.27 = f32[2816,1024]{1,0:T(8,128)S(1)} fusion(bf16[128,2816]{1,0:T(8,128)(2,1)S(1)} %broadcast_select_fusion, bf16[128,2816]{1,0:T(8,128)(2,1)S(1)} %broadcast_select_fusion.1, bf16[128,2816]{1,0:T(8,128)(2,1)S(1)} %broadcast_select_fusion.2, bf16[128,2816]{1,0:T(8,128)(2,1)} %fusion.2, bf16[128,1024]{1,0:T(8,128)(2,1)S(1)} %copy-done.29, ...), kind=kOutput, calls=%fused_computation.84 | convolution fusion | flops 2968518656 | bytes 15466496 | tf_op jit(solution)/shard_map/dot_general | solution.py:102
  137.9 2.4 slice.174
  140.3 2.4 pad_maximum_fusion.5
  144.5 5.7 %fusion = f32[512,2816]{1,0:T(8,128)S(1)} fusion(bf16[2816,512]{1,0:T(8,128)(2,1)S(1)} %collective-permute-done.13, bf16[2816,256]{1,0:T(8,128)(2,1)} %collective-permute-done.12, bf16[2816,256]{1,0:T(8,128)(2,1)S(1)} %slice.86, bf16[128,1024]{1,0:T(8,128)(2,1)S(1)} %copy-done.29, bf16[128,1024]{1,0:T(8,128)(2,1)} %collective-permute-done.6, ...), kind=kOutput, calls=%fused_computation.22 | convolution fusion | flops 2974285824 | bytes 12582912 | tf_op jit(solution)/shard_map/dot_general | solution.py:143
  152.9 5.3 %slice_add_fusion.1 = f32[2688,512]{1,0:T(8,128)S(1)} fusion(f32[2688,1024]{1,0:T(8,128)} %copy-done.5, bf16[2688,512]{1,0:T(8,128)(2,1)} %collective-permute-done.35), kind=kLoop, calls=%fused_computation.4 | loop fusion | flops 2752512 | bytes 13762560 | tf_op jit(solution)/shard_map/add | solution.py:107
  159.6 11.1 %collective-permute-done.24 = bf16[128,2816]{1,0:T(8,128)(2,1)S(1)} collective-permute-done((bf16[128,2816]{1,0:T(8,128)(2,1)S(1)}, bf16[128,2816]{1,0:T(8,128)(2,1)S(1)}, u32[]{:S(2)}, u32[]{:S(2)}) %collective-permute-start.24) | collective-permute-done | bytes 720928 | tf_op jit(solution)/shard_map/ppermute | solution.py:36
  175.6 3.0 slice_add_fusion
  181.6 3.5 %constant_dynamic-update-slice_fusion = bf16[2688,1024]{1,0:T(8,128)(2,1)} fusion(bf16[2688,1024]{1,0:T(8,128)(2,1)} %constant_dynamic-update-slice_fusion.1, bf16[2688,512]{1,0:T(8,128)(2,1)} %collective-permute-done.19), kind=kLoop, calls=%fused_computation.89 | loop fusion | bytes 5505024 | tf_op jit(solution)/shard_map/concatenate | solution.py:83
  185.2 7.4 %fusion.29 = f32[512,1024]{1,0:T(8,128)} fusion(bf16[2688,1024]{1,0:T(8,128)(2,1)} %constant_dynamic-update-slice_fusion, bf16[128,2688]{1,0:T(8,128)(2,1)S(1)} %copy-done.22, bf16[128,2688]{1,0:T(8,128)(2,1)S(1)} %copy-done.18, bf16[128,2688]{1,0:T(8,128)(2,1)S(1)} %copy-done.20, bf16[128,2688]{1,0:T(8,128)(2,1)} %fusion.13), kind=kOutput, calls=%fused_computation.86 | convolution fusion | flops 2829582336 | bytes 10354688 | tf_op jit(solution)/shard_map/dot_general | solution.py:101
  192.6 4.4 %fusion.35 = f32[512,2688]{1,0:T(8,128)S(1)} fusion(bf16[2688,1024]{1,0:T(8,128)(2,1)S(1)} %copy-done.23, bf16[128,1024]{1,0:T(8,128)(2,1)S(1)} %copy-done.30, bf16[128,1024]{1,0:T(8,128)(2,1)} %collective-permute-done.6, bf16[128,1024]{1,0:T(8,128)(2,1)} %collective-permute-done.5, bf16[128,1024]{1,0:T(8,128)(2,1)S(1)} %bitcast.27), kind=kOutput, calls=%fused_computation.115 | convolution fusion | flops 2822766592 | bytes 12058624 | tf_op jit(solution)/shard_map/dot_general | solution.py:143
  199.8 4.7 %add_convert_fusion = bf16[512,1024]{1,0:T(8,128)(2,1)S(1)} fusion(f32[512,1024]{1,0:T(8,128)S(1)} %copy-done.31, bf16[2816,512]{1,0:T(8,128)(2,1)S(1)} %copy-done.27, bf16[2816,256]{1,0:T(8,128)(2,1)} %collective-permute-done.12, bf16[2816,256]{1,0:T(8,128)(2,1)S(1)} %slice.86, bf16[128,2816]{1,0:T(8,128)(2,1)S(1)} %copy-done.16, ...), kind=kOutput, calls=%fused_computation.24 | convolution fusion | flops 2982674432 | bytes 11796480 | tf_op jit(solution)/shard_map/dot_general | solution.py:101
  204.6 3.0 collective-permute-start.22
  207.6 3.3 %collective-permute-start.21 = (bf16[128,1024]{1,0:T(8,128)(2,1)S(1)}, bf16[128,1024]{1,0:T(8,128)(2,1)S(1)}, u32[]{:S(2)}, u32[]{:S(2)}) collective-permute-start(bf16[128,1024]{1,0:T(8,128)(2,1)S(1)} %get-tuple-element.76), channel_id=1, source_target_pairs={{0,16},{2,18},{4,20},{6,22},{8,24},{10,26},{12,28},{14,30},{16,0},... | collective-permute-start | bytes 786440 | tf_op jit(solution)/shard_map/ppermute | solution.py:32
  212.5 19.4 %collective-permute-done.20 = bf16[128,1024]{1,0:T(8,128)(2,1)S(1)} collective-permute-done((bf16[128,1024]{1,0:T(8,128)(2,1)S(1)}, bf16[128,1024]{1,0:T(8,128)(2,1)S(1)}, u32[]{:S(2)}, u32[]{:S(2)}) %collective-permute-start.20) | collective-permute-done | bytes 262176 | tf_op jit(solution)/shard_map/ppermute | solution.py:32
  236.2 3.0 add_convert_fusion.7
  239.3 18.2 %collective-permute-start.33 = (bf16[128,2688]{1,0:T(8,128)(2,1)}, bf16[128,2688]{1,0:T(8,128)(2,1)}, u32[]{:S(2)}, u32[]{:S(2)}) collective-permute-start(bf16[128,2688]{1,0:T(8,128)(2,1)} %get-tuple-element.40), channel_id=1, source_target_pairs={{0,8},{2,10},{4,12},{6,14},{8,16},{10,18},{12,20},{14,22},{1,9},{3... | collective-permute-start | bytes 2064392 | tf_op jit(solution)/shard_map/ppermute | solution.py:36
  258.8 4.6 %collective-permute-start.31 = (bf16[128,2816]{1,0:T(8,128)(2,1)S(1)}, bf16[128,2816]{1,0:T(8,128)(2,1)}, u32[]{:S(2)}, u32[]{:S(2)}) collective-permute-start(bf16[128,2816]{1,0:T(8,128)(2,1)S(1)} %get-tuple-element.38), channel_id=1, source_target_pairs={{0,8},{2,10},{4,12},{6,14},{8,16},{10,18},{12,20},{14,22},{16,24},... | collective-permute-start | bytes 2162696 | tf_op jit(solution)/shard_map/ppermute | solution.py:36
  267.7 2.5 slice_add_fusion.2
  270.2 3.4 %collective-permute-done.33 = bf16[128,2688]{1,0:T(8,128)(2,1)} collective-permute-done((bf16[128,2688]{1,0:T(8,128)(2,1)}, bf16[128,2688]{1,0:T(8,128)(2,1)}, u32[]{:S(2)}, u32[]{:S(2)}) %collective-permute-start.33) | collective-permute-done | bytes 688160 | tf_op jit(solution)/shard_map/ppermute | solution.py:36
  273.7 4.4 %collective-permute-done.34 = bf16[128,2688]{1,0:T(8,128)(2,1)} collective-permute-done((bf16[128,2688]{1,0:T(8,128)(2,1)}, bf16[128,2688]{1,0:T(8,128)(2,1)}, u32[]{:S(2)}, u32[]{:S(2)}) %collective-permute-start.34) | collective-permute-done | bytes 688160 | tf_op jit(solution)/shard_map/ppermute | solution.py:36
  278.1 2.4 add_convert_fusion.5
  282.4 4.2 %collective-permute-start.37 = (bf16[128,2688]{1,0:T(8,128)(2,1)S(1)}, bf16[128,2688]{1,0:T(8,128)(2,1)S(1)}, u32[]{:S(2)}, u32[]{:S(2)}) collective-permute-start(bf16[128,2688]{1,0:T(8,128)(2,1)S(1)} %get-tuple-element.43), channel_id=1, source_target_pairs={{24,16},{26,18},{28,20},{30,22},{16,8},{18,10},{20,12},{22,14},{8,... | collective-permute-start | bytes 2064392 | tf_op jit(solution)/shard_map/ppermute | solution.py:36
  286.6 2.4 collective-permute-done.31
  289.0 4.5 %collective-permute-done.32 = bf16[128,2816]{1,0:T(8,128)(2,1)} collective-permute-done((bf16[128,2816]{1,0:T(8,128)(2,1)S(1)}, bf16[128,2816]{1,0:T(8,128)(2,1)}, u32[]{:S(2)}, u32[]{:S(2)}) %collective-permute-start.32) | collective-permute-done | bytes 720928 | tf_op jit(solution)/shard_map/ppermute | solution.py:36
  293.5 2.9 fusion.11
  296.4 3.8 %collective-permute-done.36 = bf16[128,2688]{1,0:T(8,128)(2,1)S(1)} collective-permute-done((bf16[128,2688]{1,0:T(8,128)(2,1)S(1)}, bf16[128,2688]{1,0:T(8,128)(2,1)S(1)}, u32[]{:S(2)}, u32[]{:S(2)}) %collective-permute-start.36) | collective-permute-done | bytes 688160 | tf_op jit(solution)/shard_map/ppermute | solution.py:36
  300.2 4.1 %collective-permute-done.37 = bf16[128,2688]{1,0:T(8,128)(2,1)S(1)} collective-permute-done((bf16[128,2688]{1,0:T(8,128)(2,1)S(1)}, bf16[128,2688]{1,0:T(8,128)(2,1)S(1)}, u32[]{:S(2)}, u32[]{:S(2)}) %collective-permute-start.37) | collective-permute-done | bytes 688160 | tf_op jit(solution)/shard_map/ppermute | solution.py:36
  304.3 2.2 fusion.22
  308.7 2.9 pad_maximum_fusion.1
  (170 shorter events, 63.6 us)
Async XLA Ops:
  3.4 26.4 %collective-permute-start.9 = (bf16[128,2688]{1,0:T(8,128)(2,1)}, bf16[128,2688]{1,0:T(8,128)(2,1)}, u32[]{:S(2)}, u32[]{:S(2)}) collective-permute-start(bf16[128,2688]{1,0:T(8,128)(2,1)} %fusion.13), channel_id=1, source_target_pairs={{24,16},{26,18},{28,20},{30,22},{16,8},{18,10},{20,12},{22,14},{8,... | collective-permute-start | bytes 2064392 | tf_op jit(solution)/shard_map/ppermute | solution.py:36
  5.3 24.5 %collective-permute-start.8 = (bf16[128,2688]{1,0:T(8,128)(2,1)}, bf16[128,2688]{1,0:T(8,128)(2,1)}, u32[]{:S(2)}, u32[]{:S(2)}) collective-permute-start(bf16[128,2688]{1,0:T(8,128)(2,1)} %fusion.13), channel_id=1, source_target_pairs={{0,8},{2,10},{4,12},{6,14},{8,16},{10,18},{12,20},{14,22},{16,24},... | collective-permute-start | bytes 2064392 | tf_op jit(solution)/shard_map/ppermute | solution.py:36
  10.6 13.3 %collective-permute-start.4 = (bf16[128,2048]{0,1:T(8,128)(2,1)S(1)}, bf16[128,2048]{0,1:T(8,128)(2,1)}, u32[]{:S(2)}, u32[]{:S(2)}) collective-permute-start(bf16[128,2048]{0,1:T(8,128)(2,1)S(1)} %copy.10), channel_id=1, source_target_pairs={{0,1},{1,0},{2,3},{3,2},{4,5},{5,4},{6,7},{7,6},{8,9},{9,8},{10,11... | collective-permute-start | bytes 1572872 | tf_op jit(solution)/shard_map/ppermute | solution.py:39
  13.4 26.6 %collective-permute-start.1 = (bf16[128,2816]{1,0:T(8,128)(2,1)}, bf16[128,2816]{1,0:T(8,128)(2,1)S(1)}, u32[]{:S(2)}, u32[]{:S(2)}) collective-permute-start(bf16[128,2816]{1,0:T(8,128)(2,1)} %fusion.2), channel_id=1, source_target_pairs={{0,8},{2,10},{4,12},{6,14},{8,16},{10,18},{12,20},{14,22},{16,24},... | collective-permute-start | bytes 2162696 | tf_op jit(solution)/shard_map/ppermute | solution.py:36
  17.7 22.3 %collective-permute-start = (bf16[128,2816]{1,0:T(8,128)(2,1)}, bf16[128,2816]{1,0:T(8,128)(2,1)}, u32[]{:S(2)}, u32[]{:S(2)}) collective-permute-start(bf16[128,2816]{1,0:T(8,128)(2,1)} %fusion.2), channel_id=1, source_target_pairs={{24,16},{26,18},{28,20},{30,22},{16,8},{18,10},{20,12},{22,14},{8,... | collective-permute-start | bytes 2162696 | tf_op jit(solution)/shard_map/ppermute | solution.py:36
  23.8 66.5 %collective-permute-start.12 = (bf16[2816,256]{1,0:T(8,128)(2,1)S(1)}, bf16[2816,256]{1,0:T(8,128)(2,1)}, u32[]{:S(2)}, u32[]{:S(2)}) collective-permute-start(bf16[2816,256]{1,0:T(8,128)(2,1)S(1)} %slice.86), channel_id=1, source_target_pairs={{0,4},{2,6},{4,0},{6,2},{8,12},{10,14},{12,8},{14,10},{16,20},{18,... | collective-permute-start | bytes 4325384 | tf_op jit(solution)/shard_map/ppermute | solution.py:28
  40.1 47.0 %collective-permute-start.14 = (bf16[128,2688]{1,0:T(8,128)(2,1)}, bf16[128,2688]{1,0:T(8,128)(2,1)}, u32[]{:S(2)}, u32[]{:S(2)}) collective-permute-start(bf16[128,2688]{1,0:T(8,128)(2,1)} %collective-permute-done.8), channel_id=1, source_target_pairs={{8,16},{10,18},{12,20},{14,22},{16,24},{18,26},{20,28},{22,30},{9,... | collective-permute-start | bytes 2064392 | tf_op jit(solution)/shard_map/ppermute | solution.py:36
  44.6 42.5 %collective-permute-start.15 = (bf16[128,2688]{1,0:T(8,128)(2,1)}, bf16[128,2688]{1,0:T(8,128)(2,1)}, u32[]{:S(2)}, u32[]{:S(2)}) collective-permute-start(bf16[128,2688]{1,0:T(8,128)(2,1)} %collective-permute-done.9), channel_id=1, source_target_pairs={{16,8},{18,10},{20,12},{22,14},{8,0},{10,2},{12,4},{14,6},{17,9},{... | collective-permute-start | bytes 2064392 | tf_op jit(solution)/shard_map/ppermute | solution.py:36
  46.8 22.0 %collective-permute-start.7 = (bf16[128,1024]{1,0:T(8,128)(2,1)S(1)}, bf16[128,1024]{1,0:T(8,128)(2,1)S(1)}, u32[]{:S(2)}, u32[]{:S(2)}) collective-permute-start(bf16[128,1024]{1,0:T(8,128)(2,1)S(1)} %bitcast.29), channel_id=1, source_target_pairs={{0,8},{2,10},{4,12},{6,14},{8,16},{10,18},{12,20},{14,22},{16,24},... | collective-permute-start | bytes 786440 | tf_op jit(solution)/shard_map/ppermute | solution.py:32
  50.7 27.5 %collective-permute-start.5 = (bf16[128,1024]{1,0:T(8,128)(2,1)}, bf16[128,1024]{1,0:T(8,128)(2,1)}, u32[]{:S(2)}, u32[]{:S(2)}) collective-permute-start(bf16[128,1024]{1,0:T(8,128)(2,1)} %bitcast.3), channel_id=1, source_target_pairs={{0,24},{2,26},{4,28},{6,30},{8,0},{10,2},{12,4},{14,6},{16,8},{18,... | collective-permute-start | bytes 786440 | tf_op jit(solution)/shard_map/ppermute | solution.py:32
  68.7 13.0 %collective-permute-start.6 = (bf16[128,1024]{1,0:T(8,128)(2,1)S(1)}, bf16[128,1024]{1,0:T(8,128)(2,1)}, u32[]{:S(2)}, u32[]{:S(2)}) collective-permute-start(bf16[128,1024]{1,0:T(8,128)(2,1)S(1)} %bitcast.28), channel_id=1, source_target_pairs={{0,16},{2,18},{4,20},{6,22},{8,24},{10,26},{12,28},{14,30},{16,0},... | collective-permute-start | bytes 786440 | tf_op jit(solution)/shard_map/ppermute | solution.py:32
  78.2 18.7 %collective-permute-start.2 = (bf16[128,2816]{1,0:T(8,128)(2,1)}, bf16[128,2816]{1,0:T(8,128)(2,1)S(1)}, u32[]{:S(2)}, u32[]{:S(2)}) collective-permute-start(bf16[128,2816]{1,0:T(8,128)(2,1)} %copy-done.11), channel_id=1, source_target_pairs={{8,16},{10,18},{12,20},{14,22},{16,24},{18,26},{20,28},{22,30},{9,... | collective-permute-start | bytes 2162696 | tf_op jit(solution)/shard_map/ppermute | solution.py:36
  81.7 22.2 %collective-permute-start.3 = (bf16[128,2816]{1,0:T(8,128)(2,1)}, bf16[128,2816]{1,0:T(8,128)(2,1)S(1)}, u32[]{:S(2)}, u32[]{:S(2)}) collective-permute-start(bf16[128,2816]{1,0:T(8,128)(2,1)} %collective-permute-done), channel_id=1, source_target_pairs={{16,8},{18,10},{20,12},{22,14},{8,0},{10,2},{12,4},{14,6},{17,9},{... | collective-permute-start | bytes 2162696 | tf_op jit(solution)/shard_map/ppermute | solution.py:36
  87.1 23.7 %collective-permute-start.16 = (bf16[128,2688]{1,0:T(8,128)(2,1)}, bf16[128,2688]{1,0:T(8,128)(2,1)S(1)}, u32[]{:S(2)}, u32[]{:S(2)}) collective-permute-start(bf16[128,2688]{1,0:T(8,128)(2,1)} %collective-permute-done.14), channel_id=1, source_target_pairs={{16,24},{18,26},{20,28},{22,30},{17,25},{19,27},{21,29},{23,31}} | collective-permute-start | bytes 2064392 | tf_op jit(solution)/shard_map/ppermute | solution.py:36
  87.8 30.8 %collective-permute-start.17 = (bf16[128,2688]{1,0:T(8,128)(2,1)}, bf16[128,2688]{1,0:T(8,128)(2,1)S(1)}, u32[]{:S(2)}, u32[]{:S(2)}) collective-permute-start(bf16[128,2688]{1,0:T(8,128)(2,1)} %collective-permute-done.15), channel_id=1, source_target_pairs={{8,0},{10,2},{12,4},{14,6},{9,1},{11,3},{13,5},{15,7}} | collective-permute-start | bytes 2064392 | tf_op jit(solution)/shard_map/ppermute | solution.py:36
  90.3 29.5 %copy-start.17 = (bf16[128,2688]{1,0:T(8,128)(2,1)}, bf16[128,2688]{1,0:T(8,128)(2,1)S(1)}, u32[]{:S(2)}) copy-start(bf16[128,2688]{1,0:T(8,128)(2,1)S(1)} %broadcast_select_fusion.4) | copy-start | bytes 2064388
  90.4 49.9 %collective-permute-start.18 = (bf16[2688,256]{1,0:T(8,128)(2,1)S(1)}, bf16[2688,256]{1,0:T(8,128)(2,1)S(1)}, u32[]{:S(2)}, u32[]{:S(2)}) collective-permute-start(bf16[2688,256]{1,0:T(8,128)(2,1)S(1)} %slice.87), channel_id=1, source_target_pairs={{0,4},{2,6},{4,0},{6,2},{8,12},{10,14},{12,8},{14,10},{16,20},{18,... | collective-permute-start | bytes 4128776 | tf_op jit(solution)/shard_map/ppermute | solution.py:28
  103.9 21.1 %collective-permute-start.10 = (bf16[128,2816]{1,0:T(8,128)(2,1)S(1)}, bf16[128,2816]{1,0:T(8,128)(2,1)S(1)}, u32[]{:S(2)}, u32[]{:S(2)}) collective-permute-start(bf16[128,2816]{1,0:T(8,128)(2,1)S(1)} %collective-permute-done.2), channel_id=1, source_target_pairs={{16,24},{18,26},{20,28},{22,30},{17,25},{19,27},{21,29},{23,31}} | collective-permute-start | bytes 2162696 | tf_op jit(solution)/shard_map/ppermute | solution.py:36
  104.6 28.4 %collective-permute-start.11 = (bf16[128,2816]{1,0:T(8,128)(2,1)S(1)}, bf16[128,2816]{1,0:T(8,128)(2,1)S(1)}, u32[]{:S(2)}, u32[]{:S(2)}) collective-permute-start(bf16[128,2816]{1,0:T(8,128)(2,1)S(1)} %collective-permute-done.3), channel_id=1, source_target_pairs={{8,0},{10,2},{12,4},{14,6},{9,1},{11,3},{13,5},{15,7}} | collective-permute-start | bytes 2162696 | tf_op jit(solution)/shard_map/ppermute | solution.py:36
  110.8 33.7 %collective-permute-start.13 = (bf16[2816,512]{1,0:T(8,128)(2,1)S(1)}, bf16[2816,512]{1,0:T(8,128)(2,1)S(1)}, u32[]{:S(2)}, u32[]{:S(2)}) collective-permute-start(bf16[2816,512]{1,0:T(8,128)(2,1)S(1)} %pad_maximum_fusion.3), channel_id=1, source_target_pairs={{0,2},{2,0},{4,6},{6,4},{8,10},{10,8},{12,14},{14,12},{16,18},{18,... | collective-permute-start | bytes 8650760 | tf_op jit(solution)/shard_map/ppermute | solution.py:28
  124.9 28.0 %collective-permute-start.35 = (bf16[2688,512]{1,0:T(8,128)(2,1)S(1)}, bf16[2688,512]{1,0:T(8,128)(2,1)}, u32[]{:S(2)}, u32[]{:S(2)}) collective-permute-start(bf16[2688,512]{1,0:T(8,128)(2,1)S(1)} %slice.175), channel_id=1, source_target_pairs={{0,2},{2,0},{4,6},{6,4},{8,10},{10,8},{12,14},{14,12},{16,18},{18,... | collective-permute-start | bytes 8257544 | tf_op jit(solution)/shard_map/ppermute | solution.py:28
  140.3 35.3 %collective-permute-start.28 = (bf16[2816,512]{1,0:T(8,128)(2,1)}, bf16[2816,512]{1,0:T(8,128)(2,1)}, u32[]{:S(2)}, u32[]{:S(2)}) collective-permute-start(bf16[2816,512]{1,0:T(8,128)(2,1)} %slice.174), channel_id=1, source_target_pairs={{0,2},{2,0},{4,6},{6,4},{8,10},{10,8},{12,14},{14,12},{16,18},{18,... | collective-permute-start | bytes 8650760 | tf_op jit(solution)/shard_map/ppermute | solution.py:28
  142.7 38.9 %collective-permute-start.19 = (bf16[2688,512]{1,0:T(8,128)(2,1)}, bf16[2688,512]{1,0:T(8,128)(2,1)}, u32[]{:S(2)}, u32[]{:S(2)}) collective-permute-start(bf16[2688,512]{1,0:T(8,128)(2,1)} %pad_maximum_fusion.5), channel_id=1, source_target_pairs={{0,2},{2,0},{4,6},{6,4},{8,10},{10,8},{12,14},{14,12},{16,18},{18,... | collective-permute-start | bytes 8257544 | tf_op jit(solution)/shard_map/ppermute | solution.py:28
  150.3 60.7 %copy-start.2 = (f32[512,2816]{1,0:T(8,128)}, f32[512,2816]{1,0:T(8,128)S(1)}, u32[]{:S(2)}) copy-start(f32[512,2816]{1,0:T(8,128)S(1)} %fusion) | copy-start | bytes 17301508
  150.3 25.3 %slice-start.2 = ((s8[11534336]{0:T(1024)(128)(4,1)}), s8[4194304]{0:T(1024)(128)(4,1)S(1)}, s32[]{:S(2)}) async-start(s8[11534336]{0:T(1024)(128)(4,1)} %bitcast.17), calls=%async_computation.2 | async-start | bytes 8388608
  150.4 25.2 %slice-start.3 = ((s8[11534336]{0:T(1024)(128)(4,1)}), s8[4194304]{0:T(1024)(128)(4,1)S(1)}, s32[]{:S(2)}) async-start(s8[11534336]{0:T(1024)(128)(4,1)} %bitcast.17), calls=%async_computation.3 | async-start | bytes 8388608
  150.4 25.2 %slice-start.4 = ((s8[11534336]{0:T(1024)(128)(4,1)}), s8[3145728]{0:T(1024)(128)(4,1)S(1)}, s32[]{:S(2)}) async-start(s8[11534336]{0:T(1024)(128)(4,1)} %bitcast.17), calls=%async_computation.4 | async-start | bytes 6291456
  150.4 20.2 %collective-permute-start.24 = (bf16[128,2816]{1,0:T(8,128)(2,1)S(1)}, bf16[128,2816]{1,0:T(8,128)(2,1)S(1)}, u32[]{:S(2)}, u32[]{:S(2)}) collective-permute-start(bf16[128,2816]{1,0:T(8,128)(2,1)S(1)} %get-tuple-element.32), channel_id=1, source_target_pairs={{0,8},{2,10},{4,12},{6,14},{1,9},{3,11},{5,13},{7,15}} | collective-permute-start | bytes 2162696 | tf_op jit(solution)/shard_map/ppermute | solution.py:36
  152.0 18.7 %collective-permute-start.25 = (bf16[128,2816]{1,0:T(8,128)(2,1)S(1)}, bf16[128,2816]{1,0:T(8,128)(2,1)S(1)}, u32[]{:S(2)}, u32[]{:S(2)}) collective-permute-start(bf16[128,2816]{1,0:T(8,128)(2,1)S(1)} %get-tuple-element.33), channel_id=1, source_target_pairs={{24,16},{26,18},{28,20},{30,22},{25,17},{27,19},{29,21},{31,23}} | collective-permute-start | bytes 2162696 | tf_op jit(solution)/shard_map/ppermute | solution.py:36
  172.1 35.4 %collective-permute-start.26 = (bf16[128,2816]{1,0:T(8,128)(2,1)}, bf16[128,2816]{1,0:T(8,128)(2,1)}, u32[]{:S(2)}, u32[]{:S(2)}) collective-permute-start(bf16[128,2816]{1,0:T(8,128)(2,1)} %get-tuple-element.34), channel_id=1, source_target_pairs={{0,8},{2,10},{4,12},{6,14},{8,16},{10,18},{12,20},{14,22},{1,9},{3... | collective-permute-start | bytes 2162696 | tf_op jit(solution)/shard_map/ppermute | solution.py:36
  174.0 36.9 %collective-permute-start.27 = (bf16[128,2816]{1,0:T(8,128)(2,1)}, bf16[128,2816]{1,0:T(8,128)(2,1)}, u32[]{:S(2)}, u32[]{:S(2)}) collective-permute-start(bf16[128,2816]{1,0:T(8,128)(2,1)} %get-tuple-element.35), channel_id=1, source_target_pairs={{24,16},{26,18},{28,20},{30,22},{16,8},{18,10},{20,12},{22,14},{25... | collective-permute-start | bytes 2162696 | tf_op jit(solution)/shard_map/ppermute | solution.py:36
  180.1 86.6 %collective-permute-start.38 = (bf16[2816,256]{1,0:T(8,128)(2,1)}, bf16[2816,256]{1,0:T(8,128)(2,1)}, u32[]{:S(2)}, u32[]{:S(2)}) collective-permute-start(bf16[2816,256]{1,0:T(8,128)(2,1)} %slice.176), channel_id=1, source_target_pairs={{0,4},{2,6},{4,0},{6,2},{8,12},{10,14},{12,8},{14,10},{16,20},{18,... | collective-permute-start | bytes 4325384 | tf_op jit(solution)/shard_map/ppermute | solution.py:28
  198.3 37.9 %collective-permute-start.29 = (bf16[128,2688]{1,0:T(8,128)(2,1)}, bf16[128,2688]{1,0:T(8,128)(2,1)}, u32[]{:S(2)}, u32[]{:S(2)}) collective-permute-start(bf16[128,2688]{1,0:T(8,128)(2,1)} %get-tuple-element.36), channel_id=1, source_target_pairs={{0,8},{2,10},{4,12},{6,14},{1,9},{3,11},{5,13},{7,15}} | collective-permute-start | bytes 2064392 | tf_op jit(solution)/shard_map/ppermute | solution.py:36
  204.6 28.9 %collective-permute-start.22 = (bf16[128,1024]{1,0:T(8,128)(2,1)S(1)}, bf16[128,1024]{1,0:T(8,128)(2,1)S(1)}, u32[]{:S(2)}, u32[]{:S(2)}) collective-permute-start(bf16[128,1024]{1,0:T(8,128)(2,1)S(1)} %get-tuple-element.74), channel_id=1, source_target_pairs={{0,8},{2,10},{4,12},{6,14},{8,16},{10,18},{12,20},{14,22},{16,24},... | collective-permute-start | bytes 786440 | tf_op jit(solution)/shard_map/ppermute | solution.py:32
  207.6 25.9 %collective-permute-start.21 = (bf16[128,1024]{1,0:T(8,128)(2,1)S(1)}, bf16[128,1024]{1,0:T(8,128)(2,1)S(1)}, u32[]{:S(2)}, u32[]{:S(2)}) collective-permute-start(bf16[128,1024]{1,0:T(8,128)(2,1)S(1)} %get-tuple-element.76), channel_id=1, source_target_pairs={{0,16},{2,18},{4,20},{6,22},{8,24},{10,26},{12,28},{14,30},{16,0},... | collective-permute-start | bytes 786440 | tf_op jit(solution)/shard_map/ppermute | solution.py:32
  210.9 21.0 %collective-permute-start.20 = (bf16[128,1024]{1,0:T(8,128)(2,1)S(1)}, bf16[128,1024]{1,0:T(8,128)(2,1)S(1)}, u32[]{:S(2)}, u32[]{:S(2)}) collective-permute-start(bf16[128,1024]{1,0:T(8,128)(2,1)S(1)} %get-tuple-element.77), channel_id=1, source_target_pairs={{0,24},{2,26},{4,28},{6,30},{8,0},{10,2},{12,4},{14,6},{16,8},{18,... | collective-permute-start | bytes 786440 | tf_op jit(solution)/shard_map/ppermute | solution.py:32
  231.9 4.3 %collective-permute-start.30 = (bf16[128,2688]{1,0:T(8,128)(2,1)}, bf16[128,2688]{1,0:T(8,128)(2,1)}, u32[]{:S(2)}, u32[]{:S(2)}) collective-permute-start(bf16[128,2688]{1,0:T(8,128)(2,1)} %get-tuple-element.37), channel_id=1, source_target_pairs={{24,16},{26,18},{28,20},{30,22},{25,17},{27,19},{29,21},{31,23}} | collective-permute-start | bytes 2064392 | tf_op jit(solution)/shard_map/ppermute | solution.py:36
  234.7 28.7 %collective-permute-start.23 = (bf16[128,2048]{0,1:T(8,128)(2,1)S(1)}, bf16[128,2048]{0,1:T(8,128)(2,1)S(1)}, u32[]{:S(2)}, u32[]{:S(2)}) collective-permute-start(bf16[128,2048]{0,1:T(8,128)(2,1)S(1)} %dynamic-slice_bitcast_fusion), channel_id=1, source_target_pairs={{0,1},{1,0},{2,3},{3,2},{4,5},{5,4},{6,7},{7,6},{8,9},{9,8},{10,11... | collective-permute-start | bytes 1572872 | tf_op jit(solution)/shard_map/ppermute | solution.py:39
  239.3 27.4 %copy-start.10 = (bf16[2688,256]{1,0:T(8,128)(2,1)S(1)}, bf16[2688,256]{1,0:T(8,128)(2,1)}, u32[]{:S(2)}) copy-start(bf16[2688,256]{1,0:T(8,128)(2,1)} %slice.177) | copy-start | bytes 4128772
  239.3 34.4 %collective-permute-start.33 = (bf16[128,2688]{1,0:T(8,128)(2,1)}, bf16[128,2688]{1,0:T(8,128)(2,1)}, u32[]{:S(2)}, u32[]{:S(2)}) collective-permute-start(bf16[128,2688]{1,0:T(8,128)(2,1)} %get-tuple-element.40), channel_id=1, source_target_pairs={{0,8},{2,10},{4,12},{6,14},{8,16},{10,18},{12,20},{14,22},{1,9},{3... | collective-permute-start | bytes 2064392 | tf_op jit(solution)/shard_map/ppermute | solution.py:36
  257.5 20.6 %collective-permute-start.34 = (bf16[128,2688]{1,0:T(8,128)(2,1)}, bf16[128,2688]{1,0:T(8,128)(2,1)}, u32[]{:S(2)}, u32[]{:S(2)}) collective-permute-start(bf16[128,2688]{1,0:T(8,128)(2,1)} %get-tuple-element.41), channel_id=1, source_target_pairs={{24,16},{26,18},{28,20},{30,22},{16,8},{18,10},{20,12},{22,14},{25... | collective-permute-start | bytes 2064392 | tf_op jit(solution)/shard_map/ppermute | solution.py:36
  258.8 30.2 %collective-permute-start.31 = (bf16[128,2816]{1,0:T(8,128)(2,1)S(1)}, bf16[128,2816]{1,0:T(8,128)(2,1)}, u32[]{:S(2)}, u32[]{:S(2)}) collective-permute-start(bf16[128,2816]{1,0:T(8,128)(2,1)S(1)} %get-tuple-element.38), channel_id=1, source_target_pairs={{0,8},{2,10},{4,12},{6,14},{8,16},{10,18},{12,20},{14,22},{16,24},... | collective-permute-start | bytes 2162696 | tf_op jit(solution)/shard_map/ppermute | solution.py:36
  263.3 30.2 %collective-permute-start.32 = (bf16[128,2816]{1,0:T(8,128)(2,1)S(1)}, bf16[128,2816]{1,0:T(8,128)(2,1)}, u32[]{:S(2)}, u32[]{:S(2)}) collective-permute-start(bf16[128,2816]{1,0:T(8,128)(2,1)S(1)} %get-tuple-element.39), channel_id=1, source_target_pairs={{24,16},{26,18},{28,20},{30,22},{16,8},{18,10},{20,12},{22,14},{8,... | collective-permute-start | bytes 2162696 | tf_op jit(solution)/shard_map/ppermute | solution.py:36
  266.7 41.6 %collective-permute-start.39 = (bf16[2688,256]{1,0:T(8,128)(2,1)S(1)}, bf16[2688,256]{1,0:T(8,128)(2,1)S(1)}, u32[]{:S(2)}, u32[]{:S(2)}) collective-permute-start(bf16[2688,256]{1,0:T(8,128)(2,1)S(1)} %copy-done.10), channel_id=1, source_target_pairs={{0,4},{2,6},{4,0},{6,2},{8,12},{10,14},{12,8},{14,10},{16,20},{18,... | collective-permute-start | bytes 4128776 | tf_op jit(solution)/shard_map/ppermute | solution.py:28
  270.2 23.3 %copy-start.7 = (bf16[128,5504]{1,0:T(8,128)(2,1)S(1)}, bf16[128,5504]{1,0:T(8,128)(2,1)}, u32[]{:S(2)}) copy-start(bf16[128,5504]{1,0:T(8,128)(2,1)} %param.5) | copy-start | bytes 4227076
  270.2 23.3 %copy-start.9 = (bf16[128,5504]{1,0:T(8,128)(2,1)S(1)}, bf16[128,5504]{1,0:T(8,128)(2,1)}, u32[]{:S(2)}) copy-start(bf16[128,5504]{1,0:T(8,128)(2,1)} %param.4) | copy-start | bytes 4227076
  280.4 19.8 %collective-permute-start.36 = (bf16[128,2688]{1,0:T(8,128)(2,1)S(1)}, bf16[128,2688]{1,0:T(8,128)(2,1)S(1)}, u32[]{:S(2)}, u32[]{:S(2)}) collective-permute-start(bf16[128,2688]{1,0:T(8,128)(2,1)S(1)} %get-tuple-element.42), channel_id=1, source_target_pairs={{0,8},{2,10},{4,12},{6,14},{8,16},{10,18},{12,20},{14,22},{16,24},... | collective-permute-start | bytes 2064392 | tf_op jit(solution)/shard_map/ppermute | solution.py:36
  282.4 22.0 %collective-permute-start.37 = (bf16[128,2688]{1,0:T(8,128)(2,1)S(1)}, bf16[128,2688]{1,0:T(8,128)(2,1)S(1)}, u32[]{:S(2)}, u32[]{:S(2)}) collective-permute-start(bf16[128,2688]{1,0:T(8,128)(2,1)S(1)} %get-tuple-element.43), channel_id=1, source_target_pairs={{24,16},{26,18},{28,20},{30,22},{16,8},{18,10},{20,12},{22,14},{8,... | collective-permute-start | bytes 2064392 | tf_op jit(solution)/shard_map/ppermute | solution.py:36
  (29 other events, 225.2 us)

commit v5 on v4

--- a/solution.py
+++ b/solution.py
@@ -4,7 +4,6 @@
 from jax.sharding import PartitionSpec as P
 
 QUAD = 4
-CHUNKS = 2
 ORDER = (0, 2, 1, 3)
 
 
@@ -34,6 +33,8 @@
     def hop(value, way, sources):
         pairs = [(s * QUAD + q, (s + way) * QUAD + q) for s in sources for q in range(QUAD)]
         return lax.ppermute(value, "hst", pairs)
+
+    far_groups = [[f * QUAD + q for f in range(n_far)] for q in range(QUAD)]
 
     def local_shift(value, step):
         return lax.ppermute(value, "local", [(i, (i + step) % n_local) for i in range(n_local)])
@@ -45,10 +46,9 @@
         tokens, half = cotangent.shape
         width = down_weight.shape[1]
         hidden_units = gate_act.shape[1]
-        n_chunks = CHUNKS
-        lanes = -(-hidden_units // 128)
-        chunk = 128 * -(-lanes // n_chunks)
-        bounds = [(f * chunk, min(hidden_units, (f + 1) * chunk)) for f in range(n_chunks)]
+        n_chunks = 2
+        first = 128 * (hidden_units * 24 // (43 * 128))
+        bounds = [(0, first), (first, hidden_units)]
 
         parts = [cotangent]
         for step in range(1, n_local):
@@ -70,19 +70,27 @@
             [cot_for(0)] + [shift(cot_for(n_far - e), n_far - e) for e in range(1, n_far)], axis=0
         )
 
-        weights, last = [], []
+        twice = jnp.concatenate([cot_rows, cot_rows[:-tokens]], axis=0)
+        cot_sorted = lax.dynamic_slice_in_dim(
+            twice, ((n_far - far) % n_far) * tokens, n_far * tokens, axis=0
+        )
+
+        last, history = [parts[1]], []
+        got, weights, own_pairs = {}, {}, []
         for f, (lo, hi) in enumerate(bounds):
             weight = after(down_weight[lo:hi], *last)
             other = swap(weight, 2)
             last = [other]
-            if f == 0:
-                last.append(parts[1])
-            if f == 1:
-                last.append(cot_rows)
-            pair = jnp.concatenate([weight, other], axis=1)
-            weights.append(jnp.concatenate([pair, swap(pair, 1)], axis=1))
-
-        wide, hidden, terms = {}, {}, {}
+            own_pairs.append((weight, other))
+
+        def weight_cols(f):
+            if f not in weights:
+                pair = jnp.concatenate(own_pairs[f], axis=1)
+                far_pair = swap(after(pair, cot_rows, *(history[0] if f else ())), 1)
+                weights[f] = jnp.concatenate([pair, far_pair], axis=1)
+            return weights[f]
+
+        wide, hidden = {}, {}
         for f, (lo, hi) in enumerate(bounds):
             gate_wide = gate_act[:, lo:hi].astype(jnp.float32)
             up_wide = up_act[:, lo:hi].astype(jnp.float32)
@@ -90,23 +98,21 @@
             wide[f] = gate_wide, up_wide, sigmoid_gate
             hidden[f] = (gate_wide * sigmoid_gate * up_wide).astype(jnp.bfloat16)
 
+        hidden = lax.optimization_barrier(hidden)
         gate_parts, up_parts, grad_parts, out_sums = {}, {}, {}, {}
-        ready = []
-
-        def gathered(f, above, below):
-            slots = [hidden[f]]
-            for e in range(1, n_far):
-                slots.append(jnp.where(far + e < n_far, above[e], below[n_far - e]))
-            hidden_rows = jnp.concatenate(slots, axis=0)
-            out_sums[f] = jnp.dot(hidden_rows, weights[f], preferred_element_type=jnp.float32)
+
+        def gathered(f):
+            hidden_rows = after(got["hidden", f], *history[-1])
+            out_sums[f] = jnp.dot(hidden_rows, weight_cols(f), preferred_element_type=jnp.float32)
             grad = lax.dot_general(
-                hidden_rows, cot_rows, (((0,), (0,)), ((), ())), preferred_element_type=jnp.float32
+                hidden_rows, cot_sorted, (((0,), (0,)), ((), ())), preferred_element_type=jnp.float32
             )
             theirs = swap(grad[:, 2 * width :].astype(jnp.bfloat16), 1)
-            ready.append(theirs)
+            got["gc", f] = theirs
             grad = grad[:, : 2 * width] + theirs.astype(jnp.float32)
             theirs = swap(after(grad[:, width:].astype(jnp.bfloat16), *last), 2)
             last[:] = [theirs]
+            got["gy", f] = theirs
             grad_parts[f] = grad[:, :width] + theirs.astype(jnp.float32)
 
         def reduced(f, hidden_grad):
@@ -116,32 +122,25 @@
                 hidden_grad * up_wide * sigmoid_gate * (1.0 + gate_wide * (1.0 - sigmoid_gate))
             ).astype(jnp.bfloat16)
 
-        history = []
-
-        def both_ways(up, down, sources, *awaited):
-            if len(history) > 2:
-                awaited += history[-3]
+        rounds_in_all = (n_far - 1) * n_chunks
+        due = [(2, ("hidden", 0)), (3, ("gc", 0)), (5, ("gy", 0))]
+
+        def both_ways(up, down, sources):
+            now = len(history)
+            awaited = history[-2] if now > 1 else ()
+            for place, key in list(due):
+                if key in got and now * 6 >= place * rounds_in_all:
+                    awaited += (got[key],)
+                    due.remove((place, key))
             if awaited:
                 up, down = lax.optimization_barrier((up, down) + awaited)[:2]
             downs = [n_far - 1 - z for z in sources]
             history.append((hop(up, 1, sources), hop(down, -1, downs)))
             return history[-1]
 
-        def gather_rounds(f):
-            above, below = {}, {}
-            up = down = hidden[f]
-            for j in range(1, n_far):
-                up, down = both_ways(
-                    up, down, range(j - 1, n_far - 1), *([cot_rows] if j == n_far - 1 else [])
-                )
-                below[j], above[j] = up, down
-                if j == n_far - 1:
-                    gathered(f, above, below)
-                yield
-
         def reduce_rounds(f):
             terms = lax.dot_general(
-                cot_rows, weights[f], (((1,), (1,)), ((), ())), preferred_element_type=jnp.float32
+                cot_rows, weight_cols(f), (((1,), (1,)), ((), ())), preferred_element_type=jnp.float32
             )
             slots = [terms[e * tokens : (e + 1) * tokens] for e in range(n_far)]
             up = down = None
@@ -154,27 +153,35 @@
                     up_term.astype(jnp.bfloat16),
                     down_term.astype(jnp.bfloat16),
                     range(0, n_far - d),
-                    *(ready[f : f + 1] if d == 1 else []),
                 )
                 if d == 1:
                     reduced(f, slots[0] + up.astype(jnp.float32) + down.astype(jnp.float32))
                 yield
 
-        gathers = [gather_rounds(f) for f in range(n_chunks)]
+        for f in range(n_chunks):
+            got["hidden", f] = lax.all_gather(
+                after(hidden[f], parts[1]) if f else hidden[f],
+                "hst",
+                axis=0,
+                tiled=True,
+                axis_index_groups=far_groups,
+            )
         reduces = [reduce_rounds(f) for f in range(n_chunks)]
-        gather_order = [gathers[f] for j in range(1, n_far) for f in range(n_chunks)]
-        reduce_order = [reduces[f] for j in range(1, n_far) for f in range(n_chunks)]
-        lag = len(gather_order) - n_chunks + 1
-        order = gather_order[:lag]
-        for i, rounds in enumerate(reduce_order):
-            order += [rounds] + gather_order[lag + i : lag + i + 1]
-        for rounds in order:
-            next(rounds)
+        for j in range(1, n_far):
+            for f, rounds in enumerate(reduces):
+                next(rounds)
+                if len(history) in (1, 4):
+                    gathered(len(history) // 4)
 
         out_terms = sum(out_sums[f] for f in range(n_chunks)).astype(jnp.bfloat16)
-        slots = [out_terms[:tokens]]
-        for e in range(1, n_far):
-            slots.append(shift(out_terms[e * tokens : (e + 1) * tokens], e))
+        out_terms = after(out_terms, got["gc", n_chunks - 1])
+
+        def out_for(step):
+            return lax.dynamic_slice_in_dim(
+                out_terms, ((far + step) % n_far) * tokens, tokens, axis=0
+            )
+
+        slots = [out_for(0)] + [shift(out_for(e), e) for e in range(1, n_far)]
         back = [slots[0]] + slots[:0:-1]
         twice = jnp.concatenate(back + back[:-1], axis=1)
         columns = QUAD * width

time: 313 us -> 348 us (1.11)
  waiting for transfers between devices: 112 us -> 182 us
  starting transfers between devices: 96.5 us -> 44.8 us
  local copies, waits for them, and re-layouts: 21.8 us -> 38.5 us
  between operations: 1.85 us -> 14.8 us
  other arithmetic: 48 us -> 35.4 us
    ppermute x24 -> x12, starting transfers between devices: 73.6 us -> 28.8 us  [hop(): return lax.ppermute(value, 'hst', pairs)]
    ppermute x8, waiting for transfers between devices: 0.02 us -> 25.2 us  [swap(): return lax.ppermute(value, 'hst', [(h, h ^ bit) for h in range(n_hst)])]
    ppermute x2, waiting for transfers between devices: 2.53 us -> 21.4 us  [local_shift(): lax.ppermute(value, 'local', [(i, (i + step) % n_local) for i in range(n_...]
    ppermute x6, waiting for transfers between devices: 42.3 us -> 61 us  [shift(): return lax.ppermute(value, 'hst', pairs)]
    unnamed x87 -> x79, local copies, waits for them, and re-layouts: 7.15 us -> 20.6 us
    ppermute x24 -> x12, waiting for transfers between devices: 67.1 us -> 74.6 us  [hop(): return lax.ppermute(value, 'hst', pairs)]
    ppermute x6, starting transfers between devices: 13.6 us -> 7.32 us  [shift(): return lax.ppermute(value, 'hst', pairs)]
    select_n x6 -> x0, other arithmetic: 6.05 us -> none  [gathered(): slots.append(jnp.where(far + e < n_far, above[e], below[n_far - e]))]
  transfers between devices with their start and end apart: 40 -> 30, of which waited for: 17 -> 16; matrix products, arithmetic and copies ran while one was open for 31% -> 26% of each run, Pallas kernels for 0% -> 0%
where the time goes in v5:
time: 348 us; the launch traced here: 347 us
  waiting for transfers between devices  182 us (52%)
  starting transfers between devices  44.8 us (13%)
  local copies, waits for them, and re-layouts  38.5 us (11%)
  other arithmetic  35.4 us (10%)
  matrix products  31.2 us (9%)
  between operations  14.8 us (4%)
    ppermute x12, waiting for transfers between devices, hop(): return lax.ppermute(value, 'hst', pairs)  74.6 us
    ppermute x6, waiting for transfers between devices, shift(): return lax.ppermute(value, 'hst', pairs)  61 us
    ppermute x12, starting transfers between devices, hop(): return lax.ppermute(value, 'hst', pairs)  28.8 us
    ppermute x8, waiting for transfers between devices, swap(): return lax.ppermute(value, 'hst', [(h, h ^ bit) for h in range(n_hst)])  25.2 us
    ppermute x2, waiting for transfers between devices, local_shift(): lax.ppermute(value, 'local', [(i, (i + step) % n_local) for i in range(n_...  21.4 us
    unnamed x79, local copies, waits for them, and re-layouts  20.6 us
    dot_general x2, matrix products, gathered(): jnp.dot(hidden_rows, weight_cols(f), preferred_element_type=jnp.float32)  12 us
    dot_general x2, matrix products, reduce_rounds(): lax.dot_general(cot_rows, weight_cols(f), (((1,), (1,)), ((), ())), prefe...  10.4 us
  transfers between devices with their start and end apart: 30, of which 16 were waited for; matrix products, arithmetic and copies ran while one was open for 26% of the time, Pallas kernels for 0%

profile of v5, /device:TPU:8, one launch (start us, length us, event | category | flops | bytes accessed | tf_op | source)
XLA Modules:
  0.0 346.9 jit_solution(17236303919296928959)
XLA Ops:
  7.2 2.6 fusion.11
  9.8 2.5 fusion
  15.8 10.7 %collective-permute-done = bf16[128,2048]{0,1:T(8,128)(2,1)S(1)} collective-permute-done((bf16[128,2048]{0,1:T(8,128)(2,1)S(1)}, bf16[128,2048]{0,1:T(8,128)(2,1)S(1)}, u32[]{:S(2)}, u32[]{:S(2)}) %collective-permute-start) | collective-permute-done | bytes 524320 | tf_op jit(solution)/shard_map/ppermute | solution.py:40
  28.8 2.1 fusion.23
  32.0 1.8 copy.20
  33.8 1.8 copy.19
  38.5 2.6 collective-permute-start.2
  42.1 21.5 %collective-permute-done.3 = bf16[128,1024]{1,0:T(8,128)(2,1)} collective-permute-done((bf16[128,1024]{1,0:T(8,128)(2,1)}, bf16[128,1024]{1,0:T(8,128)(2,1)}, u32[]{:S(2)}, u32[]{:S(2)}) %collective-permute-start.3) | collective-permute-done | bytes 262176 | tf_op jit(solution)/shard_map/ppermute | solution.py:31
  63.6 25.6 %collective-permute-done.2 = bf16[128,1024]{1,0:T(8,128)(2,1)} collective-permute-done((bf16[128,1024]{1,0:T(8,128)(2,1)}, bf16[128,1024]{1,0:T(8,128)(2,1)}, u32[]{:S(2)}, u32[]{:S(2)}) %collective-permute-start.2) | collective-permute-done | bytes 262176 | tf_op jit(solution)/shard_map/ppermute | solution.py:31
  89.2 2.1 pad_maximum_fusion.1
  99.0 2.4 constant_dynamic-update-slice_fusion
  101.4 5.1 %fusion.32 = f32[512,3072]{1,0:T(8,128)S(1)} fusion(bf16[3072,1024]{1,0:T(8,128)(2,1)S(1)} %constant_dynamic-update-slice_fusion, bf16[128,1024]{1,0:T(8,128)(2,1)} %collective-permute-done.3, bf16[128,1024]{1,0:T(8,128)(2,1)} %collective-permute-done.2, bf16[128,1024]{1,0:T(8,128)(2,1)} %collective-permute-done.1, bf16[128,1024]{1,0:T(8,128)(2,1)S(1)} %bitcast.34), kind=kOutput, calls=%fused_computation.116 | convolution fusion | flops 3225419776 | bytes 13631488 | tf_op jit(solution)/shard_map/dot_general | solution.py:142
  109.9 18.1 %collective-permute-done.8 = bf16[2432,256]{1,0:T(8,128)(2,1)S(1)} collective-permute-done((bf16[2432,256]{1,0:T(8,128)(2,1)S(1)}, bf16[2432,256]{1,0:T(8,128)(2,1)S(1)}, u32[]{:S(2)}, u32[]{:S(2)}) %collective-permute-start.8) | collective-permute-done | bytes 1245216 | tf_op jit(solution)/shard_map/ppermute | solution.py:27
  129.7 17.3 %collective-permute-done.6 = bf16[128,3072]{1,0:T(8,128)(2,1)S(1)} collective-permute-done((bf16[128,3072]{1,0:T(8,128)(2,1)S(1)}, bf16[128,3072]{1,0:T(8,128)(2,1)S(1)}, u32[]{:S(2)}, u32[]{:S(2)}) %collective-permute-start.6) | collective-permute-done | bytes 786464 | tf_op jit(solution)/shard_map/ppermute | solution.py:35
  148.6 2.5 collective-permute-start.20
  153.7 6.0 %fusion.27 = f32[3072,1024]{1,0:T(8,128)S(1)} fusion(bf16[512,3072]{1,0:T(8,128)(2,1)} %all-gather.3.cloned.1.call-done, bf16[896,1024]{1,0:T(8,128)(2,1)S(1)} %copy-done.19, s32[]{:T(128)S(6)} %select_n.135), kind=kOutput, calls=%fused_computation.74 | convolution fusion | flops 3221225472 | bytes 16777220 | tf_op jit(solution)/shard_map/dot_general | solution.py:107
  160.4 22.3 %collective-permute-done.20 = bf16[128,3072]{1,0:T(8,128)(2,1)S(1)} collective-permute-done((bf16[128,3072]{1,0:T(8,128)(2,1)}, bf16[128,3072]{1,0:T(8,128)(2,1)S(1)}, u32[]{:S(2)}, u32[]{:S(2)}) %collective-permute-start.20) | collective-permute-done | bytes 786464 | tf_op jit(solution)/shard_map/ppermute | solution.py:35
  184.3 4.5 %collective-permute-start.22 = (bf16[128,3072]{1,0:T(8,128)(2,1)}, bf16[128,3072]{1,0:T(8,128)(2,1)S(1)}, u32[]{:S(2)}, u32[]{:S(2)}) collective-permute-start(bf16[128,3072]{1,0:T(8,128)(2,1)} %get-tuple-element.38), channel_id=1, source_target_pairs={{0,8},{2,10},{4,12},{6,14},{8,16},{10,18},{12,20},{14,22},{16,24},... | collective-permute-start | bytes 2359304 | tf_op jit(solution)/shard_map/ppermute | solution.py:35
  188.8 1.9 collective-permute-start.23
  190.8 3.3 constant_dynamic-update-slice_fusion.3
  194.1 5.3 %fusion.31 = f32[512,2432]{1,0:T(8,128)S(1)} fusion(bf16[2432,1024]{1,0:T(8,128)(2,1)} %constant_dynamic-update-slice_fusion.3, bf16[128,1024]{1,0:T(8,128)(2,1)} %collective-permute-done.3, bf16[128,1024]{1,0:T(8,128)(2,1)} %collective-permute-done.2, bf16[128,1024]{1,0:T(8,128)(2,1)} %collective-permute-done.1, bf16[128,1024]{1,0:T(8,128)(2,1)S(1)} %bitcast.35), kind=kOutput, calls=%fused_computation.115 | convolution fusion | flops 2554331136 | bytes 11010048 | tf_op jit(solution)/shard_map/dot_general | solution.py:142
  201.8 5.0 %collective-permute-done.22 = bf16[128,3072]{1,0:T(8,128)(2,1)S(1)} collective-permute-done((bf16[128,3072]{1,0:T(8,128)(2,1)}, bf16[128,3072]{1,0:T(8,128)(2,1)S(1)}, u32[]{:S(2)}, u32[]{:S(2)}) %collective-permute-start.22) | collective-permute-done | bytes 786464 | tf_op jit(solution)/shard_map/ppermute | solution.py:35
  206.8 3.4 collective-permute-done.23
  210.2 3.3 fusion.9
  213.5 5.7 %collective-permute-done.10 = bf16[128,2432]{1,0:T(8,128)(2,1)S(1)} collective-permute-done((bf16[128,2432]{1,0:T(8,128)(2,1)S(1)}, bf16[128,2432]{1,0:T(8,128)(2,1)S(1)}, u32[]{:S(2)}, u32[]{:S(2)}) %collective-permute-start.10) | collective-permute-done | bytes 622624 | tf_op jit(solution)/shard_map/ppermute | solution.py:35
  220.4 6.5 %collective-permute-start.13 = (bf16[128,2432]{1,0:T(8,128)(2,1)}, bf16[128,2432]{1,0:T(8,128)(2,1)}, u32[]{:S(2)}, u32[]{:S(2)}) collective-permute-start(bf16[128,2432]{1,0:T(8,128)(2,1)} %get-tuple-element.32), channel_id=1, source_target_pairs={{0,8},{2,10},{4,12},{6,14},{8,16},{10,18},{12,20},{14,22},{1,9},{3... | collective-permute-start | bytes 1867784 | tf_op jit(solution)/shard_map/ppermute | solution.py:35
  229.7 2.7 copy-done
  234.1 5.6 %collective-permute-done.13 = bf16[128,2432]{1,0:T(8,128)(2,1)} collective-permute-done((bf16[128,2432]{1,0:T(8,128)(2,1)}, bf16[128,2432]{1,0:T(8,128)(2,1)}, u32[]{:S(2)}, u32[]{:S(2)}) %collective-permute-start.13) | collective-permute-done | bytes 622624 | tf_op jit(solution)/shard_map/ppermute | solution.py:35
  239.7 4.1 %collective-permute-done.14 = bf16[128,2432]{1,0:T(8,128)(2,1)} collective-permute-done((bf16[128,2432]{1,0:T(8,128)(2,1)}, bf16[128,2432]{1,0:T(8,128)(2,1)}, u32[]{:S(2)}, u32[]{:S(2)}) %collective-permute-start.14) | collective-permute-done | bytes 622624 | tf_op jit(solution)/shard_map/ppermute | solution.py:35
  243.9 5.5 %fusion.35 = f32[512,1024]{1,0:T(8,128)S(1)} fusion(bf16[512,2432]{1,0:T(8,128)(2,1)} %all-gather.5.cloned.1.call-done, bf16[2432,1024]{1,0:T(8,128)(2,1)} %constant_dynamic-update-slice_fusion.3), kind=kOutput, calls=%fused_computation.119 | convolution fusion | flops 2550136832 | bytes 9568256 | tf_op jit(solution)/shard_map/dot_general | solution.py:106
  249.4 2.8 fusion.25
  252.7 6.5 %add_convert_fusion = bf16[512,1024]{1,0:T(8,128)(2,1)S(1)} fusion(f32[512,1024]{1,0:T(8,128)S(1)} %fusion.35, bf16[512,3072]{1,0:T(8,128)(2,1)S(1)} %copy-done.21, bf16[3072,1024]{1,0:T(8,128)(2,1)} %copy-done.17), kind=kOutput, calls=%fused_computation.19 | convolution fusion | flops 3222274048 | bytes 12582912 | tf_op jit(solution)/shard_map/dot_general | solution.py:106
  260.7 7.0 %collective-permute-done.24 = bf16[3072,256]{1,0:T(8,128)(2,1)S(1)} collective-permute-done((bf16[3072,256]{1,0:T(8,128)(2,1)S(1)}, bf16[3072,256]{1,0:T(8,128)(2,1)S(1)}, u32[]{:S(2)}, u32[]{:S(2)}) %collective-permute-start.24) | collective-permute-done | bytes 1572896 | tf_op jit(solution)/shard_map/ppermute | solution.py:27
  267.8 4.3 %collective-permute-start.25 = (bf16[128,2432]{1,0:T(8,128)(2,1)S(1)}, bf16[128,2432]{1,0:T(8,128)(2,1)S(1)}, u32[]{:S(2)}, u32[]{:S(2)}) collective-permute-start(bf16[128,2432]{1,0:T(8,128)(2,1)S(1)} %get-tuple-element.41), channel_id=1, source_target_pairs={{0,8},{2,10},{4,12},{6,14},{8,16},{10,18},{12,20},{14,22},{16,24},... | collective-permute-start | bytes 1867784 | tf_op jit(solution)/shard_map/ppermute | solution.py:35
  272.1 1.9 collective-permute-start.26
  274.0 1.9 slice_add_fusion.2
  275.9 7.6 %collective-permute-done.25 = bf16[128,2432]{1,0:T(8,128)(2,1)S(1)} collective-permute-done((bf16[128,2432]{1,0:T(8,128)(2,1)S(1)}, bf16[128,2432]{1,0:T(8,128)(2,1)S(1)}, u32[]{:S(2)}, u32[]{:S(2)}) %collective-permute-start.25) | collective-permute-done | bytes 622624 | tf_op jit(solution)/shard_map/ppermute | solution.py:35
  283.5 3.7 %collective-permute-done.26 = bf16[128,2432]{1,0:T(8,128)(2,1)S(1)} collective-permute-done((bf16[128,2432]{1,0:T(8,128)(2,1)S(1)}, bf16[128,2432]{1,0:T(8,128)(2,1)S(1)}, u32[]{:S(2)}, u32[]{:S(2)}) %collective-permute-start.26) | collective-permute-done | bytes 622624 | tf_op jit(solution)/shard_map/ppermute | solution.py:35
  287.2 3.1 fusion.20
  291.0 2.1 collective-permute-start.17
  294.1 2.3 copy-done.1
  299.1 13.9 %collective-permute-done.16 = bf16[128,1024]{1,0:T(8,128)(2,1)S(1)} collective-permute-done((bf16[128,1024]{1,0:T(8,128)(2,1)S(1)}, bf16[128,1024]{1,0:T(8,128)(2,1)S(1)}, u32[]{:S(2)}, u32[]{:S(2)}) %collective-permute-start.16) | collective-permute-done | bytes 262176 | tf_op jit(solution)/shard_map/ppermute | solution.py:31
  314.2 2.3 copy.16
  319.5 1.7 pad_maximum_fusion.3
  321.2 10.7 %collective-permute-done.19 = bf16[128,2048]{0,1:T(8,128)(2,1)S(1)} collective-permute-done((bf16[128,2048]{0,1:T(8,128)(2,1)S(1)}, bf16[128,2048]{0,1:T(8,128)(2,1)S(1)}, u32[]{:S(2)}, u32[]{:S(2)}) %collective-permute-start.19) | collective-permute-done | bytes 524320 | tf_op jit(solution)/shard_map/ppermute | solution.py:40
  332.9 2.0 copy.17
  334.9 2.3 slice_add_fusion.3
  337.2 2.9 pad_maximum_fusion
  (141 shorter events, 49.4 us)
Async XLA Ops:
  7.2 141.4 %all-gather.3.cloned.1.call-start = ((), (), s32[]{:S(2)}) async-start(), calls=%async_computation | async-start | bytes 3932160 | tf_op jit(solution)/shard_map/all_gather | solution.py:162
  12.4 221.8 %all-gather.5.cloned.1.call-start = ((), (), s32[]{:S(2)}) async-start(), calls=%async_computation.1 | async-start | bytes 3112960 | tf_op jit(solution)/shard_map/all_gather | solution.py:162
  12.7 13.7 %collective-permute-start = (bf16[128,2048]{0,1:T(8,128)(2,1)S(1)}, bf16[128,2048]{0,1:T(8,128)(2,1)S(1)}, u32[]{:S(2)}, u32[]{:S(2)}) collective-permute-start(bf16[128,2048]{0,1:T(8,128)(2,1)S(1)} %copy.10), channel_id=1, source_target_pairs={{0,1},{1,0},{2,3},{3,2},{4,5},{5,4},{6,7},{7,6},{8,9},{9,8},{10,11... | collective-permute-start | bytes 1572872 | tf_op jit(solution)/shard_map/ppermute | solution.py:40
  27.2 62.0 %collective-permute-start.4 = (bf16[3072,256]{1,0:T(8,128)(2,1)S(1)}, bf16[3072,256]{1,0:T(8,128)(2,1)S(1)}, u32[]{:S(2)}, u32[]{:S(2)}) collective-permute-start(bf16[3072,256]{1,0:T(8,128)(2,1)S(1)} %slice.76), channel_id=1, source_target_pairs={{0,4},{2,6},{4,0},{6,2},{8,12},{10,14},{12,8},{14,10},{16,20},{18,... | collective-permute-start | bytes 4718600 | tf_op jit(solution)/shard_map/ppermute | solution.py:27
  36.4 27.2 %collective-permute-start.3 = (bf16[128,1024]{1,0:T(8,128)(2,1)}, bf16[128,1024]{1,0:T(8,128)(2,1)}, u32[]{:S(2)}, u32[]{:S(2)}) collective-permute-start(bf16[128,1024]{1,0:T(8,128)(2,1)} %bitcast.38), channel_id=1, source_target_pairs={{0,8},{2,10},{4,12},{6,14},{8,16},{10,18},{12,20},{14,22},{16,24},... | collective-permute-start | bytes 786440 | tf_op jit(solution)/shard_map/ppermute | solution.py:31
  38.0 25.6 %collective-permute-start.1 = (bf16[128,1024]{1,0:T(8,128)(2,1)}, bf16[128,1024]{1,0:T(8,128)(2,1)}, u32[]{:S(2)}, u32[]{:S(2)}) collective-permute-start(bf16[128,1024]{1,0:T(8,128)(2,1)} %bitcast.37), channel_id=1, source_target_pairs={{0,24},{2,26},{4,28},{6,30},{8,0},{10,2},{12,4},{14,6},{16,8},{18,... | collective-permute-start | bytes 786440 | tf_op jit(solution)/shard_map/ppermute | solution.py:31
  38.5 50.8 %collective-permute-start.2 = (bf16[128,1024]{1,0:T(8,128)(2,1)}, bf16[128,1024]{1,0:T(8,128)(2,1)}, u32[]{:S(2)}, u32[]{:S(2)}) collective-permute-start(bf16[128,1024]{1,0:T(8,128)(2,1)} %bitcast.36), channel_id=1, source_target_pairs={{0,16},{2,18},{4,20},{6,22},{8,24},{10,26},{12,28},{14,30},{16,0},... | collective-permute-start | bytes 786440 | tf_op jit(solution)/shard_map/ppermute | solution.py:31
  91.4 7.5 %collective-permute-start.5 = (bf16[3072,512]{1,0:T(8,128)(2,1)}, bf16[3072,512]{1,0:T(8,128)(2,1)}, u32[]{:S(2)}, u32[]{:S(2)}) collective-permute-start(bf16[3072,512]{1,0:T(8,128)(2,1)} %pad_maximum_fusion.1), channel_id=1, source_target_pairs={{0,2},{2,0},{4,6},{6,4},{8,10},{10,8},{12,14},{14,12},{16,18},{18,... | collective-permute-start | bytes 9437192 | tf_op jit(solution)/shard_map/ppermute | solution.py:27
  93.2 5.6 %copy-start.5 = (bf16[3072,256]{1,0:T(8,128)(2,1)S(1)}, bf16[3072,256]{1,0:T(8,128)(2,1)}, u32[]{:S(2)}) copy-start(bf16[3072,256]{1,0:T(8,128)(2,1)} %copy-done.4) | copy-start | bytes 4718596
  98.2 3.2 copy-start.18
  98.2 29.8 %collective-permute-start.8 = (bf16[2432,256]{1,0:T(8,128)(2,1)S(1)}, bf16[2432,256]{1,0:T(8,128)(2,1)S(1)}, u32[]{:S(2)}, u32[]{:S(2)}) collective-permute-start(bf16[2432,256]{1,0:T(8,128)(2,1)S(1)} %slice.79), channel_id=1, source_target_pairs={{0,4},{2,6},{4,0},{6,2},{8,12},{10,14},{12,8},{14,10},{16,20},{18,... | collective-permute-start | bytes 3735560 | tf_op jit(solution)/shard_map/ppermute | solution.py:27
  101.4 5.1 %copy-start.17 = (bf16[3072,1024]{1,0:T(8,128)(2,1)}, bf16[3072,1024]{1,0:T(8,128)(2,1)S(1)}, u32[]{:S(2)}) copy-start(bf16[3072,1024]{1,0:T(8,128)(2,1)S(1)} %constant_dynamic-update-slice_fusion) | copy-start | bytes 18874372
  106.5 40.5 %copy-start.2 = (f32[512,3072]{1,0:T(8,128)}, f32[512,3072]{1,0:T(8,128)S(1)}, u32[]{:S(2)}) copy-start(f32[512,3072]{1,0:T(8,128)S(1)} %fusion.32) | copy-start | bytes 18874372
  106.8 22.9 %collective-permute-start.7 = (bf16[128,3072]{1,0:T(8,128)(2,1)S(1)}, bf16[128,3072]{1,0:T(8,128)(2,1)S(1)}, u32[]{:S(2)}, u32[]{:S(2)}) collective-permute-start(bf16[128,3072]{1,0:T(8,128)(2,1)S(1)} %get-tuple-element.60), channel_id=1, source_target_pairs={{24,16},{26,18},{28,20},{30,22},{25,17},{27,19},{29,21},{31,23}} | collective-permute-start | bytes 2359304 | tf_op jit(solution)/shard_map/ppermute | solution.py:35
  107.5 39.5 %collective-permute-start.6 = (bf16[128,3072]{1,0:T(8,128)(2,1)S(1)}, bf16[128,3072]{1,0:T(8,128)(2,1)S(1)}, u32[]{:S(2)}, u32[]{:S(2)}) collective-permute-start(bf16[128,3072]{1,0:T(8,128)(2,1)S(1)} %get-tuple-element.61), channel_id=1, source_target_pairs={{0,8},{2,10},{4,12},{6,14},{1,9},{3,11},{5,13},{7,15}} | collective-permute-start | bytes 2359304 | tf_op jit(solution)/shard_map/ppermute | solution.py:35
  147.0 43.7 %collective-permute-start.9 = (bf16[2432,512]{1,0:T(8,128)(2,1)}, bf16[2432,512]{1,0:T(8,128)(2,1)}, u32[]{:S(2)}, u32[]{:S(2)}) collective-permute-start(bf16[2432,512]{1,0:T(8,128)(2,1)} %pad_maximum_fusion.2), channel_id=1, source_target_pairs={{0,2},{2,0},{4,6},{6,4},{8,10},{10,8},{12,14},{14,12},{16,18},{18,... | collective-permute-start | bytes 7471112 | tf_op jit(solution)/shard_map/ppermute | solution.py:27
  148.5 5.1 %copy-start.19 = (bf16[896,1024]{1,0:T(8,128)(2,1)S(1)}, bf16[896,1024]{1,0:T(8,128)(2,1)}, u32[]{:S(2)}) copy-start(bf16[896,1024]{1,0:T(8,128)(2,1)} %copy-done.18) | copy-start | bytes 5505028
  148.6 34.2 %collective-permute-start.20 = (bf16[128,3072]{1,0:T(8,128)(2,1)}, bf16[128,3072]{1,0:T(8,128)(2,1)S(1)}, u32[]{:S(2)}, u32[]{:S(2)}) collective-permute-start(bf16[128,3072]{1,0:T(8,128)(2,1)} %get-tuple-element.36), channel_id=1, source_target_pairs={{0,8},{2,10},{4,12},{6,14},{8,16},{10,18},{12,20},{14,22},{1,9},{3... | collective-permute-start | bytes 2359304 | tf_op jit(solution)/shard_map/ppermute | solution.py:35
  151.1 31.6 %collective-permute-start.21 = (bf16[128,3072]{1,0:T(8,128)(2,1)}, bf16[128,3072]{1,0:T(8,128)(2,1)S(1)}, u32[]{:S(2)}, u32[]{:S(2)}) collective-permute-start(bf16[128,3072]{1,0:T(8,128)(2,1)} %get-tuple-element.37), channel_id=1, source_target_pairs={{24,16},{26,18},{28,20},{30,22},{16,8},{18,10},{20,12},{22,14},{25... | collective-permute-start | bytes 2359304 | tf_op jit(solution)/shard_map/ppermute | solution.py:35
  152.5 30.2 %slice-start.2 = ((s8[6291456]{0:T(1024)(128)(4,1)}), s8[4194304]{0:T(1024)(128)(4,1)S(1)}, s32[]{:S(2)}) async-start(s8[6291456]{0:T(1024)(128)(4,1)} %bitcast.25), calls=%async_computation.4 | async-start | bytes 8388608
  153.7 29.0 %slice-start.3 = ((s8[6291456]{0:T(1024)(128)(4,1)}), s8[2097152]{0:T(1024)(128)(4,1)S(1)}, s32[]{:S(2)}) async-start(s8[6291456]{0:T(1024)(128)(4,1)} %bitcast.25), calls=%async_computation.5 | async-start | bytes 4194304
  160.2 60.2 %collective-permute-start.12 = (bf16[3072,512]{1,0:T(8,128)(2,1)S(1)}, bf16[3072,512]{1,0:T(8,128)(2,1)S(1)}, u32[]{:S(2)}, u32[]{:S(2)}) collective-permute-start(bf16[3072,512]{1,0:T(8,128)(2,1)S(1)} %slice.154), channel_id=1, source_target_pairs={{0,2},{2,0},{4,6},{6,4},{8,10},{10,8},{12,14},{14,12},{16,18},{18,... | collective-permute-start | bytes 9437192 | tf_op jit(solution)/shard_map/ppermute | solution.py:27
  184.3 22.5 %collective-permute-start.22 = (bf16[128,3072]{1,0:T(8,128)(2,1)}, bf16[128,3072]{1,0:T(8,128)(2,1)S(1)}, u32[]{:S(2)}, u32[]{:S(2)}) collective-permute-start(bf16[128,3072]{1,0:T(8,128)(2,1)} %get-tuple-element.38), channel_id=1, source_target_pairs={{0,8},{2,10},{4,12},{6,14},{8,16},{10,18},{12,20},{14,22},{16,24},... | collective-permute-start | bytes 2359304 | tf_op jit(solution)/shard_map/ppermute | solution.py:35
  188.8 21.3 %collective-permute-start.23 = (bf16[128,3072]{1,0:T(8,128)(2,1)}, bf16[128,3072]{1,0:T(8,128)(2,1)}, u32[]{:S(2)}, u32[]{:S(2)}) collective-permute-start(bf16[128,3072]{1,0:T(8,128)(2,1)} %get-tuple-element.39), channel_id=1, source_target_pairs={{24,16},{26,18},{28,20},{30,22},{16,8},{18,10},{20,12},{22,14},{8,... | collective-permute-start | bytes 2359304 | tf_op jit(solution)/shard_map/ppermute | solution.py:35
  194.1 16.1 %copy-start.8 = (bf16[128,5504]{1,0:T(8,128)(2,1)S(1)}, bf16[128,5504]{1,0:T(8,128)(2,1)}, u32[]{:S(2)}) copy-start(bf16[128,5504]{1,0:T(8,128)(2,1)} %param.4) | copy-start | bytes 4227076
  199.4 19.8 %copy-start.3 = (f32[512,2432]{1,0:T(8,128)}, f32[512,2432]{1,0:T(8,128)S(1)}, u32[]{:S(2)}) copy-start(f32[512,2432]{1,0:T(8,128)S(1)} %fusion.31) | copy-start | bytes 14942212
  199.4 10.8 %copy-start.7 = (bf16[128,5504]{1,0:T(8,128)(2,1)S(1)}, bf16[128,5504]{1,0:T(8,128)(2,1)}, u32[]{:S(2)}) copy-start(bf16[128,5504]{1,0:T(8,128)(2,1)} %param.5) | copy-start | bytes 4227076
  199.5 13.9 %collective-permute-start.11 = (bf16[128,2432]{1,0:T(8,128)(2,1)S(1)}, bf16[128,2432]{1,0:T(8,128)(2,1)S(1)}, u32[]{:S(2)}, u32[]{:S(2)}) collective-permute-start(bf16[128,2432]{1,0:T(8,128)(2,1)S(1)} %get-tuple-element.66), channel_id=1, source_target_pairs={{24,16},{26,18},{28,20},{30,22},{25,17},{27,19},{29,21},{31,23}} | collective-permute-start | bytes 1867784 | tf_op jit(solution)/shard_map/ppermute | solution.py:35
  200.4 18.8 %collective-permute-start.10 = (bf16[128,2432]{1,0:T(8,128)(2,1)S(1)}, bf16[128,2432]{1,0:T(8,128)(2,1)S(1)}, u32[]{:S(2)}, u32[]{:S(2)}) collective-permute-start(bf16[128,2432]{1,0:T(8,128)(2,1)S(1)} %get-tuple-element.67), channel_id=1, source_target_pairs={{0,8},{2,10},{4,12},{6,14},{1,9},{3,11},{5,13},{7,15}} | collective-permute-start | bytes 1867784 | tf_op jit(solution)/shard_map/ppermute | solution.py:35
  220.4 19.3 %collective-permute-start.13 = (bf16[128,2432]{1,0:T(8,128)(2,1)}, bf16[128,2432]{1,0:T(8,128)(2,1)}, u32[]{:S(2)}, u32[]{:S(2)}) collective-permute-start(bf16[128,2432]{1,0:T(8,128)(2,1)} %get-tuple-element.32), channel_id=1, source_target_pairs={{0,8},{2,10},{4,12},{6,14},{8,16},{10,18},{12,20},{14,22},{1,9},{3... | collective-permute-start | bytes 1867784 | tf_op jit(solution)/shard_map/ppermute | solution.py:35
  226.9 17.0 %collective-permute-start.14 = (bf16[128,2432]{1,0:T(8,128)(2,1)}, bf16[128,2432]{1,0:T(8,128)(2,1)}, u32[]{:S(2)}, u32[]{:S(2)}) collective-permute-start(bf16[128,2432]{1,0:T(8,128)(2,1)} %get-tuple-element.33), channel_id=1, source_target_pairs={{24,16},{26,18},{28,20},{30,22},{16,8},{18,10},{20,12},{22,14},{25... | collective-permute-start | bytes 1867784 | tf_op jit(solution)/shard_map/ppermute | solution.py:35
  232.6 35.2 %collective-permute-start.24 = (bf16[3072,256]{1,0:T(8,128)(2,1)S(1)}, bf16[3072,256]{1,0:T(8,128)(2,1)S(1)}, u32[]{:S(2)}, u32[]{:S(2)}) collective-permute-start(bf16[3072,256]{1,0:T(8,128)(2,1)S(1)} %slice.156), channel_id=1, source_target_pairs={{0,4},{2,6},{4,0},{6,2},{8,12},{10,14},{12,8},{14,10},{16,20},{18,... | collective-permute-start | bytes 4718600 | tf_op jit(solution)/shard_map/ppermute | solution.py:27
  234.1 15.2 %copy-start.20 = (bf16[896,1024]{1,0:T(8,128)(2,1)S(1)}, bf16[896,1024]{1,0:T(8,128)(2,1)}, u32[]{:S(2)}) copy-start(bf16[896,1024]{1,0:T(8,128)(2,1)} %copy-done.18) | copy-start | bytes 5505028
  234.1 15.2 %copy-start.22 = (bf16[512,2432]{1,0:T(8,128)(2,1)S(1)}, bf16[512,2432]{1,0:T(8,128)(2,1)}, u32[]{:S(2)}) copy-start(bf16[512,2432]{1,0:T(8,128)(2,1)} %all-gather.5.cloned.1.call-done) | copy-start | bytes 7471108
  249.4 3.3 copy-start.21
  252.2 7.0 %slice-start.4 = ((s8[4980736]{0:T(1024)(128)(4,1)}), s8[4194304]{0:T(1024)(128)(4,1)S(1)}, s32[]{:S(2)}) async-start(s8[4980736]{0:T(1024)(128)(4,1)} %bitcast.27), calls=%async_computation.6 | async-start | bytes 8388608
  252.2 21.8 %slice-start = ((s8[6291456]{0:T(1024)(128)(4,1)}), s8[2097152]{0:T(1024)(128)(4,1)S(1)}, s32[]{:S(2)}) async-start(s8[6291456]{0:T(1024)(128)(4,1)} %bitcast.23), calls=%async_computation.2 | async-start | bytes 4194304
  252.6 6.6 %slice-start.5 = ((s8[4980736]{0:T(1024)(128)(4,1)}), s8[786432]{0:T(1024)(128)(4,1)S(1)}, s32[]{:S(2)}) async-start(s8[4980736]{0:T(1024)(128)(4,1)} %bitcast.27), calls=%async_computation.7 | async-start | bytes 1572864
  252.6 21.4 %slice-start.1 = ((s8[6291456]{0:T(1024)(128)(4,1)}), s8[4194304]{0:T(1024)(128)(4,1)S(1)}, s32[]{:S(2)}) async-start(s8[6291456]{0:T(1024)(128)(4,1)} %bitcast.23), calls=%async_computation.3 | async-start | bytes 8388608
  252.7 37.7 %collective-permute-start.15 = (bf16[2432,512]{1,0:T(8,128)(2,1)S(1)}, bf16[2432,512]{1,0:T(8,128)(2,1)S(1)}, u32[]{:S(2)}, u32[]{:S(2)}) collective-permute-start(bf16[2432,512]{1,0:T(8,128)(2,1)S(1)} %slice.155), channel_id=1, source_target_pairs={{0,2},{2,0},{4,6},{6,4},{8,10},{10,8},{12,14},{14,12},{16,18},{18,... | collective-permute-start | bytes 7471112 | tf_op jit(solution)/shard_map/ppermute | solution.py:27
  267.8 4.3 %copy-start.14 = (bf16[3072,256]{1,0:T(8,128)(2,1)}, bf16[3072,256]{1,0:T(8,128)(2,1)S(1)}, u32[]{:S(2)}) copy-start(bf16[3072,256]{1,0:T(8,128)(2,1)S(1)} %collective-permute-done.24) | copy-start | bytes 4718596
  267.8 15.7 %collective-permute-start.25 = (bf16[128,2432]{1,0:T(8,128)(2,1)S(1)}, bf16[128,2432]{1,0:T(8,128)(2,1)S(1)}, u32[]{:S(2)}, u32[]{:S(2)}) collective-permute-start(bf16[128,2432]{1,0:T(8,128)(2,1)S(1)} %get-tuple-element.41), channel_id=1, source_target_pairs={{0,8},{2,10},{4,12},{6,14},{8,16},{10,18},{12,20},{14,22},{16,24},... | collective-permute-start | bytes 1867784 | tf_op jit(solution)/shard_map/ppermute | solution.py:35
  272.1 15.2 %collective-permute-start.26 = (bf16[128,2432]{1,0:T(8,128)(2,1)S(1)}, bf16[128,2432]{1,0:T(8,128)(2,1)S(1)}, u32[]{:S(2)}, u32[]{:S(2)}) collective-permute-start(bf16[128,2432]{1,0:T(8,128)(2,1)S(1)} %get-tuple-element.42), channel_id=1, source_target_pairs={{24,16},{26,18},{28,20},{30,22},{16,8},{18,10},{20,12},{22,14},{8,... | collective-permute-start | bytes 1867784 | tf_op jit(solution)/shard_map/ppermute | solution.py:35
  290.4 22.6 %collective-permute-start.18 = (bf16[128,1024]{1,0:T(8,128)(2,1)S(1)}, bf16[128,1024]{1,0:T(8,128)(2,1)S(1)}, u32[]{:S(2)}, u32[]{:S(2)}) collective-permute-start(bf16[128,1024]{1,0:T(8,128)(2,1)S(1)} %get-tuple-element.72), channel_id=1, source_target_pairs={{0,8},{2,10},{4,12},{6,14},{8,16},{10,18},{12,20},{14,22},{16,24},... | collective-permute-start | bytes 786440 | tf_op jit(solution)/shard_map/ppermute | solution.py:31
  291.0 22.0 %collective-permute-start.17 = (bf16[128,1024]{1,0:T(8,128)(2,1)S(1)}, bf16[128,1024]{1,0:T(8,128)(2,1)S(1)}, u32[]{:S(2)}, u32[]{:S(2)}) collective-permute-start(bf16[128,1024]{1,0:T(8,128)(2,1)S(1)} %get-tuple-element.74), channel_id=1, source_target_pairs={{0,16},{2,18},{4,20},{6,22},{8,24},{10,26},{12,28},{14,30},{16,0},... | collective-permute-start | bytes 786440 | tf_op jit(solution)/shard_map/ppermute | solution.py:31
  293.1 19.8 %collective-permute-start.16 = (bf16[128,1024]{1,0:T(8,128)(2,1)S(1)}, bf16[128,1024]{1,0:T(8,128)(2,1)S(1)}, u32[]{:S(2)}, u32[]{:S(2)}) collective-permute-start(bf16[128,1024]{1,0:T(8,128)(2,1)S(1)} %get-tuple-element.75), channel_id=1, source_target_pairs={{0,24},{2,26},{4,28},{6,30},{8,0},{10,2},{12,4},{14,6},{16,8},{18,... | collective-permute-start | bytes 786440 | tf_op jit(solution)/shard_map/ppermute | solution.py:31
  297.6 37.3 %collective-permute-start.27 = (bf16[2432,256]{1,0:T(8,128)(2,1)}, bf16[2432,256]{1,0:T(8,128)(2,1)}, u32[]{:S(2)}, u32[]{:S(2)}) collective-permute-start(bf16[2432,256]{1,0:T(8,128)(2,1)} %slice.157), channel_id=1, source_target_pairs={{0,4},{2,6},{4,0},{6,2},{8,12},{10,14},{12,8},{14,10},{16,20},{18,... | collective-permute-start | bytes 3735560 | tf_op jit(solution)/shard_map/ppermute | solution.py:27
  317.9 14.0 %collective-permute-start.19 = (bf16[128,2048]{0,1:T(8,128)(2,1)S(1)}, bf16[128,2048]{0,1:T(8,128)(2,1)S(1)}, u32[]{:S(2)}, u32[]{:S(2)}) collective-permute-start(bf16[128,2048]{0,1:T(8,128)(2,1)S(1)} %dynamic-slice_bitcast_fusion), channel_id=1, source_target_pairs={{0,1},{1,0},{2,3},{3,2},{4,5},{5,4},{6,7},{7,6},{8,9},{9,8},{10,11... | collective-permute-start | bytes 1572872 | tf_op jit(solution)/shard_map/ppermute | solution.py:40
  (11 other events, 23.3 us)
Sparse Core Ops, SparseCore 0:
  12.5 82.9 all-gather.2
  97.1 81.0 all-gather.4

commit v6 on v0

v6 whole, which is shorter than its diff:
```python
import jax
import jax.numpy as jnp
from jax import lax
from jax.sharding import PartitionSpec as P

QUAD = 4
ORDER = (0, 2, 1, 3)
KEEP_COLS = (((1,), (1,)), ((), ()))
SUM_ROWS = (((0,), (0,)), ((), ()))


def after(value, *others):
    return lax.optimization_barrier((value,) + others)[0] if others else value


def slot_of(near):
    return [((near ^ block) & 1) << 1 | (near ^ block) >> 1 for block in range(QUAD)]


def picked(view, places, axis):
    return jnp.concatenate(
        [lax.dynamic_slice_in_dim(view, place, 1, axis=axis) for place in places], axis=axis
    )


def solution(mesh):
    n_hst, n_local = mesh.shape["hst"], mesh.shape["local"]
    n_far = n_hst // QUAD
    last_hop = n_far - 1

    def swap(value, bit):
        return lax.ppermute(value, "hst", [(h, h ^ bit) for h in range(n_hst)])

    def shift(value, step):
        pairs = [(h, (h + step * QUAD) % n_hst) for h in range(n_hst)]
        return lax.ppermute(value, "hst", pairs)

    def hop(value, way, sources):
        pairs = [(s * QUAD + q, (s + way) * QUAD + q) for s in sources for q in range(QUAD)]
        return lax.ppermute(value, "hst", pairs)

    def both_ways(up, down, sources):
        return hop(up, 1, sources), hop(down, -1, [n_far - 1 - z for z in sources])

    def local_shift(value, step):
        return lax.ppermute(value, "local", [(i, (i + step) % n_local) for i in range(n_local)])

    def on_device(gate_act, up_act, cotangent, down_weight):
        h = lax.axis_index("hst")
        x = lax.axis_index("local")
        far, near = h // QUAD, h % QUAD
        tokens, half = cotangent.shape
        width = down_weight.shape[1]
        columns = QUAD * width
        hidden_units = gate_act.shape[1]
        per_half = half // columns
        middle = 128 * ((hidden_units // 128 + 1) // 2)
        bounds = [(0, middle), (middle, hidden_units)]

        fence = []

        def move(send, value, *args):
            return send(after(value, *fence), *args)

        hidden, wide = [], []
        for lo, hi in bounds:
            gate_wide = gate_act[:, lo:hi].astype(jnp.float32)
            up_wide = up_act[:, lo:hi].astype(jnp.float32)
            sigmoid_gate = jax.nn.sigmoid(gate_wide)
            wide.append((gate_wide, up_wide, sigmoid_gate))
            hidden.append((gate_wide * sigmoid_gate * up_wide).astype(jnp.bfloat16))

        above, below = ({}, {}), ({}, {})
        travel = {}

        def gather_hop(f, j):
            up, down = travel.get(("A", f), (hidden[f], hidden[f]))
            up, down = (after(up, *fence), after(down, *fence))
            up, down = travel["A", f] = both_ways(up, down, range(j - 1, n_far - 1))
            below[f][j], above[f][j] = up, down
            return [up, down]

        def reduce_hop(f, j):
            d = n_far - j
            up_term, down_term = terms[f][d], terms[f][n_far - d]
            if j > 1:
                up, down = travel["R", f]
                up_term = up_term + up.astype(jnp.float32)
                down_term = down_term + down.astype(jnp.float32)
            up, down = after(up_term.astype(jnp.bfloat16), *fence), after(
                down_term.astype(jnp.bfloat16), *fence
            )
            travel["R", f] = both_ways(up, down, range(0, j))
            return list(travel["R", f])

        def weight_columns(f, other):
            lo, hi = bounds[f]
            pair = jnp.concatenate([down_weight[lo:hi], other], axis=1)
            return jnp.concatenate([pair, move(swap, pair, 1)], axis=1)

        def reduce_terms(f):
            dots = lax.dot_general(
                cot_rows, weights[f], KEEP_COLS, preferred_element_type=jnp.float32
            )
            return [dots[e * tokens : (e + 1) * tokens] for e in range(n_far)]

        def gathered_rows(f):
            slots = [hidden[f]]
            for e in range(1, n_far):
                slots.append(jnp.where(far + e < n_far, above[f][e], below[f][n_far - e]))
            return jnp.concatenate(slots, axis=0)

        def grad_terms(f):
            keep, give = (
                lax.dot_general(rows[f], part, SUM_ROWS, preferred_element_type=jnp.float32)
                for part in (cot_rows[:, : 2 * width], cot_rows[:, 2 * width :])
            )
            theirs = move(swap, give.astype(jnp.bfloat16), 1).astype(jnp.float32)
            return (
                keep[:, :width] + theirs[:, :width],
                (keep[:, width:] + theirs[:, width:]).astype(jnp.bfloat16),
            )

        weights, terms, rows, out_sums, grads = {}, {}, {}, {}, {}

        own_cot = picked(
            cotangent.reshape(tokens, per_half, QUAD, width), [near ^ k for k in ORDER], 2
        ).reshape(tokens, half)
        parts = [own_cot] + [local_shift(own_cot, n_local - s) for s in range(1, n_local)]
        weight_side = swap(down_weight[:middle], 2)
        fence = gather_hop(0, 1) + parts[1:]

        cot_slots = jnp.concatenate(parts, axis=1)

        def cot_for(step):
            place = (far + step) % n_far
            start = (place // per_half - x) % n_local * half + place % per_half * columns
            return lax.dynamic_slice_in_dim(cot_slots, start, columns, axis=1)

        came = [move(shift, cot_for(n_far - e), n_far - e) for e in range(1, n_far)]
        cot_rows = jnp.concatenate([cot_for(0)] + came, axis=0)
        fence = came + [weight_side, hidden[1]]

        for j in range(2, n_far):
            waits = gather_hop(0, j)
            if j == 2:
                weights[0] = weight_columns(0, weight_side)
                weight_side = move(swap, down_weight[middle:], 2)
                terms[0] = reduce_terms(0)
                waits += [terms[0][last_hop]]
            if j == last_hop:
                waits += reduce_hop(0, 1) + [weight_side]
            fence = waits

        waits = gather_hop(1, 1)
        weights[1] = weight_columns(1, weight_side)
        terms[1] = reduce_terms(1)
        rows[0] = gathered_rows(0)
        grads[0] = grad_terms(0)
        fence = waits + [terms[1][last_hop], grads[0][1]]

        for j in range(2, n_far):
            waits = gather_hop(1, j)
            if j == 2:
                waits += reduce_hop(1, 1)
                grad_side = move(swap, grads[0][1], 2)
                out_sums[0] = jnp.dot(rows[0], weights[0], preferred_element_type=jnp.float32)
                waits += [out_sums[0]]
            else:
                waits += reduce_hop(0, j - 1)
            if j == last_hop:
                waits += [grad_side]
            fence = waits
        grad_parts = [grads[0][0] + grad_side.astype(jnp.float32)]

        waits = reduce_hop(1, 2)
        rows[1] = gathered_rows(1)
        grads[1] = grad_terms(1)
        out_terms = (
            out_sums[0] + jnp.dot(rows[1], weights[1], preferred_element_type=jnp.float32)
        ).astype(jnp.bfloat16)
        fence = waits + [grads[1][1], out_terms]

        waits = reduce_hop(0, last_hop)
        grad_side = move(swap, grads[1][1], 2)
        outs = [out_terms[:tokens]] + [
            move(shift, out_terms[e * tokens : (e + 1) * tokens], e) for e in range(1, n_far)
        ]
        fence = waits + outs[1:]

        up_parts, gate_parts = [], []

        def reduced(f):
            up, down = travel["R", f]
            hidden_grad = terms[f][0] + up.astype(jnp.float32) + down.astype(jnp.float32)
            gate_wide, up_wide, sigmoid_gate = wide[f]
            up_parts.append((hidden_grad * gate_wide * sigmoid_gate).astype(jnp.bfloat16))
            gate_parts.append(
                (
                    hidden_grad * up_wide * sigmoid_gate * (1.0 + gate_wide * (1.0 - sigmoid_gate))
                ).astype(jnp.bfloat16)
            )

        reduced(0)
        out_slots = jnp.concatenate(outs, axis=1)

        def half_of(step):
            first = (x + step) % n_local * per_half
            starts = [(far - first - q) % n_far * columns for q in range(per_half)]
            return jnp.concatenate(
                [lax.dynamic_slice_in_dim(out_slots, s, columns, axis=1) for s in starts], axis=1
            )

        for j in range(3, n_far):
            waits = reduce_hop(1, j)
            if j == 3:
                sides = [move(local_shift, half_of(step), step) for step in range(1, n_local)]
            fence = waits
        reduced(1)
        output = half_of(0).astype(jnp.float32)
        for side in sides:
            output = output + side.astype(jnp.float32)
        output = output.astype(jnp.bfloat16).reshape(tokens, per_half, QUAD, width)
        grad_parts.append(grads[1][0] + grad_side.astype(jnp.float32))
        return (
            picked(output, slot_of(near), 2).reshape(tokens, half),
            jnp.concatenate(gate_parts, axis=1),
            jnp.concatenate(up_parts, axis=1),
            jnp.concatenate(grad_parts, axis=0),
        )

    specs = (P("hst", "local"), P("hst", "local"), P("hst", "local"), P("local", "hst"))
    return jax.shard_map(
        on_device, mesh=mesh, in_specs=specs, out_specs=specs, check_vma=False
    )
```

time: 1130 us -> 294 us (0.26)
  waiting for transfers between devices: 1040 us -> 120 us
  starting transfers between devices: 0.16 us -> 69.3 us
  other arithmetic: 2.25 us -> 47 us
  matrix products: 76.8 us -> 40.7 us
  local copies, waits for them, and re-layouts: 0.01 us -> 13.9 us
  between operations: 13.8 us -> 1.46 us
    reduce_scatter x2 -> x0, waiting for transfers between devices: 798 us -> none  [the longest x1 798 us: on_device(): lax.psum_scatter(weight_terms, 'hst', scatter_dimension=1, tiled=True)]
    all_gather x2 -> x0, waiting for transfers between devices: 237 us -> none  [the longest x1 233 us: on_device(): weight_rows = lax.all_gather(down_weight, 'hst', axis=1, tiled=True)]
    ppermute x0 -> x40, waiting for transfers between devices: none -> 120 us  [the longest x24 74.1 us: hop(): return lax.ppermute(value, 'hst', pairs)]
    ppermute x0 -> x40, starting transfers between devices: none -> 69.3 us  [the longest x24 54.8 us: hop(): return lax.ppermute(value, 'hst', pairs)]
    dot_general x3 -> x8, matrix products: 76.8 us -> 40.7 us  [the longest x4 15.3 us: grad_terms(): lax.dot_general(rows[f], part, SUM_ROWS, preferred_element_type=jnp.float32)]
    convert_element_type x1 -> x13, other arithmetic: 2.25 us -> 26 us  [the longest x2 7 us: grad_terms(): theirs = move(swap, give.astype(jnp.bfloat16), 1).astype(jnp.float32)]
    concatenate x0 -> x9, other arithmetic: none -> 11.6 us  [the longest x2 3.36 us: weight_columns(): pair = jnp.concatenate([down_weight[lo:hi], other], axis=1)]
  transfers between devices with their start and end apart: 4 -> 40, of which waited for: 3 -> 21; matrix products, arithmetic and copies ran while one was open for 7% -> 31% of each run, Pallas kernels for 0% -> 0%
where the time goes in v6:
time: 294 us; the launch traced here: 292 us
  waiting for transfers between devices  120 us (41%)
  starting transfers between devices  69.3 us (24%)
  other arithmetic  47 us (16%)
  matrix products  40.7 us (14%)
  local copies, waits for them, and re-layouts  13.9 us (5%)
    ppermute x24, waiting for transfers between devices, hop(): return lax.ppermute(value, 'hst', pairs)  74.1 us
    ppermute x24, starting transfers between devices, hop(): return lax.ppermute(value, 'hst', pairs)  54.8 us
    ppermute x8, waiting for transfers between devices, swap(): return lax.ppermute(value, 'hst', [(h, h ^ bit) for h in range(n_hst)])  18.5 us
    dot_general x4, matrix products, grad_terms(): lax.dot_general(rows[f], part, SUM_ROWS, preferred_element_type=jnp.float32)  15.3 us
    ppermute x2, waiting for transfers between devices, local_shift(): lax.ppermute(value, 'local', [(i, (i + step) % n_local) for i in range(n_...  14.4 us
    ppermute x6, waiting for transfers between devices, shift(): return lax.ppermute(value, 'hst', pairs)  12.6 us
    dot_general x2, matrix products, reduce_terms(): lax.dot_general(cot_rows, weights[f], KEEP_COLS, preferred_element_type=j...  10.3 us
    dot_general x1, matrix products, on_device(): jnp.dot(rows[1], weights[1], preferred_element_type=jnp.float32)  8.07 us
  transfers between devices with their start and end apart: 40, of which 21 were waited for; matrix products, arithmetic and copies ran while one was open for 31% of the time, Pallas kernels for 0%

profile of v6, /device:TPU:8, one launch (start us, length us, event | category | flops | bytes accessed | tf_op | source)
XLA Modules:
  0.0 292.1 jit_solution(6945682047551754350)
XLA Ops:
  0.6 2.7 fusion.8
  3.3 3.5 %collective-permute-start.1 = (bf16[128,2816]{1,0:T(8,128)(2,1)}, bf16[128,2816]{1,0:T(8,128)(2,1)}, u32[]{:S(2)}, u32[]{:S(2)}) collective-permute-start(bf16[128,2816]{1,0:T(8,128)(2,1)} %fusion.8), channel_id=1, source_target_pairs={{0,8},{2,10},{4,12},{6,14},{8,16},{10,18},{12,20},{14,22},{16,24},... | collective-permute-start | bytes 2162696 | tf_op jit(solution)/shard_map/ppermute | solution.py:40
  6.8 3.2 %collective-permute-start = (bf16[128,2816]{1,0:T(8,128)(2,1)}, bf16[128,2816]{1,0:T(8,128)(2,1)}, u32[]{:S(2)}, u32[]{:S(2)}) collective-permute-start(bf16[128,2816]{1,0:T(8,128)(2,1)} %fusion.8), channel_id=1, source_target_pairs={{24,16},{26,18},{28,20},{30,22},{16,8},{18,10},{20,12},{22,14},{8,... | collective-permute-start | bytes 2162696 | tf_op jit(solution)/shard_map/ppermute | solution.py:40
  17.7 2.6 fusion.19
  20.4 8.7 %collective-permute-done.2 = bf16[128,2048]{1,0:T(8,128)(2,1)S(1)} collective-permute-done((bf16[128,2048]{1,0:T(8,128)(2,1)S(1)}, bf16[128,2048]{1,0:T(8,128)(2,1)S(1)}, u32[]{:S(2)}, u32[]{:S(2)}) %collective-permute-start.2) | collective-permute-done | bytes 524320 | tf_op jit(solution)/shard_map/ppermute | solution.py:46
  29.3 2.6 collective-permute-start.4
  31.9 2.8 collective-permute-start.5
  34.8 9.6 %collective-permute-done.6 = bf16[2816,256]{1,0:T(8,128)(2,1)} collective-permute-done((bf16[2816,256]{1,0:T(8,128)(2,1)S(1)}, bf16[2816,256]{1,0:T(8,128)(2,1)}, u32[]{:S(2)}, u32[]{:S(2)}) %collective-permute-start.6) | collective-permute-done | bytes 1441824 | tf_op jit(solution)/shard_map/ppermute | solution.py:32
  44.4 3.1 %pad_maximum_fusion.3 = bf16[2816,512]{1,0:T(8,128)(2,1)} fusion(bf16[2816,256]{1,0:T(8,128)(2,1)} %collective-permute-done.6, bf16[2816,256]{1,0:T(8,128)(2,1)S(1)} %slice.90), kind=kLoop, calls=%fused_computation.9 | loop fusion | flops 5767168 | bytes 5767168 | tf_op jit(solution)/shard_map/concatenate | solution.py:98
  49.4 3.3 %collective-permute-done.5 = bf16[128,1024]{1,0:T(8,128)(2,1)S(1)} collective-permute-done((bf16[128,1024]{1,0:T(8,128)(2,1)S(1)}, bf16[128,1024]{1,0:T(8,128)(2,1)S(1)}, u32[]{:S(2)}, u32[]{:S(2)}) %collective-permute-start.5) | collective-permute-done | bytes 262176 | tf_op jit(solution)/shard_map/ppermute | solution.py:36
  56.0 4.4 %collective-permute-start.7 = (bf16[128,2816]{1,0:T(8,128)(2,1)}, bf16[128,2816]{1,0:T(8,128)(2,1)S(1)}, u32[]{:S(2)}, u32[]{:S(2)}) collective-permute-start(bf16[128,2816]{1,0:T(8,128)(2,1)} %collective-permute-done.1), channel_id=1, source_target_pairs={{8,16},{10,18},{12,20},{14,22},{16,24},{18,26},{20,28},{22,30},{9,... | collective-permute-start | bytes 2162696 | tf_op jit(solution)/shard_map/ppermute | solution.py:40
  63.0 5.4 %fusion.5 = f32[512,2816]{1,0:T(8,128)S(1)} fusion(bf16[2816,512]{1,0:T(8,128)(2,1)} %collective-permute-done.9, bf16[2816,256]{1,0:T(8,128)(2,1)} %collective-permute-done.6, bf16[2816,256]{1,0:T(8,128)(2,1)S(1)} %slice.90, bf16[128,1024]{1,0:T(8,128)(2,1)} %copy-done.27, bf16[128,1024]{1,0:T(8,128)(2,1)} %copy-done.25, ...), kind=kOutput, calls=%fused_computation.26 | convolution fusion | flops 2974285824 | bytes 12582912 | tf_op jit(solution)/shard_map/dot_general | solution.py:102
  68.5 7.6 %collective-permute-done.7 = bf16[128,2816]{1,0:T(8,128)(2,1)S(1)} collective-permute-done((bf16[128,2816]{1,0:T(8,128)(2,1)}, bf16[128,2816]{1,0:T(8,128)(2,1)S(1)}, u32[]{:S(2)}, u32[]{:S(2)}) %collective-permute-start.7) | collective-permute-done | bytes 720928 | tf_op jit(solution)/shard_map/ppermute | solution.py:40
  76.1 4.1 %collective-permute-done.8 = bf16[128,2816]{1,0:T(8,128)(2,1)S(1)} collective-permute-done((bf16[128,2816]{1,0:T(8,128)(2,1)}, bf16[128,2816]{1,0:T(8,128)(2,1)S(1)}, u32[]{:S(2)}, u32[]{:S(2)}) %collective-permute-start.8) | collective-permute-done | bytes 720928 | tf_op jit(solution)/shard_map/ppermute | solution.py:40
  80.9 2.2 collective-permute-start.11
  85.2 8.9 %collective-permute-done.14 = bf16[2688,256]{1,0:T(8,128)(2,1)S(1)} collective-permute-done((bf16[2688,256]{1,0:T(8,128)(2,1)S(1)}, bf16[2688,256]{1,0:T(8,128)(2,1)S(1)}, u32[]{:S(2)}, u32[]{:S(2)}) %collective-permute-start.14) | collective-permute-done | bytes 1376288 | tf_op jit(solution)/shard_map/ppermute | solution.py:32
  94.3 3.2 %collective-permute-done.11 = bf16[128,2816]{1,0:T(8,128)(2,1)S(1)} collective-permute-done((bf16[128,2816]{1,0:T(8,128)(2,1)S(1)}, bf16[128,2816]{1,0:T(8,128)(2,1)S(1)}, u32[]{:S(2)}, u32[]{:S(2)}) %collective-permute-start.11) | collective-permute-done | bytes 720928 | tf_op jit(solution)/shard_map/ppermute | solution.py:40
  97.5 4.2 %collective-permute-done.12 = bf16[128,2816]{1,0:T(8,128)(2,1)S(1)} collective-permute-done((bf16[128,2816]{1,0:T(8,128)(2,1)S(1)}, bf16[128,2816]{1,0:T(8,128)(2,1)S(1)}, u32[]{:S(2)}, u32[]{:S(2)}) %collective-permute-start.12) | collective-permute-done | bytes 720928 | tf_op jit(solution)/shard_map/ppermute | solution.py:40
  103.6 5.0 %collective-permute-start.15 = (bf16[128,2688]{1,0:T(8,128)(2,1)}, bf16[128,2688]{1,0:T(8,128)(2,1)}, u32[]{:S(2)}, u32[]{:S(2)}) collective-permute-start(bf16[128,2688]{1,0:T(8,128)(2,1)} %fusion.19), channel_id=1, source_target_pairs={{24,16},{26,18},{28,20},{30,22},{16,8},{18,10},{20,12},{22,14},{8,... | collective-permute-start | bytes 2064392 | tf_op jit(solution)/shard_map/ppermute | solution.py:40
  111.1 4.4 %convolution_convert_fusion.1 = bf16[2816,512]{1,0:T(8,128)(2,1)} fusion(bf16[512,1024]{1,0:T(8,128)(2,1)S(1)} %pad_maximum_fusion.15, bf16[128,2816]{1,0:T(8,128)(2,1)S(1)} %broadcast_select_fusion, bf16[128,2816]{1,0:T(8,128)(2,1)S(1)} %broadcast_select_fusion.1, bf16[128,2816]{1,0:T(8,128)(2,1)S(1)} %broadcast_select_fusion.2, bf16[128,2816]{1,0:T(8,128)(2,1)} %fusion.8), kind=kOutput, calls=%fused_computation.4 | convolution fusion | flops 1489371136 | bytes 6291456 | tf_op jit(solution)/shard_map/dot_general | solution.py:115
  116.0 2.8 fusion.34
  118.8 6.9 %fusion.4 = f32[512,1024]{1,0:T(8,128)} fusion(bf16[2816,512]{1,0:T(8,128)(2,1)} %collective-permute-done.9, bf16[2816,256]{1,0:T(8,128)(2,1)} %collective-permute-done.6, bf16[2816,256]{1,0:T(8,128)(2,1)S(1)} %slice.90, bf16[128,2816]{1,0:T(8,128)(2,1)S(1)} %broadcast_select_fusion, bf16[128,2816]{1,0:T(8,128)(2,1)S(1)} %broadcast_select_fusion.1, ...), kind=kOutput, calls=%fused_computation.25 | convolution fusion | flops 2981625856 | bytes 10747904 | tf_op jit(solution)/shard_map/dot_general | solution.py:167
  125.8 5.0 %fusion.7 = f32[512,2688]{1,0:T(8,128)S(1)} fusion(bf16[2688,512]{1,0:T(8,128)(2,1)} %collective-permute-done.17, bf16[2688,256]{1,0:T(8,128)(2,1)S(1)} %collective-permute-done.14, bf16[2688,256]{1,0:T(8,128)(2,1)S(1)} %slice.95, bf16[128,1024]{1,0:T(8,128)(2,1)S(1)} %copy-done.28, bf16[128,1024]{1,0:T(8,128)(2,1)S(1)} %copy-done.26, ...), kind=kOutput, calls=%fused_computation.28 | convolution fusion | flops 2839281664 | bytes 12058624 | tf_op jit(solution)/shard_map/dot_general | solution.py:102
  130.9 4.4 %convert_element_type.147 = f32[2816,512]{1,0:T(8,128)S(1)} convert(bf16[2816,512]{1,0:T(8,128)(2,1)} %collective-permute-done.18) | non-fusion elementwise | flops 1441792 | bytes 8650752 | tf_op jit(solution)/shard_map/convert_element_type | solution.py:118
  142.3 10.6 %collective-permute-done.19 = bf16[128,2688]{1,0:T(8,128)(2,1)S(1)} collective-permute-done((bf16[128,2688]{1,0:T(8,128)(2,1)}, bf16[128,2688]{1,0:T(8,128)(2,1)S(1)}, u32[]{:S(2)}, u32[]{:S(2)}) %collective-permute-start.19) | collective-permute-done | bytes 688160 | tf_op jit(solution)/shard_map/ppermute | solution.py:40
  153.0 4.0 %collective-permute-done.20 = bf16[128,2688]{1,0:T(8,128)(2,1)S(1)} collective-permute-done((bf16[128,2688]{1,0:T(8,128)(2,1)}, bf16[128,2688]{1,0:T(8,128)(2,1)S(1)}, u32[]{:S(2)}, u32[]{:S(2)}) %collective-permute-start.20) | collective-permute-done | bytes 688160 | tf_op jit(solution)/shard_map/ppermute | solution.py:40
  160.9 4.4 %collective-permute-start.25 = (bf16[128,2816]{1,0:T(8,128)(2,1)S(1)}, bf16[128,2816]{1,0:T(8,128)(2,1)S(1)}, u32[]{:S(2)}, u32[]{:S(2)}) collective-permute-start(bf16[128,2816]{1,0:T(8,128)(2,1)S(1)} %get-tuple-element.59), channel_id=1, source_target_pairs={{0,8},{2,10},{4,12},{6,14},{8,16},{10,18},{12,20},{14,22},{1,9},{3... | collective-permute-start | bytes 2162696 | tf_op jit(solution)/shard_map/ppermute | solution.py:40
  169.8 5.2 %collective-permute-done.24 = bf16[128,2688]{1,0:T(8,128)(2,1)S(1)} collective-permute-done((bf16[128,2688]{1,0:T(8,128)(2,1)S(1)}, bf16[128,2688]{1,0:T(8,128)(2,1)S(1)}, u32[]{:S(2)}, u32[]{:S(2)}) %collective-permute-start.24) | collective-permute-done | bytes 688160 | tf_op jit(solution)/shard_map/ppermute | solution.py:40
  176.2 4.5 %convolution_convert_fusion = bf16[2688,512]{1,0:T(8,128)(2,1)} fusion(bf16[512,1024]{1,0:T(8,128)(2,1)S(1)} %copy-done.11, bf16[128,2688]{1,0:T(8,128)(2,1)S(1)} %broadcast_select_fusion.3, bf16[128,2688]{1,0:T(8,128)(2,1)S(1)} %broadcast_select_fusion.4, bf16[128,2688]{1,0:T(8,128)(2,1)S(1)} %broadcast_select_fusion.5, bf16[128,2688]{1,0:T(8,128)(2,1)} %fusion.19), kind=kOutput, calls=%fused_computation.3 | convolution fusion | flops 1421672448 | bytes 6029312 | tf_op jit(solution)/shard_map/dot_general | solution.py:115
  180.8 2.9 %collective-permute-done.26 = bf16[128,2816]{1,0:T(8,128)(2,1)S(1)} collective-permute-done((bf16[128,2816]{1,0:T(8,128)(2,1)S(1)}, bf16[128,2816]{1,0:T(8,128)(2,1)S(1)}, u32[]{:S(2)}, u32[]{:S(2)}) %collective-permute-start.26) | collective-permute-done | bytes 720928 | tf_op jit(solution)/shard_map/ppermute | solution.py:40
  184.6 8.1 %add_convert_fusion = bf16[512,1024]{1,0:T(8,128)(2,1)} fusion(f32[512,1024]{1,0:T(8,128)} %fusion.4, bf16[2688,512]{1,0:T(8,128)(2,1)} %collective-permute-done.17, bf16[2688,256]{1,0:T(8,128)(2,1)} %copy-done.9, bf16[2688,256]{1,0:T(8,128)(2,1)S(1)} %slice.95, bf16[128,2688]{1,0:T(8,128)(2,1)} %copy-done.23, ...), kind=kOutput, calls=%fused_computation.29 | convolution fusion | flops 2847145984 | bytes 11403264 | tf_op jit(solution)/shard_map/dot_general | solution.py:180
  192.6 2.1 fusion.42
  194.7 3.6 %fusion.32 = f32[2688,512]{1,0:T(8,128)S(1)} fusion(bf16[512,1024]{1,0:T(8,128)(2,1)} %copy-done.10, bf16[128,2688]{1,0:T(8,128)(2,1)} %copy-done.23, bf16[128,2688]{1,0:T(8,128)(2,1)} %copy-done.21, bf16[128,2688]{1,0:T(8,128)(2,1)} %copy-done.22, bf16[128,2688]{1,0:T(8,128)(2,1)} %fusion.19), kind=kOutput, calls=%fused_computation.84 | convolution fusion | flops 1420296192 | bytes 8781824 | tf_op jit(solution)/shard_map/dot_general | solution.py:115
  199.4 2.2 collective-permute-start.28
  203.8 2.6 convert_element_type.161
  209.2 9.9 %collective-permute-done.28 = bf16[128,2688]{1,0:T(8,128)(2,1)} collective-permute-done((bf16[128,2688]{1,0:T(8,128)(2,1)}, bf16[128,2688]{1,0:T(8,128)(2,1)}, u32[]{:S(2)}, u32[]{:S(2)}) %collective-permute-start.28) | collective-permute-done | bytes 688160 | tf_op jit(solution)/shard_map/ppermute | solution.py:40
  219.1 10.4 %collective-permute-done.29 = bf16[128,2688]{1,0:T(8,128)(2,1)} collective-permute-done((bf16[128,2688]{1,0:T(8,128)(2,1)}, bf16[128,2688]{1,0:T(8,128)(2,1)}, u32[]{:S(2)}, u32[]{:S(2)}) %collective-permute-start.29) | collective-permute-done | bytes 688160 | tf_op jit(solution)/shard_map/ppermute | solution.py:40
  231.5 2.6 add_convert_fusion.6
  234.2 3.6 %collective-permute-start.34 = (bf16[128,2816]{1,0:T(8,128)(2,1)S(1)}, bf16[128,2816]{1,0:T(8,128)(2,1)S(1)}, u32[]{:S(2)}, u32[]{:S(2)}) collective-permute-start(bf16[128,2816]{1,0:T(8,128)(2,1)S(1)} %copy-done.16), channel_id=1, source_target_pairs={{0,8},{2,10},{4,12},{6,14},{8,16},{10,18},{12,20},{14,22},{16,24},... | collective-permute-start | bytes 2162696 | tf_op jit(solution)/shard_map/ppermute | solution.py:40
  237.8 2.5 collective-permute-start.35
  240.9 6.6 %collective-permute-done.32 = bf16[128,1024]{1,0:T(8,128)(2,1)S(1)} collective-permute-done((bf16[128,1024]{1,0:T(8,128)(2,1)S(1)}, bf16[128,1024]{1,0:T(8,128)(2,1)S(1)}, u32[]{:S(2)}, u32[]{:S(2)}) %collective-permute-start.32) | collective-permute-done | bytes 262176 | tf_op jit(solution)/shard_map/ppermute | solution.py:36
  248.6 9.8 %collective-permute-done.34 = bf16[128,2816]{1,0:T(8,128)(2,1)S(1)} collective-permute-done((bf16[128,2816]{1,0:T(8,128)(2,1)S(1)}, bf16[128,2816]{1,0:T(8,128)(2,1)S(1)}, u32[]{:S(2)}, u32[]{:S(2)}) %collective-permute-start.34) | collective-permute-done | bytes 720928 | tf_op jit(solution)/shard_map/ppermute | solution.py:40
  258.9 4.0 %collective-permute-start.37 = (bf16[128,2688]{1,0:T(8,128)(2,1)}, bf16[128,2688]{1,0:T(8,128)(2,1)}, u32[]{:S(2)}, u32[]{:S(2)}) collective-permute-start(bf16[128,2688]{1,0:T(8,128)(2,1)} %get-tuple-element.71), channel_id=1, source_target_pairs={{0,8},{2,10},{4,12},{6,14},{8,16},{10,18},{12,20},{14,22},{16,24},... | collective-permute-start | bytes 2064392 | tf_op jit(solution)/shard_map/ppermute | solution.py:40
  262.8 3.0 %collective-permute-start.38 = (bf16[128,2688]{1,0:T(8,128)(2,1)}, bf16[128,2688]{1,0:T(8,128)(2,1)}, u32[]{:S(2)}, u32[]{:S(2)}) collective-permute-start(bf16[128,2688]{1,0:T(8,128)(2,1)} %get-tuple-element.72), channel_id=1, source_target_pairs={{24,16},{26,18},{28,20},{30,22},{16,8},{18,10},{20,12},{22,14},{8,... | collective-permute-start | bytes 2064392 | tf_op jit(solution)/shard_map/ppermute | solution.py:40
  269.4 5.7 %collective-permute-done.36 = bf16[128,2048]{1,0:T(8,128)(2,1)S(1)} collective-permute-done((bf16[128,2048]{1,0:T(8,128)(2,1)S(1)}, bf16[128,2048]{1,0:T(8,128)(2,1)S(1)}, u32[]{:S(2)}, u32[]{:S(2)}) %collective-permute-start.36) | collective-permute-done | bytes 524320 | tf_op jit(solution)/shard_map/ppermute | solution.py:46
  280.9 3.4 %fusion.2 = f32[2688,256]{1,0:T(8,128)S(1)} fusion(f32[2688,512]{1,0:T(8,128)} %copy-done, f32[2688,512]{1,0:T(8,128)} %copy-done.4, bf16[2688,256]{1,0:T(8,128)(2,1)} %collective-permute-done.39), kind=kLoop, calls=%fused_computation.12 | loop fusion | flops 2064384 | bytes 9633792 | tf_op jit(solution)/shard_map/add | solution.py:224
  284.4 2.9 pad_maximum_fusion.1
  287.2 3.1 %fusion.28 = (bf16[128,2688]{1,0:T(8,128)(2,1)S(1)}, bf16[128,2688]{1,0:T(8,128)(2,1)S(1)}) fusion(bf16[128,5504]{1,0:T(8,128)(2,1)} %param.4, bf16[128,2688]{1,0:T(8,128)(2,1)} %collective-permute-done.38, bf16[128,2688]{1,0:T(8,128)(2,1)} %collective-permute-done.37, f32[512,2688]{1,0:T(8,128)} %copy-done.1, bf16[128,5504]{1,0:T(8,128)(2,1)} %param.5), kind=kLoop, calls=%fused_computation.61 | loop fusion | flops 6537216 | bytes 5505024 | tf_op jit(solution)/shard_map/convert_element_type | solution.py:197
  (147 shorter events, 62.2 us)
Async XLA Ops:
  3.3 25.9 %collective-permute-start.1 = (bf16[128,2816]{1,0:T(8,128)(2,1)}, bf16[128,2816]{1,0:T(8,128)(2,1)}, u32[]{:S(2)}, u32[]{:S(2)}) collective-permute-start(bf16[128,2816]{1,0:T(8,128)(2,1)} %fusion.8), channel_id=1, source_target_pairs={{0,8},{2,10},{4,12},{6,14},{8,16},{10,18},{12,20},{14,22},{16,24},... | collective-permute-start | bytes 2162696 | tf_op jit(solution)/shard_map/ppermute | solution.py:40
  6.8 22.4 %collective-permute-start = (bf16[128,2816]{1,0:T(8,128)(2,1)}, bf16[128,2816]{1,0:T(8,128)(2,1)}, u32[]{:S(2)}, u32[]{:S(2)}) collective-permute-start(bf16[128,2816]{1,0:T(8,128)(2,1)} %fusion.8), channel_id=1, source_target_pairs={{24,16},{26,18},{28,20},{30,22},{16,8},{18,10},{20,12},{22,14},{8,... | collective-permute-start | bytes 2162696 | tf_op jit(solution)/shard_map/ppermute | solution.py:40
  11.5 32.9 %collective-permute-start.6 = (bf16[2816,256]{1,0:T(8,128)(2,1)S(1)}, bf16[2816,256]{1,0:T(8,128)(2,1)}, u32[]{:S(2)}, u32[]{:S(2)}) collective-permute-start(bf16[2816,256]{1,0:T(8,128)(2,1)S(1)} %slice.90), channel_id=1, source_target_pairs={{0,4},{2,6},{4,0},{6,2},{8,12},{10,14},{12,8},{14,10},{16,20},{18,... | collective-permute-start | bytes 4325384 | tf_op jit(solution)/shard_map/ppermute | solution.py:32
  16.2 12.9 %collective-permute-start.2 = (bf16[128,2048]{1,0:T(8,128)(2,1)S(1)}, bf16[128,2048]{1,0:T(8,128)(2,1)S(1)}, u32[]{:S(2)}, u32[]{:S(2)}) collective-permute-start(bf16[128,2048]{1,0:T(8,128)(2,1)S(1)} %reshape.21), channel_id=1, source_target_pairs={{0,1},{1,0},{2,3},{3,2},{4,5},{5,4},{6,7},{7,6},{8,9},{9,8},{10,11... | collective-permute-start | bytes 1572872 | tf_op jit(solution)/shard_map/ppermute | solution.py:46
  29.2 20.2 %collective-permute-start.3 = (bf16[128,1024]{1,0:T(8,128)(2,1)S(1)}, bf16[128,1024]{1,0:T(8,128)(2,1)S(1)}, u32[]{:S(2)}, u32[]{:S(2)}) collective-permute-start(bf16[128,1024]{1,0:T(8,128)(2,1)S(1)} %get-tuple-element.39), channel_id=1, source_target_pairs={{0,24},{2,26},{4,28},{6,30},{8,0},{10,2},{12,4},{14,6},{16,8},{18,... | collective-permute-start | bytes 786440 | tf_op jit(solution)/shard_map/ppermute | solution.py:36
  29.3 20.1 %collective-permute-start.4 = (bf16[128,1024]{1,0:T(8,128)(2,1)S(1)}, bf16[128,1024]{1,0:T(8,128)(2,1)S(1)}, u32[]{:S(2)}, u32[]{:S(2)}) collective-permute-start(bf16[128,1024]{1,0:T(8,128)(2,1)S(1)} %get-tuple-element.40), channel_id=1, source_target_pairs={{0,16},{2,18},{4,20},{6,22},{8,24},{10,26},{12,28},{14,30},{16,0},... | collective-permute-start | bytes 786440 | tf_op jit(solution)/shard_map/ppermute | solution.py:36
  31.9 20.8 %collective-permute-start.5 = (bf16[128,1024]{1,0:T(8,128)(2,1)S(1)}, bf16[128,1024]{1,0:T(8,128)(2,1)S(1)}, u32[]{:S(2)}, u32[]{:S(2)}) collective-permute-start(bf16[128,1024]{1,0:T(8,128)(2,1)S(1)} %get-tuple-element.41), channel_id=1, source_target_pairs={{0,8},{2,10},{4,12},{6,14},{8,16},{10,18},{12,20},{14,22},{16,24},... | collective-permute-start | bytes 786440 | tf_op jit(solution)/shard_map/ppermute | solution.py:36
  52.7 10.2 %collective-permute-start.9 = (bf16[2816,512]{1,0:T(8,128)(2,1)}, bf16[2816,512]{1,0:T(8,128)(2,1)}, u32[]{:S(2)}, u32[]{:S(2)}) collective-permute-start(bf16[2816,512]{1,0:T(8,128)(2,1)} %pad_maximum_fusion.3), channel_id=1, source_target_pairs={{0,2},{2,0},{4,6},{6,4},{8,10},{10,8},{12,14},{14,12},{16,18},{18,... | collective-permute-start | bytes 8650760 | tf_op jit(solution)/shard_map/ppermute | solution.py:32
  56.0 59.9 %copy-start.10 = (bf16[512,1024]{1,0:T(8,128)(2,1)}, bf16[512,1024]{1,0:T(8,128)(2,1)S(1)}, u32[]{:S(2)}) copy-start(bf16[512,1024]{1,0:T(8,128)(2,1)S(1)} %pad_maximum_fusion.15) | copy-start | bytes 3145732
  56.0 20.1 %collective-permute-start.7 = (bf16[128,2816]{1,0:T(8,128)(2,1)}, bf16[128,2816]{1,0:T(8,128)(2,1)S(1)}, u32[]{:S(2)}, u32[]{:S(2)}) collective-permute-start(bf16[128,2816]{1,0:T(8,128)(2,1)} %collective-permute-done.1), channel_id=1, source_target_pairs={{8,16},{10,18},{12,20},{14,22},{16,24},{18,26},{20,28},{22,30},{9,... | collective-permute-start | bytes 2162696 | tf_op jit(solution)/shard_map/ppermute | solution.py:40
  60.5 19.7 %collective-permute-start.8 = (bf16[128,2816]{1,0:T(8,128)(2,1)}, bf16[128,2816]{1,0:T(8,128)(2,1)S(1)}, u32[]{:S(2)}, u32[]{:S(2)}) collective-permute-start(bf16[128,2816]{1,0:T(8,128)(2,1)} %collective-permute-done), channel_id=1, source_target_pairs={{16,8},{18,10},{20,12},{22,14},{8,0},{10,2},{12,4},{14,6},{17,9},{... | collective-permute-start | bytes 2162696 | tf_op jit(solution)/shard_map/ppermute | solution.py:40
  62.4 31.7 %collective-permute-start.14 = (bf16[2688,256]{1,0:T(8,128)(2,1)S(1)}, bf16[2688,256]{1,0:T(8,128)(2,1)S(1)}, u32[]{:S(2)}, u32[]{:S(2)}) collective-permute-start(bf16[2688,256]{1,0:T(8,128)(2,1)S(1)} %slice.95), channel_id=1, source_target_pairs={{0,4},{2,6},{4,0},{6,2},{8,12},{10,14},{12,8},{14,10},{16,20},{18,... | collective-permute-start | bytes 4128776 | tf_op jit(solution)/shard_map/ppermute | solution.py:32
  80.2 14.2 %collective-permute-start.10 = (bf16[128,2816]{1,0:T(8,128)(2,1)S(1)}, bf16[128,2816]{1,0:T(8,128)(2,1)S(1)}, u32[]{:S(2)}, u32[]{:S(2)}) collective-permute-start(bf16[128,2816]{1,0:T(8,128)(2,1)S(1)} %collective-permute-done.7), channel_id=1, source_target_pairs={{16,24},{18,26},{20,28},{22,30},{17,25},{19,27},{21,29},{23,31}} | collective-permute-start | bytes 2162696 | tf_op jit(solution)/shard_map/ppermute | solution.py:40
  80.9 16.7 %collective-permute-start.11 = (bf16[128,2816]{1,0:T(8,128)(2,1)S(1)}, bf16[128,2816]{1,0:T(8,128)(2,1)S(1)}, u32[]{:S(2)}, u32[]{:S(2)}) collective-permute-start(bf16[128,2816]{1,0:T(8,128)(2,1)S(1)} %collective-permute-done.8), channel_id=1, source_target_pairs={{8,0},{10,2},{12,4},{14,6},{9,1},{11,3},{13,5},{15,7}} | collective-permute-start | bytes 2162696 | tf_op jit(solution)/shard_map/ppermute | solution.py:40
  83.1 18.6 %collective-permute-start.12 = (bf16[128,2816]{1,0:T(8,128)(2,1)S(1)}, bf16[128,2816]{1,0:T(8,128)(2,1)S(1)}, u32[]{:S(2)}, u32[]{:S(2)}) collective-permute-start(bf16[128,2816]{1,0:T(8,128)(2,1)S(1)} %get-tuple-element.47), channel_id=1, source_target_pairs={{0,8},{2,10},{4,12},{6,14},{1,9},{3,11},{5,13},{7,15}} | collective-permute-start | bytes 2162696 | tf_op jit(solution)/shard_map/ppermute | solution.py:40
  84.4 17.3 %collective-permute-start.13 = (bf16[128,2816]{1,0:T(8,128)(2,1)S(1)}, bf16[128,2816]{1,0:T(8,128)(2,1)S(1)}, u32[]{:S(2)}, u32[]{:S(2)}) collective-permute-start(bf16[128,2816]{1,0:T(8,128)(2,1)S(1)} %get-tuple-element.48), channel_id=1, source_target_pairs={{24,16},{26,18},{28,20},{30,22},{25,17},{27,19},{29,21},{31,23}} | collective-permute-start | bytes 2162696 | tf_op jit(solution)/shard_map/ppermute | solution.py:40
  94.1 31.7 %copy-start.9 = (bf16[2688,256]{1,0:T(8,128)(2,1)}, bf16[2688,256]{1,0:T(8,128)(2,1)S(1)}, u32[]{:S(2)}) copy-start(bf16[2688,256]{1,0:T(8,128)(2,1)S(1)} %collective-permute-done.14) | copy-start | bytes 4128772
  101.7 34.5 %collective-permute-start.16 = (bf16[128,2688]{1,0:T(8,128)(2,1)}, bf16[128,2688]{1,0:T(8,128)(2,1)}, u32[]{:S(2)}, u32[]{:S(2)}) collective-permute-start(bf16[128,2688]{1,0:T(8,128)(2,1)} %fusion.19), channel_id=1, source_target_pairs={{0,8},{2,10},{4,12},{6,14},{8,16},{10,18},{12,20},{14,22},{16,24},... | collective-permute-start | bytes 2064392 | tf_op jit(solution)/shard_map/ppermute | solution.py:40
  103.6 32.6 %collective-permute-start.15 = (bf16[128,2688]{1,0:T(8,128)(2,1)}, bf16[128,2688]{1,0:T(8,128)(2,1)}, u32[]{:S(2)}, u32[]{:S(2)}) collective-permute-start(bf16[128,2688]{1,0:T(8,128)(2,1)} %fusion.19), channel_id=1, source_target_pairs={{24,16},{26,18},{28,20},{30,22},{16,8},{18,10},{20,12},{22,14},{8,... | collective-permute-start | bytes 2064392 | tf_op jit(solution)/shard_map/ppermute | solution.py:40
  108.6 17.1 %collective-permute-start.17 = (bf16[2688,512]{1,0:T(8,128)(2,1)S(1)}, bf16[2688,512]{1,0:T(8,128)(2,1)}, u32[]{:S(2)}, u32[]{:S(2)}) collective-permute-start(bf16[2688,512]{1,0:T(8,128)(2,1)S(1)} %pad_maximum_fusion.5), channel_id=1, source_target_pairs={{0,2},{2,0},{4,6},{6,4},{8,10},{10,8},{12,14},{14,12},{16,18},{18,... | collective-permute-start | bytes 8257544 | tf_op jit(solution)/shard_map/ppermute | solution.py:32
  115.5 15.4 %collective-permute-start.18 = (bf16[2816,512]{1,0:T(8,128)(2,1)}, bf16[2816,512]{1,0:T(8,128)(2,1)}, u32[]{:S(2)}, u32[]{:S(2)}) collective-permute-start(bf16[2816,512]{1,0:T(8,128)(2,1)} %convolution_convert_fusion.1), channel_id=1, source_target_pairs={{0,2},{2,0},{4,6},{6,4},{8,10},{10,8},{12,14},{14,12},{16,18},{18,... | collective-permute-start | bytes 8650760 | tf_op jit(solution)/shard_map/ppermute | solution.py:32
  130.7 100.8 %copy-start.1 = (f32[512,2688]{1,0:T(8,128)}, f32[512,2688]{1,0:T(8,128)S(1)}, u32[]{:S(2)}) copy-start(f32[512,2688]{1,0:T(8,128)S(1)} %fusion.7) | copy-start | bytes 16515076
  136.2 16.8 %collective-permute-start.19 = (bf16[128,2688]{1,0:T(8,128)(2,1)}, bf16[128,2688]{1,0:T(8,128)(2,1)S(1)}, u32[]{:S(2)}, u32[]{:S(2)}) collective-permute-start(bf16[128,2688]{1,0:T(8,128)(2,1)} %collective-permute-done.16), channel_id=1, source_target_pairs={{8,16},{10,18},{12,20},{14,22},{16,24},{18,26},{20,28},{22,30},{9,... | collective-permute-start | bytes 2064392 | tf_op jit(solution)/shard_map/ppermute | solution.py:40
  137.5 19.5 %collective-permute-start.20 = (bf16[128,2688]{1,0:T(8,128)(2,1)}, bf16[128,2688]{1,0:T(8,128)(2,1)S(1)}, u32[]{:S(2)}, u32[]{:S(2)}) collective-permute-start(bf16[128,2688]{1,0:T(8,128)(2,1)} %collective-permute-done.15), channel_id=1, source_target_pairs={{16,8},{18,10},{20,12},{22,14},{8,0},{10,2},{12,4},{14,6},{17,9},{... | collective-permute-start | bytes 2064392 | tf_op jit(solution)/shard_map/ppermute | solution.py:40
  139.5 19.3 %collective-permute-start.21 = (bf16[128,2688]{1,0:T(8,128)(2,1)S(1)}, bf16[128,2688]{1,0:T(8,128)(2,1)S(1)}, u32[]{:S(2)}, u32[]{:S(2)}) collective-permute-start(bf16[128,2688]{1,0:T(8,128)(2,1)S(1)} %get-tuple-element.55), channel_id=1, source_target_pairs={{0,8},{2,10},{4,12},{6,14},{1,9},{3,11},{5,13},{7,15}} | collective-permute-start | bytes 2064392 | tf_op jit(solution)/shard_map/ppermute | solution.py:40
  140.8 18.0 %collective-permute-start.22 = (bf16[128,2688]{1,0:T(8,128)(2,1)S(1)}, bf16[128,2688]{1,0:T(8,128)(2,1)S(1)}, u32[]{:S(2)}, u32[]{:S(2)}) collective-permute-start(bf16[128,2688]{1,0:T(8,128)(2,1)S(1)} %get-tuple-element.56), channel_id=1, source_target_pairs={{24,16},{26,18},{28,20},{30,22},{25,17},{27,19},{29,21},{31,23}} | collective-permute-start | bytes 2064392 | tf_op jit(solution)/shard_map/ppermute | solution.py:40
  141.7 42.0 %collective-permute-start.27 = (bf16[2816,256]{1,0:T(8,128)(2,1)S(1)}, bf16[2816,256]{1,0:T(8,128)(2,1)S(1)}, u32[]{:S(2)}, u32[]{:S(2)}) collective-permute-start(bf16[2816,256]{1,0:T(8,128)(2,1)S(1)} %fusion.1), channel_id=1, source_target_pairs={{0,4},{2,6},{4,0},{6,2},{8,12},{10,14},{12,8},{14,10},{16,20},{18,... | collective-permute-start | bytes 4325384 | tf_op jit(solution)/shard_map/ppermute | solution.py:32
  158.7 9.5 %collective-permute-start.23 = (bf16[128,2688]{1,0:T(8,128)(2,1)S(1)}, bf16[128,2688]{1,0:T(8,128)(2,1)S(1)}, u32[]{:S(2)}, u32[]{:S(2)}) collective-permute-start(bf16[128,2688]{1,0:T(8,128)(2,1)S(1)} %collective-permute-done.19), channel_id=1, source_target_pairs={{16,24},{18,26},{20,28},{22,30},{17,25},{19,27},{21,29},{23,31}} | collective-permute-start | bytes 2064392 | tf_op jit(solution)/shard_map/ppermute | solution.py:40
  159.4 15.6 %collective-permute-start.24 = (bf16[128,2688]{1,0:T(8,128)(2,1)S(1)}, bf16[128,2688]{1,0:T(8,128)(2,1)S(1)}, u32[]{:S(2)}, u32[]{:S(2)}) collective-permute-start(bf16[128,2688]{1,0:T(8,128)(2,1)S(1)} %collective-permute-done.20), channel_id=1, source_target_pairs={{8,0},{10,2},{12,4},{14,6},{9,1},{11,3},{13,5},{15,7}} | collective-permute-start | bytes 2064392 | tf_op jit(solution)/shard_map/ppermute | solution.py:40
  160.9 19.8 %collective-permute-start.25 = (bf16[128,2816]{1,0:T(8,128)(2,1)S(1)}, bf16[128,2816]{1,0:T(8,128)(2,1)S(1)}, u32[]{:S(2)}, u32[]{:S(2)}) collective-permute-start(bf16[128,2816]{1,0:T(8,128)(2,1)S(1)} %get-tuple-element.59), channel_id=1, source_target_pairs={{0,8},{2,10},{4,12},{6,14},{8,16},{10,18},{12,20},{14,22},{1,9},{3... | collective-permute-start | bytes 2162696 | tf_op jit(solution)/shard_map/ppermute | solution.py:40
  165.3 18.4 %collective-permute-start.26 = (bf16[128,2816]{1,0:T(8,128)(2,1)S(1)}, bf16[128,2816]{1,0:T(8,128)(2,1)S(1)}, u32[]{:S(2)}, u32[]{:S(2)}) collective-permute-start(bf16[128,2816]{1,0:T(8,128)(2,1)S(1)} %get-tuple-element.60), channel_id=1, source_target_pairs={{24,16},{26,18},{28,20},{30,22},{16,8},{18,10},{20,12},{22,14},{25... | collective-permute-start | bytes 2162696 | tf_op jit(solution)/shard_map/ppermute | solution.py:40
  168.3 16.3 %copy-start.21 = (bf16[128,2688]{1,0:T(8,128)(2,1)}, bf16[128,2688]{1,0:T(8,128)(2,1)S(1)}, u32[]{:S(2)}) copy-start(bf16[128,2688]{1,0:T(8,128)(2,1)S(1)} %broadcast_select_fusion.4) | copy-start | bytes 2064388
  184.6 19.2 %collective-permute-start.30 = (bf16[2688,512]{1,0:T(8,128)(2,1)}, bf16[2688,512]{1,0:T(8,128)(2,1)}, u32[]{:S(2)}, u32[]{:S(2)}) collective-permute-start(bf16[2688,512]{1,0:T(8,128)(2,1)} %convolution_convert_fusion), channel_id=1, source_target_pairs={{0,2},{2,0},{4,6},{6,4},{8,10},{10,8},{12,14},{14,12},{16,18},{18,... | collective-permute-start | bytes 8257544 | tf_op jit(solution)/shard_map/ppermute | solution.py:32
  199.4 19.7 %collective-permute-start.28 = (bf16[128,2688]{1,0:T(8,128)(2,1)}, bf16[128,2688]{1,0:T(8,128)(2,1)}, u32[]{:S(2)}, u32[]{:S(2)}) collective-permute-start(bf16[128,2688]{1,0:T(8,128)(2,1)} %get-tuple-element.62), channel_id=1, source_target_pairs={{0,8},{2,10},{4,12},{6,14},{8,16},{10,18},{12,20},{14,22},{1,9},{3... | collective-permute-start | bytes 2064392 | tf_op jit(solution)/shard_map/ppermute | solution.py:40
  201.7 27.8 %collective-permute-start.29 = (bf16[128,2688]{1,0:T(8,128)(2,1)}, bf16[128,2688]{1,0:T(8,128)(2,1)}, u32[]{:S(2)}, u32[]{:S(2)}) collective-permute-start(bf16[128,2688]{1,0:T(8,128)(2,1)} %get-tuple-element.63), channel_id=1, source_target_pairs={{24,16},{26,18},{28,20},{30,22},{16,8},{18,10},{20,12},{22,14},{25... | collective-permute-start | bytes 2064392 | tf_op jit(solution)/shard_map/ppermute | solution.py:40
  206.4 23.1 %copy-start.30 = (bf16[128,1024]{1,0:T(8,128)(2,1)S(1)}, bf16[128,1024]{1,0:T(8,128)(2,1)}, u32[]{:S(2)}) copy-start(bf16[128,1024]{1,0:T(8,128)(2,1)} %get-tuple-element.65) | copy-start | bytes 786436
  206.4 23.1 %copy-start.29 = (bf16[128,1024]{1,0:T(8,128)(2,1)S(1)}, bf16[128,1024]{1,0:T(8,128)(2,1)}, u32[]{:S(2)}) copy-start(bf16[128,1024]{1,0:T(8,128)(2,1)} %get-tuple-element.66) | copy-start | bytes 786436
  229.5 10.8 %collective-permute-start.31 = (bf16[128,1024]{1,0:T(8,128)(2,1)S(1)}, bf16[128,1024]{1,0:T(8,128)(2,1)S(1)}, u32[]{:S(2)}, u32[]{:S(2)}) collective-permute-start(bf16[128,1024]{1,0:T(8,128)(2,1)S(1)} %copy-done.30), channel_id=1, source_target_pairs={{0,8},{2,10},{4,12},{6,14},{8,16},{10,18},{12,20},{14,22},{16,24},... | collective-permute-start | bytes 786440 | tf_op jit(solution)/shard_map/ppermute | solution.py:36
  229.5 18.0 %collective-permute-start.32 = (bf16[128,1024]{1,0:T(8,128)(2,1)S(1)}, bf16[128,1024]{1,0:T(8,128)(2,1)S(1)}, u32[]{:S(2)}, u32[]{:S(2)}) collective-permute-start(bf16[128,1024]{1,0:T(8,128)(2,1)S(1)} %copy-done.29), channel_id=1, source_target_pairs={{0,16},{2,18},{4,20},{6,22},{8,24},{10,26},{12,28},{14,30},{16,0},... | collective-permute-start | bytes 786440 | tf_op jit(solution)/shard_map/ppermute | solution.py:36
  229.6 18.8 %collective-permute-start.33 = (bf16[128,1024]{1,0:T(8,128)(2,1)S(1)}, bf16[128,1024]{1,0:T(8,128)(2,1)S(1)}, u32[]{:S(2)}, u32[]{:S(2)}) collective-permute-start(bf16[128,1024]{1,0:T(8,128)(2,1)S(1)} %get-tuple-element.67), channel_id=1, source_target_pairs={{0,24},{2,26},{4,28},{6,30},{8,0},{10,2},{12,4},{14,6},{16,8},{18,... | collective-permute-start | bytes 786440 | tf_op jit(solution)/shard_map/ppermute | solution.py:36
  234.2 33.2 %copy-start.2 = (bf16[128,5504]{1,0:T(8,128)(2,1)S(1)}, bf16[128,5504]{1,0:T(8,128)(2,1)}, u32[]{:S(2)}) copy-start(bf16[128,5504]{1,0:T(8,128)(2,1)} %param.5) | copy-start | bytes 4227076
  234.2 33.2 %copy-start.3 = (bf16[128,5504]{1,0:T(8,128)(2,1)S(1)}, bf16[128,5504]{1,0:T(8,128)(2,1)}, u32[]{:S(2)}) copy-start(bf16[128,5504]{1,0:T(8,128)(2,1)} %param.4) | copy-start | bytes 4227076
  234.2 24.3 %collective-permute-start.34 = (bf16[128,2816]{1,0:T(8,128)(2,1)S(1)}, bf16[128,2816]{1,0:T(8,128)(2,1)S(1)}, u32[]{:S(2)}, u32[]{:S(2)}) collective-permute-start(bf16[128,2816]{1,0:T(8,128)(2,1)S(1)} %copy-done.16), channel_id=1, source_target_pairs={{0,8},{2,10},{4,12},{6,14},{8,16},{10,18},{12,20},{14,22},{16,24},... | collective-permute-start | bytes 2162696 | tf_op jit(solution)/shard_map/ppermute | solution.py:40
  237.8 21.1 %collective-permute-start.35 = (bf16[128,2816]{1,0:T(8,128)(2,1)S(1)}, bf16[128,2816]{1,0:T(8,128)(2,1)S(1)}, u32[]{:S(2)}, u32[]{:S(2)}) collective-permute-start(bf16[128,2816]{1,0:T(8,128)(2,1)S(1)} %get-tuple-element.69), channel_id=1, source_target_pairs={{24,16},{26,18},{28,20},{30,22},{16,8},{18,10},{20,12},{22,14},{8,... | collective-permute-start | bytes 2162696 | tf_op jit(solution)/shard_map/ppermute | solution.py:40
  240.3 40.6 %collective-permute-start.39 = (bf16[2688,256]{1,0:T(8,128)(2,1)}, bf16[2688,256]{1,0:T(8,128)(2,1)}, u32[]{:S(2)}, u32[]{:S(2)}) collective-permute-start(bf16[2688,256]{1,0:T(8,128)(2,1)} %fusion.3), channel_id=1, source_target_pairs={{0,4},{2,6},{4,0},{6,2},{8,12},{10,14},{12,8},{14,10},{16,20},{18,... | collective-permute-start | bytes 4128776 | tf_op jit(solution)/shard_map/ppermute | solution.py:32
  258.9 28.3 %collective-permute-start.37 = (bf16[128,2688]{1,0:T(8,128)(2,1)}, bf16[128,2688]{1,0:T(8,128)(2,1)}, u32[]{:S(2)}, u32[]{:S(2)}) collective-permute-start(bf16[128,2688]{1,0:T(8,128)(2,1)} %get-tuple-element.71), channel_id=1, source_target_pairs={{0,8},{2,10},{4,12},{6,14},{8,16},{10,18},{12,20},{14,22},{16,24},... | collective-permute-start | bytes 2064392 | tf_op jit(solution)/shard_map/ppermute | solution.py:40
  262.8 24.4 %collective-permute-start.38 = (bf16[128,2688]{1,0:T(8,128)(2,1)}, bf16[128,2688]{1,0:T(8,128)(2,1)}, u32[]{:S(2)}, u32[]{:S(2)}) collective-permute-start(bf16[128,2688]{1,0:T(8,128)(2,1)} %get-tuple-element.72), channel_id=1, source_target_pairs={{24,16},{26,18},{28,20},{30,22},{16,8},{18,10},{20,12},{22,14},{8,... | collective-permute-start | bytes 2064392 | tf_op jit(solution)/shard_map/ppermute | solution.py:40
  265.8 9.2 %collective-permute-start.36 = (bf16[128,2048]{1,0:T(8,128)(2,1)S(1)}, bf16[128,2048]{1,0:T(8,128)(2,1)S(1)}, u32[]{:S(2)}, u32[]{:S(2)}) collective-permute-start(bf16[128,2048]{1,0:T(8,128)(2,1)S(1)} %pad_maximum_fusion.18), channel_id=1, source_target_pairs={{0,1},{1,0},{2,3},{3,2},{4,5},{5,4},{6,7},{7,6},{8,9},{9,8},{10,11... | collective-permute-start | bytes 1572872 | tf_op jit(solution)/shard_map/ppermute | solution.py:46
  (23 other events, 139.3 us)
